TPU v7x, 256 devices: a whole 4x4x8 slice. The times are simulated.
256 devices in a mesh: gx: 16 (over x, y_hi, core), gy: 16 (over y_lo, z).
Axes of the slice: x: 4, y: 4 (y_hi: 2, y_lo: 2; y = y_hi * 2 + y_lo), z: 8, core: 2. Of those that a mesh axis runs over, the one named last changes fastest.
Arguments:
- state: float32 [8, 128, 32, 2048], P(None, 'gx', None, 'gy'), may hold values from -6 to 6
- shifts: int32 [2, 128], P(None, 'gx'), may hold values from 0 to 2047
- fracs: float32 [2, 128], P(None, 'gx'), may hold values from 0 to 1
- offsets: int32 [2], replicated, may hold values from 0 to 2047
- kappa: float32 [8], replicated, may hold values from 0.04 to 0.16
Outputs:
- evolved: float32 [8, 128, 32, 2048], P(None, 'gx', None, 'gy')
All inputs are finite; a program needn't handle non-finite values.
Results may differ from a plain program's by a relative error of at most 0.00002.
Values sent between devices are 32-bit elements; how exact they have to be, the bound alone decides.
No kernel may reach another device: no remote copies, remote signals or barrier semaphores. Data moves between devices by JAX's collectives and lax.ppermute only.
A program may use at most 64 MiB of HBM per device.

v0:
```python
import jax
import jax.numpy as jnp
from jax import lax
from jax.sharding import PartitionSpec as P

spin_gain = 0.2
spin_drag = 0.05
tidal_gain = 0.3


def shifted_2(value, axis, steps):
    count = lax.axis_size(axis)
    pairs = [(source, (source + steps) % count) for source in range(count)]
    return lax.ppermute(value, axis, pairs)


def padded_2(block, sides, width):
    for axis, dim in sides:
        count = lax.axis_size(axis)
        forward = [(i, i + 1) for i in range(count - 1)]
        forward.append((count - 1, 0))
        backward = [(target, source) for source, target in forward]
        low = lax.ppermute(
            lax.slice_in_dim(block, block.shape[dim] - width, None, axis=dim), axis, forward
        )
        high = lax.ppermute(lax.slice_in_dim(block, 0, width, axis=dim), axis, backward)
        block = jnp.concatenate([low, block, high], axis=dim)
    return block


def take_rows(turned, earlier, remains, weights):
    joined = jnp.concatenate([earlier, turned], axis=3)
    extent = turned.shape[3]

    def column(stripe, anchor, weight):
        nearer = lax.dynamic_slice_in_dim(stripe, anchor, extent, 2)
        farther = lax.dynamic_slice_in_dim(stripe, anchor - 1, extent, 2)
        return (1.0 - weight) * nearer + weight * farther

    anchors = extent - remains
    return jax.vmap(column, in_axes=(1, 0, 0), out_axes=1)(joined, anchors, weights)


def turn_blocks(current, blocks):
    cycle_size = lax.axis_size("gy")
    turned = current
    for degree in range(cycle_size.bit_length() - 1):
        arrived = shifted_2(turned, "gy", 2**degree)
        chosen = (blocks // 2**degree % 2 == 1)[None, :, None, None]
        turned = jnp.where(chosen, arrived, turned)
    return turned


def remap_blocks(values, shifted, weights):
    extent = values.shape[3]
    blocks = shifted // extent
    remains = shifted % extent
    turned = turn_blocks(values, blocks)
    earlier = shifted_2(turned, "gy", 1)
    return take_rows(turned, earlier, remains, weights)


def remap(values, shifted, weights):
    return remap_blocks(values, shifted, weights)


def radial_rims(advected):
    return padded_2(advected, (("gx", 1),), 1)


def stencil(values, lower, upper, kappa, column_start, total_x):
    columns = values.shape[1]
    radial_sum = jnp.concatenate([lower[:, None], values[:, :-1]], axis=1) + jnp.concatenate(
        [values[:, 1:], upper[:, None]], axis=1
    )
    widened = padded_2(values, (("gy", 3),), 1)
    azimuthal_sum = widened[:, :, :, 2:] + widened[:, :, :, :-2]
    vertical_sum = jnp.concatenate([values[:, :, :1], values[:, :, :-1]], axis=2) + jnp.concatenate(
        [values[:, :, 1:], values[:, :, -1:]], axis=2
    )
    laplace = radial_sum + azimuthal_sum + vertical_sum - 6.0 * values
    mixed = values + kappa[:, None, None, None] * laplace
    position = ((column_start + jnp.arange(columns)).astype(jnp.float32) + 0.5) / total_x - 0.5
    position = position[:, None, None]
    density = mixed[0]
    radial_mom = mixed[1]
    azimuthal_mom = mixed[2]
    new_radial = radial_mom + spin_gain * azimuthal_mom + tidal_gain * position * density
    new_azimuthal = azimuthal_mom - spin_drag * radial_mom
    return jnp.concatenate(
        [density[None], new_radial[None], new_azimuthal[None], mixed[3:]], axis=0
    )


def shear_ghosts(lower_raw, upper_raw, offset, total_y, extent):
    cycle_size = lax.axis_size("gy")
    lower_total = offset % total_y
    upper_total = (total_y - offset) % total_y
    lower_blocks = lower_total // extent
    upper_blocks = upper_total // extent
    lower_turn = lower_raw
    upper_turn = upper_raw
    for degree in range(cycle_size.bit_length() - 1):
        arrived = shifted_2((lower_turn, upper_turn), "gy", 2**degree)
        lower_turn = jnp.where(lower_blocks // 2**degree % 2 == 1, arrived[0], lower_turn)
        upper_turn = jnp.where(upper_blocks // 2**degree % 2 == 1, arrived[1], upper_turn)
    earlier = shifted_2((lower_turn, upper_turn), "gy", 1)
    no_weight = jnp.zeros((1,), jnp.float32)
    lower_rest = jnp.reshape(lower_total % extent, (1,))
    upper_rest = jnp.reshape(upper_total % extent, (1,))
    lower_new = take_rows(lower_turn[:, None], earlier[0][:, None], lower_rest, no_weight)[:, 0]
    upper_new = take_rows(upper_turn[:, None], earlier[1][:, None], upper_rest, no_weight)[:, 0]
    return (lower_new, upper_new)


def on_device(state, shifts, fracs, offsets, kappa):
    columns = state.shape[1]
    cycle_size = lax.axis_size("gy")
    radial_size = lax.axis_size("gx")
    total_y = state.shape[3] * cycle_size
    total_x = columns * radial_size
    radial_index = lax.axis_index("gx")
    column_start = radial_index * columns
    current = state
    extent = current.shape[3]
    for section in range(shifts.shape[0]):
        shifted = shifts[section]
        weights = fracs[section]
        offset = offsets[section]
        advected = remap(current, shifted, weights)
        padded = radial_rims(advected)
        lower_raw = padded[:, 0]
        upper_raw = padded[:, -1]
        lower_new, upper_new = shear_ghosts(lower_raw, upper_raw, offset, total_y, extent)
        lower = jnp.where(radial_index == 0, lower_new, lower_raw)
        upper = jnp.where(radial_index == radial_size - 1, upper_new, upper_raw)
        current = stencil(advected, lower, upper, kappa, column_start, total_x)
    return current


def solution(mesh):
    placed = (P(None, "gx", None, "gy"), P(None, "gx"), P(None, "gx"), P(), P())
    return jax.shard_map(
        on_device, mesh=mesh, in_specs=placed, out_specs=P(None, "gx", None, "gy"), check_vma=False
    )
```

profile of v0, /device:TPU:28, one launch (start us, length us, event | category | flops | bytes accessed | tf_op | source)
XLA Modules:
  0.0 551.0 jit_solution(6034089422606936607)
XLA Ops:
  3.3 26.1 %collective-permute-done = f32[8,8,32,128]{3,2,1,0:T(8,128)S(1)} collective-permute-done((f32[8,8,32,128]{3,2,1,0:T(8,128)}, f32[8,8,32,128]{3,2,1,0:T(8,128)S(1)}, u32[]{:S(2)}, u32[]{:S(2)}) %collective-permute-start) | collective-permute-done | bytes 1048608 | tf_op jit(solution)/shard_map/ppermute | solution.py:14
  31.0 49.4 %collective-permute-done.1 = f32[8,8,32,128]{3,2,1,0:T(8,128)S(1)} collective-permute-done((f32[8,8,32,128]{3,2,1,0:T(8,128)S(1)}, f32[8,8,32,128]{3,2,1,0:T(8,128)S(1)}, u32[]{:S(2)}, u32[]{:S(2)}) %collective-permute-start.1) | collective-permute-done | bytes 1048608 | tf_op jit(solution)/shard_map/ppermute | solution.py:14
  82.8 47.4 %collective-permute-done.2 = f32[8,8,32,128]{3,2,1,0:T(8,128)S(1)} collective-permute-done((f32[8,8,32,128]{3,2,1,0:T(8,128)S(1)}, f32[8,8,32,128]{3,2,1,0:T(8,128)S(1)}, u32[]{:S(2)}, u32[]{:S(2)}) %collective-permute-start.2) | collective-permute-done | bytes 1048608 | tf_op jit(solution)/shard_map/ppermute | solution.py:14
  132.0 23.5 %collective-permute-done.3 = f32[8,8,32,128]{3,2,1,0:T(8,128)S(1)} collective-permute-done((f32[8,8,32,128]{3,2,1,0:T(8,128)S(1)}, f32[8,8,32,128]{3,2,1,0:T(8,128)S(1)}, u32[]{:S(2)}, u32[]{:S(2)}) %collective-permute-start.3) | collective-permute-done | bytes 1048608 | tf_op jit(solution)/shard_map/ppermute | solution.py:14
  160.5 21.5 %collective-permute-done.4 = f32[8,8,32,128]{3,2,1,0:T(8,128)} collective-permute-done((f32[8,8,32,128]{3,2,1,0:T(8,128)S(1)}, f32[8,8,32,128]{3,2,1,0:T(8,128)}, u32[]{:S(2)}, u32[]{:S(2)}) %collective-permute-start.4) | collective-permute-done | bytes 1048608 | tf_op jit(solution)/shard_map/ppermute | solution.py:14
  183.4 7.6 %copy.108 = f32[8,8,32,256]{2,0,1,3:T(8,128)} copy(f32[8,8,32,256]{3,2,1,0:T(8,128)S(1)} %pad_maximum_fusion) | data formatting | bytes 4194304 | tf_op jit(solution)/shard_map/concatenate | solution.py:32
  191.0 6.6 %gather_fusion.1 = f32[8,8,32,128]{2,1,3,0:T(8,128)} fusion(f32[8,8,32,256]{2,1,0,3:T(8,128)} %bitcast.100, s32[8]{0:T(128)S(1)} %get-tuple-element.144), kind=kCustom, calls=%fused_computation.1 | custom fusion | bytes 2097280 | tf_op jit(solution)/shard_map/vmap()/gather | solution.py:37
  200.4 6.6 %gather_fusion = f32[8,8,32,128]{2,1,3,0:T(8,128)} fusion(f32[8,8,32,256]{2,1,0,3:T(8,128)} %bitcast.101, s32[8]{0:T(128)S(1)} %get-tuple-element.131), kind=kCustom, calls=%fused_computation | custom fusion | bytes 2097280 | tf_op jit(solution)/shard_map/vmap()/gather | solution.py:36
  240.7 7.8 %collective-permute-done.13 = f32[8,32,128]{2,1,0:T(8,128)S(1)} collective-permute-done((f32[8,32,128]{2,1,0:T(8,128)S(1)}, f32[8,32,128]{2,1,0:T(8,128)S(1)}, u32[]{:S(2)}, u32[]{:S(2)}) %collective-permute-start.13) | collective-permute-done | bytes 131104 | tf_op jit(solution)/shard_map/ppermute | solution.py:14
  252.9 8.7 %collective-permute-start.9 = (f32[8,32,128]{2,1,0:T(8,128)S(1)}, f32[8,32,128]{2,1,0:T(8,128)S(1)}, u32[]{:S(2)}, u32[]{:S(2)}) collective-permute-start(f32[8,32,128]{2,1,0:T(8,128)S(1)} %broadcast_select_fusion.22), channel_id=1, source_target_pairs={{0,8},{1,9},{2,10},{3,11},{4,12},{5,13},{6,14},{7,15},{8,0},{9,1},... | collective-permute-start | bytes 393224 | tf_op jit(solution)/shard_map/ppermute | solution.py:14
  278.0 25.0 %collective-permute-done.19 = f32[8,8,32,128]{3,2,1,0:T(8,128)S(1)} collective-permute-done((f32[8,8,32,128]{3,2,1,0:T(8,128)S(1)}, f32[8,8,32,128]{3,2,1,0:T(8,128)S(1)}, u32[]{:S(2)}, u32[]{:S(2)}) %collective-permute-start.19) | collective-permute-done | bytes 1048608 | tf_op jit(solution)/shard_map/ppermute | solution.py:14
  303.6 49.6 %collective-permute-done.20 = f32[8,8,32,128]{3,2,1,0:T(8,128)S(1)} collective-permute-done((f32[8,8,32,128]{3,2,1,0:T(8,128)S(1)}, f32[8,8,32,128]{3,2,1,0:T(8,128)S(1)}, u32[]{:S(2)}, u32[]{:S(2)}) %collective-permute-start.20) | collective-permute-done | bytes 1048608 | tf_op jit(solution)/shard_map/ppermute | solution.py:14
  353.5 47.6 %collective-permute-done.21 = f32[8,8,32,128]{3,2,1,0:T(8,128)S(1)} collective-permute-done((f32[8,8,32,128]{3,2,1,0:T(8,128)S(1)}, f32[8,8,32,128]{3,2,1,0:T(8,128)S(1)}, u32[]{:S(2)}, u32[]{:S(2)}) %collective-permute-start.21) | collective-permute-done | bytes 1048608 | tf_op jit(solution)/shard_map/ppermute | solution.py:14
  401.5 24.6 %collective-permute-done.22 = f32[8,8,32,128]{3,2,1,0:T(8,128)S(1)} collective-permute-done((f32[8,8,32,128]{3,2,1,0:T(8,128)S(1)}, f32[8,8,32,128]{3,2,1,0:T(8,128)S(1)}, u32[]{:S(2)}, u32[]{:S(2)}) %collective-permute-start.22) | collective-permute-done | bytes 1048608 | tf_op jit(solution)/shard_map/ppermute | solution.py:14
  426.3 6.3 %collective-permute-start.23 = (f32[8,8,32,128]{3,2,1,0:T(8,128)S(1)}, f32[8,8,32,128]{3,2,1,0:T(8,128)}, u32[]{:S(2)}, u32[]{:S(2)}) collective-permute-start(f32[8,8,32,128]{3,2,1,0:T(8,128)S(1)} %broadcast_select_fusion.7), channel_id=1, source_target_pairs={{0,1},{1,2},{2,3},{3,4},{4,5},{5,6},{6,7},{7,8},{8,9},{9,10},{10,1... | collective-permute-start | bytes 3145736 | tf_op jit(solution)/shard_map/ppermute | solution.py:14
  435.7 16.6 %collective-permute-done.23 = f32[8,8,32,128]{3,2,1,0:T(8,128)} collective-permute-done((f32[8,8,32,128]{3,2,1,0:T(8,128)S(1)}, f32[8,8,32,128]{3,2,1,0:T(8,128)}, u32[]{:S(2)}, u32[]{:S(2)}) %collective-permute-start.23) | collective-permute-done | bytes 1048608 | tf_op jit(solution)/shard_map/ppermute | solution.py:14
  453.7 7.6 %copy.119 = f32[8,8,32,256]{2,0,1,3:T(8,128)} copy(f32[8,8,32,256]{3,2,1,0:T(8,128)S(1)} %pad_maximum_fusion.1) | data formatting | bytes 4194304 | tf_op jit(solution)/shard_map/concatenate | solution.py:32
  461.2 6.6 %gather_fusion.3 = f32[8,8,32,128]{2,1,3,0:T(8,128)} fusion(f32[8,8,32,256]{2,1,0,3:T(8,128)} %bitcast.98, s32[8]{0:T(128)S(1)} %get-tuple-element.143), kind=kCustom, calls=%fused_computation.3 | custom fusion | bytes 2097280 | tf_op jit(solution)/shard_map/vmap()/gather | solution.py:37
  470.6 6.6 %gather_fusion.2 = f32[8,8,32,128]{2,1,3,0:T(8,128)} fusion(f32[8,8,32,256]{2,1,0,3:T(8,128)} %bitcast.99, s32[8]{0:T(128)S(1)} %get-tuple-element.93), kind=kCustom, calls=%fused_computation.2 | custom fusion | bytes 2097280 | tf_op jit(solution)/shard_map/vmap()/gather | solution.py:36
  500.2 6.1 %collective-permute-done.31 = f32[8,32,128]{2,1,0:T(8,128)S(1)} collective-permute-done((f32[8,32,128]{2,1,0:T(8,128)S(1)}, f32[8,32,128]{2,1,0:T(8,128)S(1)}, u32[]{:S(2)}, u32[]{:S(2)}) %collective-permute-start.31) | collective-permute-done | bytes 131104 | tf_op jit(solution)/shard_map/ppermute | solution.py:14
  508.3 12.4 %collective-permute-done.32 = f32[8,32,128]{2,1,0:T(8,128)S(1)} collective-permute-done((f32[8,32,128]{2,1,0:T(8,128)S(1)}, f32[8,32,128]{2,1,0:T(8,128)S(1)}, u32[]{:S(2)}, u32[]{:S(2)}) %collective-permute-start.32) | collective-permute-done | bytes 131104 | tf_op jit(solution)/shard_map/ppermute | solution.py:14
  521.4 11.1 %collective-permute-done.33 = f32[8,32,128]{2,1,0:T(8,128)S(1)} collective-permute-done((f32[8,32,128]{2,1,0:T(8,128)S(1)}, f32[8,32,128]{2,1,0:T(8,128)S(1)}, u32[]{:S(2)}, u32[]{:S(2)}) %collective-permute-start.33) | collective-permute-done | bytes 131104 | tf_op jit(solution)/shard_map/ppermute | solution.py:14
  532.8 8.1 %collective-permute-done.34 = f32[8,32,128]{2,1,0:T(8,128)S(1)} collective-permute-done((f32[8,32,128]{2,1,0:T(8,128)S(1)}, f32[8,32,128]{2,1,0:T(8,128)S(1)}, u32[]{:S(2)}, u32[]{:S(2)}) %collective-permute-start.34) | collective-permute-done | bytes 131104 | tf_op jit(solution)/shard_map/ppermute | solution.py:14
  541.3 6.8 %collective-permute-done.35 = f32[8,32,128]{2,1,0:T(8,128)S(1)} collective-permute-done((f32[8,32,128]{2,1,0:T(8,128)S(1)}, f32[8,32,128]{2,1,0:T(8,128)S(1)}, u32[]{:S(2)}, u32[]{:S(2)}) %collective-permute-start.35) | collective-permute-done | bytes 131104 | tf_op jit(solution)/shard_map/ppermute | solution.py:14
  (163 shorter events, 104.0 us)
Async XLA Ops:
  0.0 29.4 %collective-permute-start = (f32[8,8,32,128]{3,2,1,0:T(8,128)}, f32[8,8,32,128]{3,2,1,0:T(8,128)S(1)}, u32[]{:S(2)}, u32[]{:S(2)}) collective-permute-start(f32[8,8,32,128]{3,2,1,0:T(8,128)} %param.5), channel_id=1, source_target_pairs={{0,1},{1,2},{2,3},{3,4},{4,5},{5,6},{6,7},{7,8},{8,9},{9,10},{10,1... | collective-permute-start | bytes 3145736 | tf_op jit(solution)/shard_map/ppermute | solution.py:14
  30.9 49.5 %collective-permute-start.1 = (f32[8,8,32,128]{3,2,1,0:T(8,128)S(1)}, f32[8,8,32,128]{3,2,1,0:T(8,128)S(1)}, u32[]{:S(2)}, u32[]{:S(2)}) collective-permute-start(f32[8,8,32,128]{3,2,1,0:T(8,128)S(1)} %broadcast_select_fusion), channel_id=1, source_target_pairs={{0,2},{1,3},{2,4},{3,5},{4,6},{5,7},{6,8},{7,9},{8,10},{9,11},{10,... | collective-permute-start | bytes 3145736 | tf_op jit(solution)/shard_map/ppermute | solution.py:14
  80.6 49.6 %collective-permute-start.2 = (f32[8,8,32,128]{3,2,1,0:T(8,128)S(1)}, f32[8,8,32,128]{3,2,1,0:T(8,128)S(1)}, u32[]{:S(2)}, u32[]{:S(2)}) collective-permute-start(f32[8,8,32,128]{3,2,1,0:T(8,128)S(1)} %broadcast_select_fusion.1), channel_id=1, source_target_pairs={{0,4},{1,5},{2,6},{3,7},{4,8},{5,9},{6,10},{7,11},{8,12},{9,13},{1... | collective-permute-start | bytes 3145736 | tf_op jit(solution)/shard_map/ppermute | solution.py:14
  130.5 25.0 %collective-permute-start.3 = (f32[8,8,32,128]{3,2,1,0:T(8,128)S(1)}, f32[8,8,32,128]{3,2,1,0:T(8,128)S(1)}, u32[]{:S(2)}, u32[]{:S(2)}) collective-permute-start(f32[8,8,32,128]{3,2,1,0:T(8,128)S(1)} %broadcast_select_fusion.2), channel_id=1, source_target_pairs={{0,8},{1,9},{2,10},{3,11},{4,12},{5,13},{6,14},{7,15},{8,0},{9,1},... | collective-permute-start | bytes 3145736 | tf_op jit(solution)/shard_map/ppermute | solution.py:14
  155.7 26.3 %collective-permute-start.4 = (f32[8,8,32,128]{3,2,1,0:T(8,128)S(1)}, f32[8,8,32,128]{3,2,1,0:T(8,128)}, u32[]{:S(2)}, u32[]{:S(2)}) collective-permute-start(f32[8,8,32,128]{3,2,1,0:T(8,128)S(1)} %broadcast_select_fusion.3), channel_id=1, source_target_pairs={{0,1},{1,2},{2,3},{3,4},{4,5},{5,6},{6,7},{7,8},{8,9},{9,10},{10,1... | collective-permute-start | bytes 3145736 | tf_op jit(solution)/shard_map/ppermute | solution.py:14
  212.7 10.3 %collective-permute-start.5 = (f32[8,1,32,128]{3,2,0,1:T(8,128)S(1)}, f32[8,1,32,128]{3,2,0,1:T(8,128)S(1)}, u32[]{:S(2)}, u32[]{:S(2)}) collective-permute-start(f32[8,1,32,128]{3,2,0,1:T(8,128)S(1)} %get-tuple-element.124), channel_id=1, source_target_pairs={{0,16},{16,32},{32,48},{48,64},{64,80},{80,96},{96,112},{112,128},... | collective-permute-start | bytes 393224 | tf_op jit(solution)/shard_map/ppermute | solution.py:23
  231.2 9.4 %collective-permute-start.7 = (f32[8,32,128]{2,1,0:T(8,128)S(1)}, f32[8,32,128]{2,1,0:T(8,128)S(1)}, u32[]{:S(2)}, u32[]{:S(2)}) collective-permute-start(f32[8,32,128]{2,1,0:T(8,128)S(1)} %broadcast_select_fusion.20), channel_id=1, source_target_pairs={{0,2},{1,3},{2,4},{3,5},{4,6},{5,7},{6,8},{7,9},{8,10},{9,11},{10,... | collective-permute-start | bytes 393224 | tf_op jit(solution)/shard_map/ppermute | solution.py:14
  234.9 13.6 %collective-permute-start.13 = (f32[8,32,128]{2,1,0:T(8,128)S(1)}, f32[8,32,128]{2,1,0:T(8,128)S(1)}, u32[]{:S(2)}, u32[]{:S(2)}) collective-permute-start(f32[8,32,128]{2,1,0:T(8,128)S(1)} %broadcast_select_fusion.16), channel_id=1, source_target_pairs={{0,2},{1,3},{2,4},{3,5},{4,6},{5,7},{6,8},{7,9},{8,10},{9,11},{10,... | collective-permute-start | bytes 393224 | tf_op jit(solution)/shard_map/ppermute | solution.py:14
  240.6 12.3 %collective-permute-start.8 = (f32[8,32,128]{2,1,0:T(8,128)S(1)}, f32[8,32,128]{2,1,0:T(8,128)S(1)}, u32[]{:S(2)}, u32[]{:S(2)}) collective-permute-start(f32[8,32,128]{2,1,0:T(8,128)S(1)} %broadcast_select_fusion.21), channel_id=1, source_target_pairs={{0,4},{1,5},{2,6},{3,7},{4,8},{5,9},{6,10},{7,11},{8,12},{9,13},{1... | collective-permute-start | bytes 393224 | tf_op jit(solution)/shard_map/ppermute | solution.py:14
  248.5 13.1 %collective-permute-start.14 = (f32[8,32,128]{2,1,0:T(8,128)S(1)}, f32[8,32,128]{2,1,0:T(8,128)S(1)}, u32[]{:S(2)}, u32[]{:S(2)}) collective-permute-start(f32[8,32,128]{2,1,0:T(8,128)S(1)} %broadcast_select_fusion.17), channel_id=1, source_target_pairs={{0,4},{1,5},{2,6},{3,7},{4,8},{5,9},{6,10},{7,11},{8,12},{9,13},{1... | collective-permute-start | bytes 393224 | tf_op jit(solution)/shard_map/ppermute | solution.py:14
  252.9 11.9 %collective-permute-start.9 = (f32[8,32,128]{2,1,0:T(8,128)S(1)}, f32[8,32,128]{2,1,0:T(8,128)S(1)}, u32[]{:S(2)}, u32[]{:S(2)}) collective-permute-start(f32[8,32,128]{2,1,0:T(8,128)S(1)} %broadcast_select_fusion.22), channel_id=1, source_target_pairs={{0,8},{1,9},{2,10},{3,11},{4,12},{5,13},{6,14},{7,15},{8,0},{9,1},... | collective-permute-start | bytes 393224 | tf_op jit(solution)/shard_map/ppermute | solution.py:14
  277.6 25.5 %collective-permute-start.19 = (f32[8,8,32,128]{3,2,1,0:T(8,128)S(1)}, f32[8,8,32,128]{3,2,1,0:T(8,128)S(1)}, u32[]{:S(2)}, u32[]{:S(2)}) collective-permute-start(f32[8,8,32,128]{3,2,1,0:T(8,128)S(1)} %pad_maximum_fusion.6), channel_id=1, source_target_pairs={{0,1},{1,2},{2,3},{3,4},{4,5},{5,6},{6,7},{7,8},{8,9},{9,10},{10,1... | collective-permute-start | bytes 3145736 | tf_op jit(solution)/shard_map/ppermute | solution.py:14
  303.3 49.8 %collective-permute-start.20 = (f32[8,8,32,128]{3,2,1,0:T(8,128)S(1)}, f32[8,8,32,128]{3,2,1,0:T(8,128)S(1)}, u32[]{:S(2)}, u32[]{:S(2)}) collective-permute-start(f32[8,8,32,128]{3,2,1,0:T(8,128)S(1)} %broadcast_select_fusion.4), channel_id=1, source_target_pairs={{0,2},{1,3},{2,4},{3,5},{4,6},{5,7},{6,8},{7,9},{8,10},{9,11},{10,... | collective-permute-start | bytes 3145736 | tf_op jit(solution)/shard_map/ppermute | solution.py:14
  353.4 47.7 %collective-permute-start.21 = (f32[8,8,32,128]{3,2,1,0:T(8,128)S(1)}, f32[8,8,32,128]{3,2,1,0:T(8,128)S(1)}, u32[]{:S(2)}, u32[]{:S(2)}) collective-permute-start(f32[8,8,32,128]{3,2,1,0:T(8,128)S(1)} %broadcast_select_fusion.5), channel_id=1, source_target_pairs={{0,4},{1,5},{2,6},{3,7},{4,8},{5,9},{6,10},{7,11},{8,12},{9,13},{1... | collective-permute-start | bytes 3145736 | tf_op jit(solution)/shard_map/ppermute | solution.py:14
  401.4 24.7 %collective-permute-start.22 = (f32[8,8,32,128]{3,2,1,0:T(8,128)S(1)}, f32[8,8,32,128]{3,2,1,0:T(8,128)S(1)}, u32[]{:S(2)}, u32[]{:S(2)}) collective-permute-start(f32[8,8,32,128]{3,2,1,0:T(8,128)S(1)} %broadcast_select_fusion.6), channel_id=1, source_target_pairs={{0,8},{1,9},{2,10},{3,11},{4,12},{5,13},{6,14},{7,15},{8,0},{9,1},... | collective-permute-start | bytes 3145736 | tf_op jit(solution)/shard_map/ppermute | solution.py:14
  426.3 26.0 %collective-permute-start.23 = (f32[8,8,32,128]{3,2,1,0:T(8,128)S(1)}, f32[8,8,32,128]{3,2,1,0:T(8,128)}, u32[]{:S(2)}, u32[]{:S(2)}) collective-permute-start(f32[8,8,32,128]{3,2,1,0:T(8,128)S(1)} %broadcast_select_fusion.7), channel_id=1, source_target_pairs={{0,1},{1,2},{2,3},{3,4},{4,5},{5,6},{6,7},{7,8},{8,9},{9,10},{10,1... | collective-permute-start | bytes 3145736 | tf_op jit(solution)/shard_map/ppermute | solution.py:14
  482.9 9.8 %collective-permute-start.24 = (f32[8,1,32,128]{3,2,0,1:T(8,128)S(1)}, f32[8,1,32,128]{3,2,0,1:T(8,128)S(1)}, u32[]{:S(2)}, u32[]{:S(2)}) collective-permute-start(f32[8,1,32,128]{3,2,0,1:T(8,128)S(1)} %get-tuple-element.111), channel_id=1, source_target_pairs={{0,16},{16,32},{32,48},{48,64},{64,80},{80,96},{96,112},{112,128},... | collective-permute-start | bytes 393224 | tf_op jit(solution)/shard_map/ppermute | solution.py:23
  497.1 9.3 %collective-permute-start.31 = (f32[8,32,128]{2,1,0:T(8,128)S(1)}, f32[8,32,128]{2,1,0:T(8,128)S(1)}, u32[]{:S(2)}, u32[]{:S(2)}) collective-permute-start(f32[8,32,128]{2,1,0:T(8,128)S(1)} %bitcast.104), channel_id=1, source_target_pairs={{0,1},{1,2},{2,3},{3,4},{4,5},{5,6},{6,7},{7,8},{8,9},{9,10},{10,1... | collective-permute-start | bytes 393224 | tf_op jit(solution)/shard_map/ppermute | solution.py:14
  506.4 14.3 %collective-permute-start.32 = (f32[8,32,128]{2,1,0:T(8,128)S(1)}, f32[8,32,128]{2,1,0:T(8,128)S(1)}, u32[]{:S(2)}, u32[]{:S(2)}) collective-permute-start(f32[8,32,128]{2,1,0:T(8,128)S(1)} %broadcast_select_fusion.8), channel_id=1, source_target_pairs={{0,2},{1,3},{2,4},{3,5},{4,6},{5,7},{6,8},{7,9},{8,10},{9,11},{10,... | collective-permute-start | bytes 393224 | tf_op jit(solution)/shard_map/ppermute | solution.py:14
  508.2 12.6 %collective-permute-start.27 = (f32[8,32,128]{2,1,0:T(8,128)S(1)}, f32[8,32,128]{2,1,0:T(8,128)S(1)}, u32[]{:S(2)}, u32[]{:S(2)}) collective-permute-start(f32[8,32,128]{2,1,0:T(8,128)S(1)} %broadcast_select_fusion.13), channel_id=1, source_target_pairs={{0,4},{1,5},{2,6},{3,7},{4,8},{5,9},{6,10},{7,11},{8,12},{9,13},{1... | collective-permute-start | bytes 393224 | tf_op jit(solution)/shard_map/ppermute | solution.py:14
  520.7 11.8 %collective-permute-start.33 = (f32[8,32,128]{2,1,0:T(8,128)S(1)}, f32[8,32,128]{2,1,0:T(8,128)S(1)}, u32[]{:S(2)}, u32[]{:S(2)}) collective-permute-start(f32[8,32,128]{2,1,0:T(8,128)S(1)} %broadcast_select_fusion.9), channel_id=1, source_target_pairs={{0,4},{1,5},{2,6},{3,7},{4,8},{5,9},{6,10},{7,11},{8,12},{9,13},{1... | collective-permute-start | bytes 393224 | tf_op jit(solution)/shard_map/ppermute | solution.py:14
  520.8 11.8 %collective-permute-start.28 = (f32[8,32,128]{2,1,0:T(8,128)S(1)}, f32[8,32,128]{2,1,0:T(8,128)S(1)}, u32[]{:S(2)}, u32[]{:S(2)}) collective-permute-start(f32[8,32,128]{2,1,0:T(8,128)S(1)} %broadcast_select_fusion.14), channel_id=1, source_target_pairs={{0,8},{1,9},{2,10},{3,11},{4,12},{5,13},{6,14},{7,15},{8,0},{9,1},... | collective-permute-start | bytes 393224 | tf_op jit(solution)/shard_map/ppermute | solution.py:14
  532.6 8.4 %collective-permute-start.34 = (f32[8,32,128]{2,1,0:T(8,128)S(1)}, f32[8,32,128]{2,1,0:T(8,128)S(1)}, u32[]{:S(2)}, u32[]{:S(2)}) collective-permute-start(f32[8,32,128]{2,1,0:T(8,128)S(1)} %broadcast_select_fusion.10), channel_id=1, source_target_pairs={{0,8},{1,9},{2,10},{3,11},{4,12},{5,13},{6,14},{7,15},{8,0},{9,1},... | collective-permute-start | bytes 393224 | tf_op jit(solution)/shard_map/ppermute | solution.py:14
  532.7 8.3 %collective-permute-start.29 = (f32[8,32,128]{2,1,0:T(8,128)S(1)}, f32[8,32,128]{2,1,0:T(8,128)S(1)}, u32[]{:S(2)}, u32[]{:S(2)}) collective-permute-start(f32[8,32,128]{2,1,0:T(8,128)S(1)} %broadcast_select_fusion.15), channel_id=1, source_target_pairs={{0,1},{1,2},{2,3},{3,4},{4,5},{5,6},{6,7},{7,8},{8,9},{9,10},{10,1... | collective-permute-start | bytes 393224 | tf_op jit(solution)/shard_map/ppermute | solution.py:14
  (31 other events, 956.3 us)
where the time goes:
time: 560 us; the launch traced here: 551 us
  waiting for transfers between devices  416 us (74%)
  local copies, waits for them, and re-layouts  68.3 us (12%)
  starting transfers between devices  44.9 us (8%)
  other arithmetic  14.7 us (3%)
  between operations  6.93 us (1%)
    ppermute x30, waiting for transfers between devices, shifted_2(): return lax.ppermute(value, axis, pairs)  411 us
    ppermute x30, starting transfers between devices, shifted_2(): return lax.ppermute(value, axis, pairs)  30.7 us
    gather x4, local copies, waits for them, and re-layouts, column(): nearer = lax.dynamic_slice_in_dim(stripe, anchor, extent, 2)  18.8 us
    gather x4, local copies, waits for them, and re-layouts, column(): farther = lax.dynamic_slice_in_dim(stripe, anchor - 1, extent, 2)  18.8 us
    concatenate x2, local copies, waits for them, and re-layouts, take_rows(): joined = jnp.concatenate([earlier, turned], axis=3)  15.1 us
    ppermute x4, starting transfers between devices, padded_2(): lax.ppermute(lax.slice_in_dim(block, 0, width, axis=dim), axis, backward)  14.2 us
  transfers between devices with their start and end apart: 38, of which 27 were waited for; matrix products, arithmetic and copies ran while one was open for 3% of the time, Pallas kernels for 0%

commit v1 on v0

v1 whole, which is shorter than its diff:
```python
import jax
import jax.numpy as jnp
from jax import lax
from jax.experimental import pallas as pl
from jax.experimental.pallas import tpu as pltpu
from jax.sharding import PartitionSpec as P

spin_gain = 0.2
spin_drag = 0.05
tidal_gain = 0.3

LANES = 128
BLOCKS = 16
COLS = 8
HALF_VARS = 4
LEVELS = 4
COL_ROWS = HALF_VARS * LEVELS
ROWS = COLS * COL_ROWS
RIM = ROWS // LEVELS
HALVES = 2
LEVEL_BLOCKS = 8

F32 = jnp.float32
VMEM = pl.BlockSpec(memory_space=pltpu.VMEM)
SMEM = pl.BlockSpec(memory_space=pltpu.SMEM)
PARAMS = pltpu.CompilerParams(vmem_limit_bytes=24 * 1024 * 1024)


def shape(*dims):
    return jax.ShapeDtypeStruct(dims, F32)


def cost(flops, moved):
    return pl.CostEstimate(flops=flops, bytes_accessed=moved, transcendentals=0)


def lane_index():
    return lax.broadcasted_iota(jnp.int32, (8, LANES), 1)


def row_index():
    return lax.broadcasted_iota(jnp.int32, (8, LANES), 0)


def rotated(block, earlier, amount, lanes):
    joined = jnp.where(lanes < LANES - amount, block, earlier)
    return pltpu.roll(joined, amount & (LANES - 1), 1)


def pack_kernel(state, out):
    for half in range(HALVES):
        for col in range(COLS):
            for pair in range(2):
                var = half * HALF_VARS + 2 * pair
                base = col * COL_ROWS + pair * 8
                for tile in range(LEVEL_BLOCKS // 2):
                    first = state[var, col, pl.ds(tile * 8, 8), :]
                    second = state[var + 1, col, pl.ds(tile * 8, 8), :]
                    dest = half * LEVEL_BLOCKS + 2 * tile
                    out[dest, pl.ds(base, 8), :] = jnp.concatenate([first[:4], second[:4]], axis=0)
                    out[dest + 1, pl.ds(base, 8), :] = jnp.concatenate([first[4:], second[4:]], axis=0)


def unpack_kernel(packed, out):
    for half in range(HALVES):
        for col in range(COLS):
            for pair in range(2):
                var = half * HALF_VARS + 2 * pair
                base = col * COL_ROWS + pair * 8
                for tile in range(LEVEL_BLOCKS // 2):
                    source = half * LEVEL_BLOCKS + 2 * tile
                    low = packed[source, pl.ds(base, 8), :]
                    high = packed[source + 1, pl.ds(base, 8), :]
                    out[var, col, pl.ds(tile * 8, 8), :] = jnp.concatenate([low[:4], high[:4]], axis=0)
                    out[var + 1, col, pl.ds(tile * 8, 8), :] = jnp.concatenate([low[4:], high[4:]], axis=0)


def advect(step, shifts, fracs, values, adv, col_low, col_high, level_low, level_high):
    lanes = lane_index()
    turns = [shifts[step, col] for col in range(COLS)]
    far = [fracs[step, col] for col in range(COLS)]
    near = [1.0 - weight for weight in far]

    def block_step(block, carry):
        for col in range(COLS):
            source = (block - turns[col] // LANES) & (BLOCKS - 1)
            before = (source - 1) & (BLOCKS - 1)
            rest = turns[col] & (LANES - 1)
            for pair in range(2):
                rows = pl.ds(col * COL_ROWS + pair * 8, 8)
                here = values[source, rows, :]
                earlier = values[before, rows, :]
                nearer = rotated(here, earlier, rest, lanes)
                farther = rotated(here, earlier, rest + 1, lanes)
                result = near[col] * nearer + far[col] * farther
                adv[block, rows, :] = result
                if col == 0:
                    col_low[block, pl.ds(pair * 8, 8), :] = result
                if col == COLS - 1:
                    col_high[block, pl.ds(pair * 8, 8), :] = result
        level_low[block] = adv[block, pl.ds(0, RIM, stride=LEVELS), :]
        level_high[block] = adv[block, pl.ds(LEVELS - 1, RIM, stride=LEVELS), :]
        return carry

    lax.fori_loop(0, BLOCKS, block_step, 0)


def ghost_roll(source, target, amount):
    lanes = lane_index()
    whole = amount // LANES
    rest = amount & (LANES - 1)

    def block_step(block, carry):
        here = (block - whole) & (BLOCKS - 1)
        before = (here - 1) & (BLOCKS - 1)
        for pair in range(2):
            rows = pl.ds(pair * 8, 8)
            target[block, rows, :] = rotated(source[here, rows, :], source[before, rows, :], rest, lanes)
        return carry

    lax.fori_loop(0, BLOCKS, block_step, 0)


def diffuse(step, place, offsets, kappa, adv, col_before, col_after, level_below, level_above, out,
            ghost_low, ghost_high, under, over):
    radial, half, vertical = place[0], place[1], place[2]
    total_y = BLOCKS * LANES
    offset = offsets[step]
    ghost_roll(col_before, ghost_low, jnp.where(radial == 0, offset, 0))
    ghost_roll(col_after, ghost_high, jnp.where(radial == place[3] - 1, (total_y - offset) & (total_y - 1), 0))
    lanes = lane_index()
    rows8 = row_index()
    level = rows8 & (LEVELS - 1)
    upper_rows = rows8 >= LEVELS
    bottom = level == 0
    top = level == LEVELS - 1
    rates = [
        jnp.where(upper_rows, kappa[half * HALF_VARS + 2 * pair + 1], kappa[half * HALF_VARS + 2 * pair])
        for pair in range(2)
    ]
    coupled = jnp.where(half == 0, 1.0, 0.0)
    gain = jnp.where(upper_rows, spin_gain * coupled, 0.0)
    drag = jnp.where(upper_rows, 0.0, -spin_drag * coupled)
    total_x = (place[3] * COLS).astype(F32)
    tides = []
    for col in range(COLS):
        position = ((radial * COLS + col).astype(F32) + 0.5) / total_x - 0.5
        tides.append(jnp.where(upper_rows, tidal_gain * position * coupled, 0.0))
    has_below = vertical > 0
    has_above = vertical < LEVEL_BLOCKS - 1

    def block_step(block, carry):
        after = (block + 1) & (BLOCKS - 1)
        before = (block - 1) & (BLOCKS - 1)
        low_rim = pl.ds(0, RIM, stride=LEVELS)
        high_rim = pl.ds(LEVELS - 1, RIM, stride=LEVELS)
        under[low_rim, :] = jnp.where(has_below, level_below[block], adv[block, low_rim, :])
        over[high_rim, :] = jnp.where(has_above, level_above[block], adv[block, high_rim, :])
        for col in range(COLS):
            mixed = []
            for pair in range(2):
                base = col * COL_ROWS + pair * 8
                rows = pl.ds(base, 8)
                value = adv[block, rows, :]
                if col > 0:
                    inner = adv[block, pl.ds(base - COL_ROWS, 8), :]
                else:
                    inner = ghost_low[block, pl.ds(pair * 8, 8), :]
                if col < COLS - 1:
                    outer = adv[block, pl.ds(base + COL_ROWS, 8), :]
                else:
                    outer = ghost_high[block, pl.ds(pair * 8, 8), :]
                prior = pltpu.roll(jnp.where(lanes < LANES - 1, value, adv[before, rows, :]), 1, 1)
                following = pltpu.roll(jnp.where(lanes >= 1, value, adv[after, rows, :]), LANES - 1, 1)
                lower = jnp.where(bottom, under[rows, :], pltpu.roll(value, 1, 0))
                upper = jnp.where(top, over[rows, :], pltpu.roll(value, 7, 0))
                laplace = (inner + outer) + (prior + following) + (lower + upper) - 6.0 * value
                mixed.append(value + rates[pair] * laplace)
            swapped = [pltpu.roll(part, 4, 0) for part in mixed]
            first = mixed[0] + gain * swapped[1] + tides[col] * swapped[0]
            second = mixed[1] + drag * swapped[0]
            out[block, pl.ds(col * COL_ROWS, 8), :] = first
            out[block, pl.ds(col * COL_ROWS + 8, 8), :] = second
        return carry

    lax.fori_loop(0, BLOCKS, block_step, 0)


def pack(state):
    return pl.pallas_call(
        pack_kernel,
        out_shape=shape(BLOCKS, ROWS, LANES),
        in_specs=[VMEM],
        out_specs=VMEM,
        compiler_params=PARAMS,
        name="pack",
    )(state)


def unpack(packed):
    return pl.pallas_call(
        unpack_kernel,
        out_shape=shape(HALVES * HALF_VARS, COLS, LEVELS * LEVEL_BLOCKS, LANES),
        in_specs=[VMEM],
        out_specs=VMEM,
        compiler_params=PARAMS,
        name="unpack",
    )(packed)


ADVECTED = (
    shape(BLOCKS, ROWS, LANES),
    shape(BLOCKS, COL_ROWS, LANES),
    shape(BLOCKS, COL_ROWS, LANES),
    shape(BLOCKS, RIM, LANES),
    shape(BLOCKS, RIM, LANES),
)
GHOSTS = [
    pltpu.VMEM((BLOCKS, COL_ROWS, LANES), F32),
    pltpu.VMEM((BLOCKS, COL_ROWS, LANES), F32),
    pltpu.VMEM((ROWS, LANES), F32),
    pltpu.VMEM((ROWS, LANES), F32),
]


def first_advect(step, shifts, fracs, values):
    def kernel(shifts, fracs, values, *outs):
        advect(step, shifts, fracs, values, *outs)

    return pl.pallas_call(
        kernel,
        out_shape=ADVECTED,
        in_specs=[SMEM, SMEM, VMEM],
        out_specs=(VMEM,) * 5,
        compiler_params=PARAMS,
        name="advect",
    )(shifts, fracs, values)


def diffuse_advect(step, place, offsets, kappa, shifts, fracs, adv, halos):
    def kernel(place, offsets, kappa, shifts, fracs, adv, h0, h1, h2, h3, o0, o1, o2, o3, o4,
               current, ghost_low, ghost_high, under, over):
        diffuse(step, place, offsets, kappa, adv, h0, h1, h2, h3, current, ghost_low, ghost_high, under, over)
        advect(step + 1, shifts, fracs, current, o0, o1, o2, o3, o4)

    return pl.pallas_call(
        kernel,
        out_shape=ADVECTED,
        in_specs=[SMEM] * 5 + [VMEM] * 5,
        out_specs=(VMEM,) * 5,
        scratch_shapes=[pltpu.VMEM((BLOCKS, ROWS, LANES), F32)] + GHOSTS,
        compiler_params=PARAMS,
        name="diffuse_advect",
    )(place, offsets, kappa, shifts, fracs, adv, *halos)


def last_diffuse(step, place, offsets, kappa, adv, halos):
    def kernel(place, offsets, kappa, adv, h0, h1, h2, h3, out, ghost_low, ghost_high, under, over):
        diffuse(step, place, offsets, kappa, adv, h0, h1, h2, h3, out, ghost_low, ghost_high, under, over)

    return pl.pallas_call(
        kernel,
        out_shape=shape(BLOCKS, ROWS, LANES),
        in_specs=[SMEM] * 3 + [VMEM] * 5,
        out_specs=VMEM,
        scratch_shapes=GHOSTS,
        compiler_params=PARAMS,
        name="last_diffuse",
    )(place, offsets, kappa, adv, *halos)


def exchange(rims):
    col_low, col_high, level_low, level_high = rims
    radial_size = lax.axis_size("gx")
    up = [(i, (i + 1) % radial_size) for i in range(radial_size)]
    down = [(target, source) for source, target in up]
    ring = [
        (half * LEVEL_BLOCKS + block, half * LEVEL_BLOCKS + (block + 1) % LEVEL_BLOCKS)
        for half in range(HALVES)
        for block in range(LEVEL_BLOCKS)
    ]
    back = [(target, source) for source, target in ring]
    level_below = lax.ppermute(level_high, "gy", ring)
    level_above = lax.ppermute(level_low, "gy", back)
    col_before = lax.ppermute(col_high, "gx", up)
    col_after = lax.ppermute(col_low, "gx", down)
    return col_before, col_after, level_below, level_above


def on_device(state, shifts, fracs, offsets, kappa):
    around = lax.axis_index("gy")
    place = jnp.stack(
        [
            lax.axis_index("gx"),
            around // LEVEL_BLOCKS,
            around % LEVEL_BLOCKS,
            jnp.int32(lax.axis_size("gx")),
        ]
    ).astype(jnp.int32)
    steps = shifts.shape[0]
    values = lax.all_to_all(pack(state), "gy", 0, 0, tiled=True)
    adv, *rims = first_advect(0, shifts, fracs, values)
    for step in range(steps - 1):
        adv, *rims = diffuse_advect(step, place, offsets, kappa, shifts, fracs, adv, exchange(rims))
    values = last_diffuse(steps - 1, place, offsets, kappa, adv, exchange(rims))
    return unpack(lax.all_to_all(values, "gy", 0, 0, tiled=True))


def solution(mesh):
    placed = (P(None, "gx", None, "gy"), P(None, "gx"), P(None, "gx"), P(), P())
    return jax.shard_map(
        on_device, mesh=mesh, in_specs=placed, out_specs=P(None, "gx", None, "gy"), check_vma=False
    )
```

time: 560 us -> 107 us (0.19)
  the two profiles are of different devices: /device:TPU:28 before, /device:TPU:32 now
where the time goes in v1:
time: 107 us
  blocking collectives  70 us (65%)
  Pallas kernels  15.4 us (14%)
  starting transfers between devices  15 us (14%)
  waiting for transfers between devices  5.36 us (5%)
  local copies, waits for them, and re-layouts  1.24 us (1%)
    all_to_all x1, blocking collectives, on_device(): values = lax.all_to_all(pack(state), 'gy', 0, 0, tiled=True)  35.6 us
    all_to_all x1, blocking collectives, on_device(): return unpack(lax.all_to_all(values, 'gy', 0, 0, tiled=True))  34.4 us
    ppermute x2, starting transfers between devices, exchange(): col_after = lax.ppermute(col_low, 'gx', down)  9.81 us
    pallas_call x1, Pallas kernels, diffuse_advect(): pl.pallas_call(kernel, out_shape=ADVECTED, in_specs=[SMEM] * 5 + [VMEM] *...  6.87 us
    ppermute x2, waiting for transfers between devices, exchange(): col_before = lax.ppermute(col_high, 'gx', up)  5.34 us
    pallas_call x1, Pallas kernels, last_diffuse(): pl.pallas_call(kernel, out_shape=shape(BLOCKS, ROWS, LANES), in_specs=[SM...  4.79 us
    pallas_call x1, Pallas kernels, first_advect(): pl.pallas_call(kernel, out_shape=ADVECTED, in_specs=[SMEM, SMEM, VMEM], o...  2.67 us
    ppermute x2, starting transfers between devices, exchange(): level_below = lax.ppermute(level_high, 'gy', ring)  2.3 us
  transfers between devices with their start and end apart: 8, of which 2 were waited for; matrix products, arithmetic and copies ran while one was open for 0% of the time, Pallas kernels for 0%

profile of v1, /device:TPU:32, one launch (start us, length us, event | category | flops | bytes accessed | tf_op | source)
XLA Modules:
  0.0 107.2 jit_solution(11443711148514301323)
XLA Ops:
  0.0 1.2 %copy-done = f32[8,8,32,128]{3,2,1,0:T(8,128)S(1)} copy-done((f32[8,8,32,128]{3,2,1,0:T(8,128)S(1)}, f32[8,8,32,128]{3,2,1,0:T(8,128)}, u32[]{:S(2)}) %copy-start) | copy-done | bytes 1048600
  1.2 0.1 pack.1
  1.3 0.0 copy-start.1
  1.3 0.0 copy-start.2
  1.3 35.6 %all_to_all.10.values = f32[16,128,128]{2,1,0:T(8,128)S(1)} all-to-all(f32[16,128,128]{2,1,0:T(8,128)S(1)} %pack.1), channel_id=1, replica_groups=mesh['gx'=16,'gy'=16] {'gy'}, dimensions={0} | all-to-all | bytes 2097152 | tf_op jit(solution)/shard_map/all_to_all | solution.py:301
  36.9 2.7 %advect.1 = (f32[16,128,128]{2,1,0:T(8,128)S(1)}, f32[16,16,128]{2,1,0:T(8,128)S(1)}, f32[16,16,128]{2,1,0:T(8,128)S(1)}, f32[16,32,128]{2,1,0:T(8,128)S(1)}, f32[16,32,128]{2,1,0:T(8,128)S(1)}) custom-call(s32[2,8]{1,0:T(2,128)S(1)} %copy-done.1, f32[2,8]{1,0:T(2,128)S(1)} %copy-done.2, f32[16,128,128]{2,1,0:T(8,128)S(1)} %all_to_all.10.values), custom_call_target="tpu_custom_call" | custom-call | tf_op jit(solution)/shard_map/advect/pallas_call | solution.py:230
  39.6 1.1 %collective-permute-start.2 = (f32[16,32,128]{2,1,0:T(8,128)S(1)}, f32[16,32,128]{2,1,0:T(8,128)S(1)}, u32[]{:S(2)}, u32[]{:S(2)}) collective-permute-start(f32[16,32,128]{2,1,0:T(8,128)S(1)} %get-tuple-element.18), channel_id=1, source_target_pairs={{0,1},{1,2},{2,3},{3,4},{4,5},{5,6},{6,7},{7,0},{8,9},{9,10},{10,1... | collective-permute-start | bytes 786440 | tf_op jit(solution)/shard_map/ppermute | solution.py:283
  40.8 0.9 collective-permute-start.3
  41.7 0.0 collective-permute-start
  41.7 5.4 %collective-permute-start.1 = (f32[16,16,128]{2,1,0:T(8,128)S(1)}, f32[16,16,128]{2,1,0:T(8,128)S(1)}, u32[]{:S(2)}, u32[]{:S(2)}) collective-permute-start(f32[16,16,128]{2,1,0:T(8,128)S(1)} %get-tuple-element.17), channel_id=1, source_target_pairs={{16,0},{32,16},{48,32},{64,48},{80,64},{96,80},{112,96},{128,112},... | collective-permute-start | bytes 393224 | tf_op jit(solution)/shard_map/ppermute | solution.py:286
  47.1 0.1 pad_add_fusion.place
  47.1 2.6 %collective-permute-done.h0 = f32[16,16,128]{2,1,0:T(8,128)S(1)} collective-permute-done((f32[16,16,128]{2,1,0:T(8,128)S(1)}, f32[16,16,128]{2,1,0:T(8,128)S(1)}, u32[]{:S(2)}, u32[]{:S(2)}) %collective-permute-start) | collective-permute-done | bytes 131104 | tf_op jit(solution)/shard_map/ppermute | solution.py:285
  49.7 0.0 collective-permute-done.1.h1
  49.7 0.0 collective-permute-done.2.h2
  49.8 0.0 collective-permute-done.3.h3
  49.8 6.9 %diffuse_advect.1 = (f32[16,128,128]{2,1,0:T(8,128)S(1)}, f32[16,16,128]{2,1,0:T(8,128)S(1)}, f32[16,16,128]{2,1,0:T(8,128)S(1)}, f32[16,32,128]{2,1,0:T(8,128)S(1)}, f32[16,32,128]{2,1,0:T(8,128)S(1)}) custom-call(s32[4]{0:T(128)S(1)} %pad_add_fusion.place, s32[2]{0:T(128)S(1)} %copy-done.3, f32[8]{0:T(128)S(1)} %copy-done.4, s32[2,8]{1,0:T(2,128)S(1)} %copy-done.1, ...), custom_call_target="tpu_custom_call" | custom-call | tf_op jit(solution)/shard_map/diffuse_advect/pallas_call | solution.py:246
  56.6 1.2 %collective-permute-start.6 = (f32[16,32,128]{2,1,0:T(8,128)S(1)}, f32[16,32,128]{2,1,0:T(8,128)S(1)}, u32[]{:S(2)}, u32[]{:S(2)}) collective-permute-start(f32[16,32,128]{2,1,0:T(8,128)S(1)} %get-tuple-element.23), channel_id=1, source_target_pairs={{0,1},{1,2},{2,3},{3,4},{4,5},{5,6},{6,7},{7,0},{8,9},{9,10},{10,1... | collective-permute-start | bytes 786440 | tf_op jit(solution)/shard_map/ppermute | solution.py:283
  57.8 1.0 collective-permute-start.7
  58.8 0.9 collective-permute-start.4
  59.7 4.5 %collective-permute-start.5 = (f32[16,16,128]{2,1,0:T(8,128)S(1)}, f32[16,16,128]{2,1,0:T(8,128)S(1)}, u32[]{:S(2)}, u32[]{:S(2)}) collective-permute-start(f32[16,16,128]{2,1,0:T(8,128)S(1)} %get-tuple-element.22), channel_id=1, source_target_pairs={{16,0},{32,16},{48,32},{64,48},{80,64},{96,80},{112,96},{128,112},... | collective-permute-start | bytes 393224 | tf_op jit(solution)/shard_map/ppermute | solution.py:286
  64.2 2.7 %collective-permute-done.4.h0 = f32[16,16,128]{2,1,0:T(8,128)S(1)} collective-permute-done((f32[16,16,128]{2,1,0:T(8,128)S(1)}, f32[16,16,128]{2,1,0:T(8,128)S(1)}, u32[]{:S(2)}, u32[]{:S(2)}) %collective-permute-start.4) | collective-permute-done | bytes 131104 | tf_op jit(solution)/shard_map/ppermute | solution.py:285
  67.0 4.8 %last_diffuse.1 = f32[16,128,128]{2,1,0:T(8,128)S(1)} custom-call(s32[4]{0:T(128)S(1)} %pad_add_fusion.place, s32[2]{0:T(128)S(1)} %copy-done.3, f32[8]{0:T(128)S(1)} %copy-done.4, f32[16,128,128]{2,1,0:T(8,128)S(1)} %get-tuple-element.20.adv, f32[16,16,128]{2,1,0:T(8,128)S(1)} %collective-permute-done.4.h0, f32[16,16,128]{2,1,0:T(8,128)S(1)} %collective-permute-done.5.h1, ...), custom_call_target="tpu_custom_call" | custom-call | tf_op jit(solution)/shard_map/last_diffuse/pallas_call | solution.py:261
  71.8 34.4 %all_to_all.11.packed = f32[16,128,128]{2,1,0:T(8,128)S(1)} all-to-all(f32[16,128,128]{2,1,0:T(8,128)S(1)} %last_diffuse.1), channel_id=1, replica_groups=mesh['gx'=16,'gy'=16] {'gy'}, dimensions={0} | all-to-all | bytes 2097152 | tf_op jit(solution)/shard_map/all_to_all | solution.py:306
  106.1 1.0 unpack.1
  (10 shorter events, 0.0 us)
Async XLA Ops:
  0.0 1.2 %copy-start = (f32[8,8,32,128]{3,2,1,0:T(8,128)S(1)}, f32[8,8,32,128]{3,2,1,0:T(8,128)}, u32[]{:S(2)}) copy-start(f32[8,8,32,128]{3,2,1,0:T(8,128)} %state.1) | copy-start | bytes 3145732
  1.3 35.6 %copy-start.1 = (s32[2,8]{1,0:T(2,128)S(1)}, s32[2,8]{1,0:T(2,128)}, u32[]{:S(2)}) copy-start(s32[2,8]{1,0:T(2,128)} %shifts.3) | copy-start | bytes 196
  1.3 35.6 %copy-start.2 = (f32[2,8]{1,0:T(2,128)S(1)}, f32[2,8]{1,0:T(2,128)}, u32[]{:S(2)}) copy-start(f32[2,8]{1,0:T(2,128)} %fracs.3) | copy-start | bytes 196
  39.6 10.1 %collective-permute-start.2 = (f32[16,32,128]{2,1,0:T(8,128)S(1)}, f32[16,32,128]{2,1,0:T(8,128)S(1)}, u32[]{:S(2)}, u32[]{:S(2)}) collective-permute-start(f32[16,32,128]{2,1,0:T(8,128)S(1)} %get-tuple-element.18), channel_id=1, source_target_pairs={{0,1},{1,2},{2,3},{3,4},{4,5},{5,6},{6,7},{7,0},{8,9},{9,10},{10,1... | collective-permute-start | bytes 786440 | tf_op jit(solution)/shard_map/ppermute | solution.py:283
  40.8 9.0 %collective-permute-start.3 = (f32[16,32,128]{2,1,0:T(8,128)S(1)}, f32[16,32,128]{2,1,0:T(8,128)S(1)}, u32[]{:S(2)}, u32[]{:S(2)}) collective-permute-start(f32[16,32,128]{2,1,0:T(8,128)S(1)} %get-tuple-element.19), channel_id=1, source_target_pairs={{1,0},{2,1},{3,2},{4,3},{5,4},{6,5},{7,6},{0,7},{9,8},{10,9},{11,1... | collective-permute-start | bytes 786440 | tf_op jit(solution)/shard_map/ppermute | solution.py:284
  41.7 8.0 %collective-permute-start = (f32[16,16,128]{2,1,0:T(8,128)S(1)}, f32[16,16,128]{2,1,0:T(8,128)S(1)}, u32[]{:S(2)}, u32[]{:S(2)}) collective-permute-start(f32[16,16,128]{2,1,0:T(8,128)S(1)} %get-tuple-element.16), channel_id=1, source_target_pairs={{0,16},{16,32},{32,48},{48,64},{64,80},{80,96},{96,112},{112,128},... | collective-permute-start | bytes 393224 | tf_op jit(solution)/shard_map/ppermute | solution.py:285
  41.7 8.0 %collective-permute-start.1 = (f32[16,16,128]{2,1,0:T(8,128)S(1)}, f32[16,16,128]{2,1,0:T(8,128)S(1)}, u32[]{:S(2)}, u32[]{:S(2)}) collective-permute-start(f32[16,16,128]{2,1,0:T(8,128)S(1)} %get-tuple-element.17), channel_id=1, source_target_pairs={{16,0},{32,16},{48,32},{64,48},{80,64},{96,80},{112,96},{128,112},... | collective-permute-start | bytes 393224 | tf_op jit(solution)/shard_map/ppermute | solution.py:286
  47.1 2.6 %copy-start.3 = (s32[2]{0:T(128)S(1)}, s32[2]{0:T(128)}, u32[]{:S(2)}) copy-start(s32[2]{0:T(128)} %offsets.3) | copy-start | bytes 28
  47.1 2.6 %copy-start.4 = (f32[8]{0:T(128)S(1)}, f32[8]{0:T(128)}, u32[]{:S(2)}) copy-start(f32[8]{0:T(128)} %kappa.3) | copy-start | bytes 100
  56.6 10.3 %collective-permute-start.6 = (f32[16,32,128]{2,1,0:T(8,128)S(1)}, f32[16,32,128]{2,1,0:T(8,128)S(1)}, u32[]{:S(2)}, u32[]{:S(2)}) collective-permute-start(f32[16,32,128]{2,1,0:T(8,128)S(1)} %get-tuple-element.23), channel_id=1, source_target_pairs={{0,1},{1,2},{2,3},{3,4},{4,5},{5,6},{6,7},{7,0},{8,9},{9,10},{10,1... | collective-permute-start | bytes 786440 | tf_op jit(solution)/shard_map/ppermute | solution.py:283
  57.8 9.2 %collective-permute-start.7 = (f32[16,32,128]{2,1,0:T(8,128)S(1)}, f32[16,32,128]{2,1,0:T(8,128)S(1)}, u32[]{:S(2)}, u32[]{:S(2)}) collective-permute-start(f32[16,32,128]{2,1,0:T(8,128)S(1)} %get-tuple-element.24), channel_id=1, source_target_pairs={{1,0},{2,1},{3,2},{4,3},{5,4},{6,5},{7,6},{0,7},{9,8},{10,9},{11,1... | collective-permute-start | bytes 786440 | tf_op jit(solution)/shard_map/ppermute | solution.py:284
  58.8 8.1 %collective-permute-start.4 = (f32[16,16,128]{2,1,0:T(8,128)S(1)}, f32[16,16,128]{2,1,0:T(8,128)S(1)}, u32[]{:S(2)}, u32[]{:S(2)}) collective-permute-start(f32[16,16,128]{2,1,0:T(8,128)S(1)} %get-tuple-element.21), channel_id=1, source_target_pairs={{0,16},{16,32},{32,48},{48,64},{64,80},{80,96},{96,112},{112,128},... | collective-permute-start | bytes 393224 | tf_op jit(solution)/shard_map/ppermute | solution.py:285
  59.7 7.2 %collective-permute-start.5 = (f32[16,16,128]{2,1,0:T(8,128)S(1)}, f32[16,16,128]{2,1,0:T(8,128)S(1)}, u32[]{:S(2)}, u32[]{:S(2)}) collective-permute-start(f32[16,16,128]{2,1,0:T(8,128)S(1)} %get-tuple-element.22), channel_id=1, source_target_pairs={{16,0},{32,16},{48,32},{64,48},{80,64},{96,80},{112,96},{128,112},... | collective-permute-start | bytes 393224 | tf_op jit(solution)/shard_map/ppermute | solution.py:286

commit v2 on v1

--- a/solution.py
+++ b/solution.py
@@ -102,7 +102,7 @@
         level_high[block] = adv[block, pl.ds(LEVELS - 1, RIM, stride=LEVELS), :]
         return carry
 
-    lax.fori_loop(0, BLOCKS, block_step, 0)
+    lax.fori_loop(0, BLOCKS, block_step, 0, unroll=16)
 
 
 def ghost_roll(source, target, amount):
@@ -118,7 +118,7 @@
             target[block, rows, :] = rotated(source[here, rows, :], source[before, rows, :], rest, lanes)
         return carry
 
-    lax.fori_loop(0, BLOCKS, block_step, 0)
+    lax.fori_loop(0, BLOCKS, block_step, 0, unroll=16)
 
 
 def diffuse(step, place, offsets, kappa, adv, col_before, col_after, level_below, level_above, out,
@@ -183,7 +183,7 @@
             out[block, pl.ds(col * COL_ROWS + 8, 8), :] = second
         return carry
 
-    lax.fori_loop(0, BLOCKS, block_step, 0)
+    lax.fori_loop(0, BLOCKS, block_step, 0, unroll=16)
 
 
 def pack(state):

time: 107 us -> 98.2 us (0.918)
  Pallas kernels: 15.4 us -> 6.29 us
    pallas_call x1, Pallas kernels: 6.87 us -> 2.27 us  [diffuse_advect(): pl.pallas_call(kernel, out_shape=ADVECTED, in_specs=[SMEM] * 5 + [VMEM] *...]
    pallas_call x1, Pallas kernels: 4.79 us -> 1.59 us  [last_diffuse(): pl.pallas_call(kernel, out_shape=shape(BLOCKS, ROWS, LANES), in_specs=[SM...]
    pallas_call x1, Pallas kernels: 2.67 us -> 1.31 us  [first_advect(): pl.pallas_call(kernel, out_shape=ADVECTED, in_specs=[SMEM, SMEM, VMEM], o...]
where the time goes in v2:
time: 98.2 us; the launch traced here: 98 us
  blocking collectives  70 us (71%)
  starting transfers between devices  15 us (15%)
  Pallas kernels  6.29 us (6%)
  waiting for transfers between devices  5.36 us (5%)
  local copies, waits for them, and re-layouts  1.24 us (1%)
    all_to_all x1, blocking collectives, on_device(): values = lax.all_to_all(pack(state), 'gy', 0, 0, tiled=True)  35.6 us
    all_to_all x1, blocking collectives, on_device(): return unpack(lax.all_to_all(values, 'gy', 0, 0, tiled=True))  34.4 us
    ppermute x2, starting transfers between devices, exchange(): col_after = lax.ppermute(col_low, 'gx', down)  9.81 us
    ppermute x2, waiting for transfers between devices, exchange(): col_before = lax.ppermute(col_high, 'gx', up)  5.34 us
    ppermute x2, starting transfers between devices, exchange(): level_below = lax.ppermute(level_high, 'gy', ring)  2.31 us
    pallas_call x1, Pallas kernels, diffuse_advect(): pl.pallas_call(kernel, out_shape=ADVECTED, in_specs=[SMEM] * 5 + [VMEM] *...  2.27 us
    ppermute x2, starting transfers between devices, exchange(): level_above = lax.ppermute(level_low, 'gy', back)  1.98 us
  transfers between devices with their start and end apart: 8, of which 2 were waited for; matrix products, arithmetic and copies ran while one was open for 0% of the time, Pallas kernels for 0%

profile of v2, /device:TPU:32, one launch (start us, length us, event | category | flops | bytes accessed | tf_op | source)
XLA Modules:
  0.0 98.0 jit_solution(4892759908070119085)
XLA Ops:
  0.0 1.2 %copy-done = f32[8,8,32,128]{3,2,1,0:T(8,128)S(1)} copy-done((f32[8,8,32,128]{3,2,1,0:T(8,128)S(1)}, f32[8,8,32,128]{3,2,1,0:T(8,128)}, u32[]{:S(2)}) %copy-start) | copy-done | bytes 1048600
  1.2 0.1 pack.1
  1.3 0.0 copy-start.1
  1.3 0.0 copy-start.2
  1.3 35.6 %all_to_all.10.values = f32[16,128,128]{2,1,0:T(8,128)S(1)} all-to-all(f32[16,128,128]{2,1,0:T(8,128)S(1)} %pack.1), channel_id=1, replica_groups=mesh['gx'=16,'gy'=16] {'gy'}, dimensions={0} | all-to-all | bytes 2097152 | tf_op jit(solution)/shard_map/all_to_all | solution.py:301
  36.9 1.3 %advect.1 = (f32[16,128,128]{2,1,0:T(8,128)S(1)}, f32[16,16,128]{2,1,0:T(8,128)S(1)}, f32[16,16,128]{2,1,0:T(8,128)S(1)}, f32[16,32,128]{2,1,0:T(8,128)S(1)}, f32[16,32,128]{2,1,0:T(8,128)S(1)}) custom-call(s32[2,8]{1,0:T(2,128)S(1)} %copy-done.1, f32[2,8]{1,0:T(2,128)S(1)} %copy-done.2, f32[16,128,128]{2,1,0:T(8,128)S(1)} %all_to_all.10.values), custom_call_target="tpu_custom_call" | custom-call | tf_op jit(solution)/shard_map/advect/pallas_call | solution.py:230
  38.3 1.2 %collective-permute-start.2 = (f32[16,32,128]{2,1,0:T(8,128)S(1)}, f32[16,32,128]{2,1,0:T(8,128)S(1)}, u32[]{:S(2)}, u32[]{:S(2)}) collective-permute-start(f32[16,32,128]{2,1,0:T(8,128)S(1)} %get-tuple-element.18), channel_id=1, source_target_pairs={{0,1},{1,2},{2,3},{3,4},{4,5},{5,6},{6,7},{7,0},{8,9},{9,10},{10,1... | collective-permute-start | bytes 786440 | tf_op jit(solution)/shard_map/ppermute | solution.py:283
  39.4 0.9 collective-permute-start.3
  40.4 5.4 %collective-permute-start.1 = (f32[16,16,128]{2,1,0:T(8,128)S(1)}, f32[16,16,128]{2,1,0:T(8,128)S(1)}, u32[]{:S(2)}, u32[]{:S(2)}) collective-permute-start(f32[16,16,128]{2,1,0:T(8,128)S(1)} %get-tuple-element.17), channel_id=1, source_target_pairs={{16,0},{32,16},{48,32},{64,48},{80,64},{96,80},{112,96},{128,112},... | collective-permute-start | bytes 393224 | tf_op jit(solution)/shard_map/ppermute | solution.py:286
  45.7 0.1 pad_add_fusion.place
  45.8 2.6 %collective-permute-done.h0 = f32[16,16,128]{2,1,0:T(8,128)S(1)} collective-permute-done((f32[16,16,128]{2,1,0:T(8,128)S(1)}, f32[16,16,128]{2,1,0:T(8,128)S(1)}, u32[]{:S(2)}, u32[]{:S(2)}) %collective-permute-start) | collective-permute-done | bytes 131104 | tf_op jit(solution)/shard_map/ppermute | solution.py:285
  48.4 0.0 collective-permute-done.2.h2
  48.4 0.0 collective-permute-done.3.h3
  48.4 2.3 %diffuse_advect.1 = (f32[16,128,128]{2,1,0:T(8,128)S(1)}, f32[16,16,128]{2,1,0:T(8,128)S(1)}, f32[16,16,128]{2,1,0:T(8,128)S(1)}, f32[16,32,128]{2,1,0:T(8,128)S(1)}, f32[16,32,128]{2,1,0:T(8,128)S(1)}) custom-call(s32[4]{0:T(128)S(1)} %pad_add_fusion.place, s32[2]{0:T(128)S(1)} %copy-done.3, f32[8]{0:T(128)S(1)} %copy-done.4, s32[2,8]{1,0:T(2,128)S(1)} %copy-done.1, ...), custom_call_target="tpu_custom_call" | custom-call | tf_op jit(solution)/shard_map/diffuse_advect/pallas_call | solution.py:246
  50.7 1.2 %collective-permute-start.6 = (f32[16,32,128]{2,1,0:T(8,128)S(1)}, f32[16,32,128]{2,1,0:T(8,128)S(1)}, u32[]{:S(2)}, u32[]{:S(2)}) collective-permute-start(f32[16,32,128]{2,1,0:T(8,128)S(1)} %get-tuple-element.23), channel_id=1, source_target_pairs={{0,1},{1,2},{2,3},{3,4},{4,5},{5,6},{6,7},{7,0},{8,9},{9,10},{10,1... | collective-permute-start | bytes 786440 | tf_op jit(solution)/shard_map/ppermute | solution.py:283
  51.9 1.0 %collective-permute-start.7 = (f32[16,32,128]{2,1,0:T(8,128)S(1)}, f32[16,32,128]{2,1,0:T(8,128)S(1)}, u32[]{:S(2)}, u32[]{:S(2)}) collective-permute-start(f32[16,32,128]{2,1,0:T(8,128)S(1)} %get-tuple-element.24), channel_id=1, source_target_pairs={{1,0},{2,1},{3,2},{4,3},{5,4},{6,5},{7,6},{0,7},{9,8},{10,9},{11,1... | collective-permute-start | bytes 786440 | tf_op jit(solution)/shard_map/ppermute | solution.py:284
  52.9 0.9 collective-permute-start.4
  53.8 4.5 %collective-permute-start.5 = (f32[16,16,128]{2,1,0:T(8,128)S(1)}, f32[16,16,128]{2,1,0:T(8,128)S(1)}, u32[]{:S(2)}, u32[]{:S(2)}) collective-permute-start(f32[16,16,128]{2,1,0:T(8,128)S(1)} %get-tuple-element.22), channel_id=1, source_target_pairs={{16,0},{32,16},{48,32},{64,48},{80,64},{96,80},{112,96},{128,112},... | collective-permute-start | bytes 393224 | tf_op jit(solution)/shard_map/ppermute | solution.py:286
  58.3 2.7 %collective-permute-done.4.h0 = f32[16,16,128]{2,1,0:T(8,128)S(1)} collective-permute-done((f32[16,16,128]{2,1,0:T(8,128)S(1)}, f32[16,16,128]{2,1,0:T(8,128)S(1)}, u32[]{:S(2)}, u32[]{:S(2)}) %collective-permute-start.4) | collective-permute-done | bytes 131104 | tf_op jit(solution)/shard_map/ppermute | solution.py:285
  61.0 0.0 collective-permute-done.5.h1
  61.0 0.0 collective-permute-done.6.h2
  61.0 1.6 %last_diffuse.1 = f32[16,128,128]{2,1,0:T(8,128)S(1)} custom-call(s32[4]{0:T(128)S(1)} %pad_add_fusion.place, s32[2]{0:T(128)S(1)} %copy-done.3, f32[8]{0:T(128)S(1)} %copy-done.4, f32[16,128,128]{2,1,0:T(8,128)S(1)} %get-tuple-element.20.adv, f32[16,16,128]{2,1,0:T(8,128)S(1)} %collective-permute-done.4.h0, f32[16,16,128]{2,1,0:T(8,128)S(1)} %collective-permute-done.5.h1, ...), custom_call_target="tpu_custom_call" | custom-call | tf_op jit(solution)/shard_map/last_diffuse/pallas_call | solution.py:261
  62.6 34.4 %all_to_all.11.packed = f32[16,128,128]{2,1,0:T(8,128)S(1)} all-to-all(f32[16,128,128]{2,1,0:T(8,128)S(1)} %last_diffuse.1), channel_id=1, replica_groups=mesh['gx'=16,'gy'=16] {'gy'}, dimensions={0} | all-to-all | bytes 2097152 | tf_op jit(solution)/shard_map/all_to_all | solution.py:306
  97.0 1.0 %unpack.1 = f32[8,8,32,128]{3,2,1,0:T(8,128)} custom-call(f32[16,128,128]{2,1,0:T(8,128)S(1)} %all_to_all.11.packed), custom_call_target="tpu_custom_call" | custom-call | tf_op jit(solution)/shard_map/unpack/pallas_call | solution.py:201
  (10 shorter events, 0.0 us)
Async XLA Ops:
  0.0 1.2 %copy-start = (f32[8,8,32,128]{3,2,1,0:T(8,128)S(1)}, f32[8,8,32,128]{3,2,1,0:T(8,128)}, u32[]{:S(2)}) copy-start(f32[8,8,32,128]{3,2,1,0:T(8,128)} %state.1) | copy-start | bytes 3145732
  1.3 35.6 %copy-start.1 = (s32[2,8]{1,0:T(2,128)S(1)}, s32[2,8]{1,0:T(2,128)}, u32[]{:S(2)}) copy-start(s32[2,8]{1,0:T(2,128)} %shifts.3) | copy-start | bytes 196
  1.3 35.6 %copy-start.2 = (f32[2,8]{1,0:T(2,128)S(1)}, f32[2,8]{1,0:T(2,128)}, u32[]{:S(2)}) copy-start(f32[2,8]{1,0:T(2,128)} %fracs.3) | copy-start | bytes 196
  38.3 10.1 %collective-permute-start.2 = (f32[16,32,128]{2,1,0:T(8,128)S(1)}, f32[16,32,128]{2,1,0:T(8,128)S(1)}, u32[]{:S(2)}, u32[]{:S(2)}) collective-permute-start(f32[16,32,128]{2,1,0:T(8,128)S(1)} %get-tuple-element.18), channel_id=1, source_target_pairs={{0,1},{1,2},{2,3},{3,4},{4,5},{5,6},{6,7},{7,0},{8,9},{9,10},{10,1... | collective-permute-start | bytes 786440 | tf_op jit(solution)/shard_map/ppermute | solution.py:283
  39.4 9.0 %collective-permute-start.3 = (f32[16,32,128]{2,1,0:T(8,128)S(1)}, f32[16,32,128]{2,1,0:T(8,128)S(1)}, u32[]{:S(2)}, u32[]{:S(2)}) collective-permute-start(f32[16,32,128]{2,1,0:T(8,128)S(1)} %get-tuple-element.19), channel_id=1, source_target_pairs={{1,0},{2,1},{3,2},{4,3},{5,4},{6,5},{7,6},{0,7},{9,8},{10,9},{11,1... | collective-permute-start | bytes 786440 | tf_op jit(solution)/shard_map/ppermute | solution.py:284
  40.4 8.0 %collective-permute-start = (f32[16,16,128]{2,1,0:T(8,128)S(1)}, f32[16,16,128]{2,1,0:T(8,128)S(1)}, u32[]{:S(2)}, u32[]{:S(2)}) collective-permute-start(f32[16,16,128]{2,1,0:T(8,128)S(1)} %get-tuple-element.16), channel_id=1, source_target_pairs={{0,16},{16,32},{32,48},{48,64},{64,80},{80,96},{96,112},{112,128},... | collective-permute-start | bytes 393224 | tf_op jit(solution)/shard_map/ppermute | solution.py:285
  40.4 8.0 %collective-permute-start.1 = (f32[16,16,128]{2,1,0:T(8,128)S(1)}, f32[16,16,128]{2,1,0:T(8,128)S(1)}, u32[]{:S(2)}, u32[]{:S(2)}) collective-permute-start(f32[16,16,128]{2,1,0:T(8,128)S(1)} %get-tuple-element.17), channel_id=1, source_target_pairs={{16,0},{32,16},{48,32},{64,48},{80,64},{96,80},{112,96},{128,112},... | collective-permute-start | bytes 393224 | tf_op jit(solution)/shard_map/ppermute | solution.py:286
  45.8 2.6 %copy-start.3 = (s32[2]{0:T(128)S(1)}, s32[2]{0:T(128)}, u32[]{:S(2)}) copy-start(s32[2]{0:T(128)} %offsets.3) | copy-start | bytes 28
  45.8 2.6 %copy-start.4 = (f32[8]{0:T(128)S(1)}, f32[8]{0:T(128)}, u32[]{:S(2)}) copy-start(f32[8]{0:T(128)} %kappa.3) | copy-start | bytes 100
  50.7 10.3 %collective-permute-start.6 = (f32[16,32,128]{2,1,0:T(8,128)S(1)}, f32[16,32,128]{2,1,0:T(8,128)S(1)}, u32[]{:S(2)}, u32[]{:S(2)}) collective-permute-start(f32[16,32,128]{2,1,0:T(8,128)S(1)} %get-tuple-element.23), channel_id=1, source_target_pairs={{0,1},{1,2},{2,3},{3,4},{4,5},{5,6},{6,7},{7,0},{8,9},{9,10},{10,1... | collective-permute-start | bytes 786440 | tf_op jit(solution)/shard_map/ppermute | solution.py:283
  51.9 9.2 %collective-permute-start.7 = (f32[16,32,128]{2,1,0:T(8,128)S(1)}, f32[16,32,128]{2,1,0:T(8,128)S(1)}, u32[]{:S(2)}, u32[]{:S(2)}) collective-permute-start(f32[16,32,128]{2,1,0:T(8,128)S(1)} %get-tuple-element.24), channel_id=1, source_target_pairs={{1,0},{2,1},{3,2},{4,3},{5,4},{6,5},{7,6},{0,7},{9,8},{10,9},{11,1... | collective-permute-start | bytes 786440 | tf_op jit(solution)/shard_map/ppermute | solution.py:284
  52.9 8.1 %collective-permute-start.4 = (f32[16,16,128]{2,1,0:T(8,128)S(1)}, f32[16,16,128]{2,1,0:T(8,128)S(1)}, u32[]{:S(2)}, u32[]{:S(2)}) collective-permute-start(f32[16,16,128]{2,1,0:T(8,128)S(1)} %get-tuple-element.21), channel_id=1, source_target_pairs={{0,16},{16,32},{32,48},{48,64},{64,80},{80,96},{96,112},{112,128},... | collective-permute-start | bytes 393224 | tf_op jit(solution)/shard_map/ppermute | solution.py:285
  53.8 7.2 %collective-permute-start.5 = (f32[16,16,128]{2,1,0:T(8,128)S(1)}, f32[16,16,128]{2,1,0:T(8,128)S(1)}, u32[]{:S(2)}, u32[]{:S(2)}) collective-permute-start(f32[16,16,128]{2,1,0:T(8,128)S(1)} %get-tuple-element.22), channel_id=1, source_target_pairs={{16,0},{32,16},{48,32},{64,48},{80,64},{96,80},{112,96},{128,112},... | collective-permute-start | bytes 393224 | tf_op jit(solution)/shard_map/ppermute | solution.py:286

commit v3 on v2

v3 whole, which is shorter than its diff:
```python
import jax
import jax.numpy as jnp
from jax import lax
from jax.experimental import pallas as pl
from jax.experimental.pallas import tpu as pltpu
from jax.sharding import PartitionSpec as P

spin_gain = 0.2
spin_drag = 0.05
tidal_gain = 0.3

LANES = 128
BLOCKS = 16
COLS = 8
HALF_VARS = 4
LEVELS = 4
COL_ROWS = HALF_VARS * LEVELS
ROWS = COLS * COL_ROWS
RIM = ROWS // LEVELS
HALVES = 2
LEVEL_BLOCKS = 8
VARS = HALVES * HALF_VARS

F32 = jnp.float32
VMEM = pl.BlockSpec(memory_space=pltpu.VMEM)
PARAMS = pltpu.CompilerParams(vmem_limit_bytes=24 * 1024 * 1024)


def shape(*dims):
    return jax.ShapeDtypeStruct(dims, F32)


def lane_index():
    return lax.broadcasted_iota(jnp.int32, (8, LANES), 1)


def row_index():
    return lax.broadcasted_iota(jnp.int32, (8, LANES), 0)


def rotated(block, earlier, amount, lanes):
    joined = jnp.where(lanes < LANES - amount, block, earlier)
    return pltpu.roll(joined, amount & (LANES - 1), 1)


def pack_kernel(state, out):
    for half in range(HALVES):
        for col in range(COLS):
            for pair in range(2):
                var = half * HALF_VARS + 2 * pair
                base = col * COL_ROWS + pair * 8
                for tile in range(LEVEL_BLOCKS // 2):
                    first = state[var, col, pl.ds(tile * 8, 8), :]
                    second = state[var + 1, col, pl.ds(tile * 8, 8), :]
                    dest = half * LEVEL_BLOCKS + 2 * tile
                    out[dest, pl.ds(base, 8), :] = jnp.concatenate([first[:4], second[:4]], axis=0)
                    out[dest + 1, pl.ds(base, 8), :] = jnp.concatenate([first[4:], second[4:]], axis=0)


def unpack_kernel(packed, out):
    for half in range(HALVES):
        for col in range(COLS):
            for pair in range(2):
                var = half * HALF_VARS + 2 * pair
                base = col * COL_ROWS + pair * 8
                for tile in range(LEVEL_BLOCKS // 2):
                    source = half * LEVEL_BLOCKS + 2 * tile
                    low = packed[source, pl.ds(base, 8), :]
                    high = packed[source + 1, pl.ds(base, 8), :]
                    out[var, col, pl.ds(tile * 8, 8), :] = jnp.concatenate([low[:4], high[:4]], axis=0)
                    out[var + 1, col, pl.ds(tile * 8, 8), :] = jnp.concatenate([low[4:], high[4:]], axis=0)


def advect(step, place, offset, shifts, fracs, values, adv, col_near, col_far, level_near, level_far):
    lanes = lane_index()
    turns = [shifts[step, col] for col in range(COLS)]
    far = [fracs[step, col] for col in range(COLS)]
    near = [1.0 - weight for weight in far]
    radial, vertical = place[0], place[2]
    even = (radial & 1) == 0
    level_even = (vertical & 1) == 0
    for block in range(BLOCKS):
        for col in range(COLS):
            source = (block - turns[col] // LANES) & (BLOCKS - 1)
            before = (source - 1) & (BLOCKS - 1)
            rest = turns[col] & (LANES - 1)
            for pair in range(2):
                rows = pl.ds(col * COL_ROWS + pair * 8, 8)
                here = values[source, rows, :]
                earlier = values[before, rows, :]
                nearer = rotated(here, earlier, rest, lanes)
                farther = rotated(here, earlier, rest + 1, lanes)
                adv[block, rows, :] = near[col] * nearer + far[col] * farther
        low = adv[block, pl.ds(0, RIM, stride=LEVELS), :]
        high = adv[block, pl.ds(LEVELS - 1, RIM, stride=LEVELS), :]
        level_near[block] = jnp.where(level_even, high, low)
        level_far[block] = jnp.where(level_even, low, high)
        for pair in range(2):
            rows = pl.ds(pair * 8, 8)
            low = adv[block, rows, :]
            high = adv[block, pl.ds((COLS - 1) * COL_ROWS + pair * 8, 8), :]
            col_near[block, rows, :] = jnp.where(even, high, low)
    start = jnp.where(even, 0, (COLS - 1) * COL_ROWS)
    far_ghost(place, offset, -1, adv, start, col_far)


def far_ghost(place, offset, sign, source, start, target):
    radial, radial_size = place[0], place[3]
    lanes = lane_index()
    signed = jnp.where(radial == 0, sign, jnp.where(radial == radial_size - 1, -sign, 0))
    turn = (signed * offset) & (BLOCKS * LANES - 1)
    whole = turn // LANES
    rest = turn & (LANES - 1)
    for block in range(BLOCKS):
        here = (block - whole) & (BLOCKS - 1)
        before = (here - 1) & (BLOCKS - 1)
        for pair in range(2):
            rows = pl.ds(pl.multiple_of(start + pair * 8, 8), 8)
            target[block, pl.ds(pair * 8, 8), :] = rotated(source[here, rows, :], source[before, rows, :], rest, lanes)


def where_am_i():
    around = lax.axis_index("gy")
    return lax.axis_index("gx"), around // LEVEL_BLOCKS, around % LEVEL_BLOCKS, lax.axis_size("gx")


def prepare(place, kappa, coefs):
    radial, half = place[0], place[1]
    first_half = half == 0
    upper_rows = row_index() >= LEVELS
    for pair in range(2):
        lower, upper = [
            jnp.where(first_half, kappa[0, 2 * pair + var], kappa[0, HALF_VARS + 2 * pair + var]) for var in range(2)
        ]
        coefs[pair] = jnp.where(upper_rows, upper, lower)
    coupled = jnp.where(first_half, 1.0, 0.0)
    coefs[2] = jnp.where(upper_rows, spin_gain * coupled, 0.0)
    coefs[3] = jnp.where(upper_rows, 0.0, -spin_drag * coupled)
    total_x = float(place[3] * COLS)
    for col in range(COLS):
        position = ((radial * COLS + col).astype(F32) + 0.5) / total_x - 0.5
        coefs[4 + col] = jnp.where(upper_rows, tidal_gain * position * coupled, 0.0)


def diffuse(place, coefs, adv, col_near, col_far, level_near, level_far, out, under, over):
    radial, vertical = place[0], place[2]
    even = (radial & 1) == 0
    level_even = (vertical & 1) == 0
    lanes = lane_index()
    level = row_index() & (LEVELS - 1)
    bottom = level == 0
    top = level == LEVELS - 1
    rates = [coefs[0], coefs[1]]
    gain = coefs[2]
    drag = coefs[3]
    tides = [coefs[4 + col] for col in range(COLS)]
    has_below = vertical > 0
    has_above = vertical < LEVEL_BLOCKS - 1
    low_rim = pl.ds(0, RIM, stride=LEVELS)
    high_rim = pl.ds(LEVELS - 1, RIM, stride=LEVELS)

    for block in range(BLOCKS):
        after = (block + 1) % BLOCKS
        before = (block - 1) % BLOCKS
        below = jnp.where(level_even, level_far[block], level_near[block])
        above = jnp.where(level_even, level_near[block], level_far[block])
        under[block, low_rim, :] = jnp.where(has_below, below, adv[block, low_rim, :])
        over[block, high_rim, :] = jnp.where(has_above, above, adv[block, high_rim, :])
        for col in range(COLS):
            mixed = []
            for pair in range(2):
                base = col * COL_ROWS + pair * 8
                rows = pl.ds(base, 8)
                ghost = pl.ds(pair * 8, 8)
                value = adv[block, rows, :]
                if col > 0:
                    inner = adv[block, pl.ds(base - COL_ROWS, 8), :]
                else:
                    inner = jnp.where(even, col_far[block, ghost, :], col_near[block, ghost, :])
                if col < COLS - 1:
                    outer = adv[block, pl.ds(base + COL_ROWS, 8), :]
                else:
                    outer = jnp.where(even, col_near[block, ghost, :], col_far[block, ghost, :])
                prior = pltpu.roll(jnp.where(lanes < LANES - 1, value, adv[before, rows, :]), 1, 1)
                following = pltpu.roll(jnp.where(lanes >= 1, value, adv[after, rows, :]), LANES - 1, 1)
                lower = jnp.where(bottom, under[block, rows, :], pltpu.roll(value, 1, 0))
                upper = jnp.where(top, over[block, rows, :], pltpu.roll(value, 7, 0))
                laplace = (inner + outer) + (prior + following) + (lower + upper) - 6.0 * value
                mixed.append(value + rates[pair] * laplace)
            swapped = [pltpu.roll(part, 4, 0) for part in mixed]
            first = mixed[0] + gain * swapped[1] + tides[col] * swapped[0]
            second = mixed[1] + drag * swapped[0]
            out[block, pl.ds(col * COL_ROWS, 8), :] = first
            out[block, pl.ds(col * COL_ROWS + 8, 8), :] = second


def unpack(packed):
    return call(unpack_kernel, "unpack", shape(VARS, COLS, LEVELS * LEVEL_BLOCKS, LANES), packed)


ADVECTED = (
    shape(BLOCKS, ROWS, LANES),
    shape(BLOCKS, COL_ROWS, LANES),
    shape(BLOCKS, COL_ROWS, LANES),
    shape(BLOCKS, RIM, LANES),
    shape(BLOCKS, RIM, LANES),
)
RIMS = [pltpu.VMEM((BLOCKS, ROWS, LANES), F32)] * 2


def call(kernel, name, outs, *args, scratch=()):
    return pl.pallas_call(
        kernel,
        out_shape=outs,
        in_specs=[VMEM] * len(args),
        out_specs=jax.tree.map(lambda _: VMEM, outs),
        scratch_shapes=scratch,
        compiler_params=PARAMS,
        name=name,
    )(*args)


def pack(state):
    return call(pack_kernel, "pack", shape(BLOCKS, ROWS, LANES), state)


def first_advect(shifts, fracs, values):
    def kernel(shifts, fracs, values, *outs):
        advect(0, where_am_i(), 0, shifts[...], fracs[...], values, *outs)

    return call(kernel, "advect", ADVECTED, shifts, fracs, values)


def constants(after, offsets, kappa):
    def kernel(after, offsets, kappa, offsets_out, coefs):
        offsets_out[...] = offsets[...]
        prepare(where_am_i(), kappa[...], coefs)

    return pl.pallas_call(
        kernel,
        out_shape=(jax.ShapeDtypeStruct(offsets.shape, offsets.dtype), shape(4 + COLS, 8, LANES)),
        in_specs=[pl.BlockSpec(memory_space=pl.ANY), VMEM, VMEM],
        out_specs=(VMEM, VMEM),
        compiler_params=PARAMS,
        name="constants",
    )(after, offsets, kappa)


def diffuse_advect(offsets, coefs, shifts, fracs, adv, halos):
    def kernel(offsets, coefs, shifts, fracs, adv, h0, h1, h2, h3, o0, o1, o2, o3, o4, current, ghost, under, over):
        place = where_am_i()
        offsets = offsets[...]
        far_ghost(place, offsets[0, 0], 1, h1, 0, ghost)
        diffuse(place, coefs, adv, h0, ghost, h2, h3, current, under, over)
        advect(1, place, offsets[0, 1], shifts[...], fracs[...], current, o0, o1, o2, o3, o4)

    scratch = [pltpu.VMEM((BLOCKS, ROWS, LANES), F32), pltpu.VMEM((BLOCKS, COL_ROWS, LANES), F32)] + RIMS
    return call(
        kernel, "diffuse_advect", ADVECTED, offsets, coefs, shifts, fracs, adv, *halos, scratch=scratch
    )


def last_diffuse(coefs, adv, halos):
    def kernel(coefs, adv, h0, h1, h2, h3, out, under, over):
        diffuse(where_am_i(), coefs, adv, h0, h1, h2, h3, out, under, over)

    return call(kernel, "last_diffuse", shape(BLOCKS, ROWS, LANES), coefs, adv, *halos, scratch=RIMS)


def swaps(count, first):
    pairs = [(i % count, (i + 1) % count) for i in range(first, count, 2)]
    return pairs + [(target, source) for source, target in pairs]


def exchange(rims):
    col_near, col_far, level_near, level_far = rims
    radial_size = lax.axis_size("gx")
    level_pairs = [
        [
            (half * LEVEL_BLOCKS + source, half * LEVEL_BLOCKS + target)
            for half in range(HALVES)
            for source, target in swaps(LEVEL_BLOCKS, first)
        ]
        for first in range(2)
    ]
    level_near = lax.ppermute(level_near, "gy", level_pairs[0])
    level_far = lax.ppermute(level_far, "gy", level_pairs[1])
    col_near = lax.ppermute(col_near, "gx", swaps(radial_size, 0))
    col_far = lax.ppermute(col_far, "gx", swaps(radial_size, 1))
    return col_near, col_far, level_near, level_far


def on_device(state, shifts, fracs, offsets, kappa):
    values = lax.all_to_all(pack(state), "gy", 0, 0, tiled=True)
    adv, *rims = first_advect(shifts, fracs, values)
    offsets, coefs = constants(adv, offsets[None], kappa[None])
    adv, *rims = diffuse_advect(offsets, coefs, shifts, fracs, adv, exchange(rims))
    values = last_diffuse(coefs, adv, exchange(rims))
    return unpack(lax.all_to_all(values, "gy", 0, 0, tiled=True))


def solution(mesh):
    placed = (P(None, "gx", None, "gy"), P(None, "gx"), P(None, "gx"), P(), P())
    return jax.shard_map(
        on_device, mesh=mesh, in_specs=placed, out_specs=P(None, "gx", None, "gy"), check_vma=False
    )
```

time: 98.2 us -> 94.9 us (0.966); the launches traced: 98 us -> 93.1 us
  blocking collectives: 70 us -> 66.1 us
  Pallas kernels: 6.29 us -> 4.87 us
    all_to_all x1, blocking collectives: 34.4 us -> 30.5 us  [on_device(): return unpack(lax.all_to_all(values, 'gy', 0, 0, tiled=True))]
    pallas_call x5 -> x6, Pallas kernels: 6.29 us -> 4.87 us  [the longest x5 4.76 us: call(): pl.pallas_call(kernel, out_shape=outs, in_specs=[VMEM] * len(args), out_s...]
where the time goes in v3:
time: 94.9 us; the launch traced here: 93.1 us
  blocking collectives  66.1 us (70%)
  starting transfers between devices  14.8 us (16%)
  waiting for transfers between devices  5.37 us (6%)
  Pallas kernels  4.87 us (5%)
  local copies, waits for them, and re-layouts  1.91 us (2%)
    all_to_all x1, blocking collectives, on_device(): values = lax.all_to_all(pack(state), 'gy', 0, 0, tiled=True)  35.6 us
    all_to_all x1, blocking collectives, on_device(): return unpack(lax.all_to_all(values, 'gy', 0, 0, tiled=True))  30.5 us
    ppermute x2, starting transfers between devices, exchange(): col_far = lax.ppermute(col_far, 'gx', swaps(radial_size, 1))  9.86 us
    ppermute x2, waiting for transfers between devices, exchange(): col_far = lax.ppermute(col_far, 'gx', swaps(radial_size, 1))  5.35 us
    pallas_call x5, Pallas kernels, call(): pl.pallas_call(kernel, out_shape=outs, in_specs=[VMEM] * len(args), out_s...  4.76 us
    ppermute x2, starting transfers between devices, exchange(): level_near = lax.ppermute(level_near, 'gy', level_pairs[0])  2.52 us
    ppermute x2, starting transfers between devices, exchange(): level_far = lax.ppermute(level_far, 'gy', level_pairs[1])  2.41 us
    unnamed x10, local copies, waits for them, and re-layouts  1.91 us
  transfers between devices with their start and end apart: 8, of which 2 were waited for; matrix products, arithmetic and copies ran while one was open for 0% of the time, Pallas kernels for 0%

profile of v3, /device:TPU:32, one launch (start us, length us, event | category | flops | bytes accessed | tf_op | source)
XLA Modules:
  0.0 93.1 jit_solution(13955973975439147119)
XLA Ops:
  0.0 1.2 %copy-done = f32[8,8,32,128]{3,2,1,0:T(8,128)S(1)} copy-done((f32[8,8,32,128]{3,2,1,0:T(8,128)S(1)}, f32[8,8,32,128]{3,2,1,0:T(8,128)}, u32[]{:S(2)}) %copy-start) | copy-done | bytes 1048600
  1.2 0.1 pack.1
  1.3 0.0 copy-start.1
  1.3 0.0 copy-start.2
  1.3 35.6 %all_to_all.10.values = f32[16,128,128]{2,1,0:T(8,128)S(1)} all-to-all(f32[16,128,128]{2,1,0:T(8,128)S(1)} %pack.1), channel_id=1, replica_groups=mesh['gx'=16,'gy'=16] {'gy'}, dimensions={0} | all-to-all | bytes 2097152 | tf_op jit(solution)/shard_map/all_to_all | solution.py:294
  36.9 0.8 advect.1
  37.8 0.9 collective-permute-start.2
  38.7 1.4 %collective-permute-start.3 = (f32[16,32,128]{2,1,0:T(8,128)S(1)}, f32[16,32,128]{2,1,0:T(8,128)S(1)}, u32[]{:S(2)}, u32[]{:S(2)}) collective-permute-start(f32[16,32,128]{2,1,0:T(8,128)S(1)} %get-tuple-element.23), channel_id=1, source_target_pairs={{1,2},{3,4},{5,6},{7,0},{2,1},{4,3},{6,5},{0,7},{9,10},{11,12},{13... | collective-permute-start | bytes 786440 | tf_op jit(solution)/shard_map/ppermute | solution.py:287
  40.0 0.0 collective-permute-start
  40.1 5.2 %collective-permute-start.1 = (f32[16,16,128]{2,1,0:T(8,128)S(1)}, f32[16,16,128]{2,1,0:T(8,128)S(1)}, u32[]{:S(2)}, u32[]{:S(2)}) collective-permute-start(f32[16,16,128]{2,1,0:T(8,128)S(1)} %get-tuple-element.21), channel_id=1, source_target_pairs={{16,32},{48,64},{80,96},{112,128},{144,160},{176,192},{208,224},{2... | collective-permute-start | bytes 393224 | tf_op jit(solution)/shard_map/ppermute | solution.py:289
  45.3 0.7 copy-done.3
  45.9 0.0 copy-done.4
  45.9 0.1 constants.1
  46.0 0.0 collective-permute-done.h0
  46.1 2.0 %collective-permute-done.1.h1 = f32[16,16,128]{2,1,0:T(8,128)S(1)} collective-permute-done((f32[16,16,128]{2,1,0:T(8,128)S(1)}, f32[16,16,128]{2,1,0:T(8,128)S(1)}, u32[]{:S(2)}, u32[]{:S(2)}) %collective-permute-start.1) | collective-permute-done | bytes 131104 | tf_op jit(solution)/shard_map/ppermute | solution.py:289
  48.1 0.0 collective-permute-done.2.h2
  48.1 1.9 %diffuse_advect.1 = (f32[16,128,128]{2,1,0:T(8,128)S(1)}, f32[16,16,128]{2,1,0:T(8,128)S(1)}, f32[16,16,128]{2,1,0:T(8,128)S(1)}, f32[16,32,128]{2,1,0:T(8,128)S(1)}, f32[16,32,128]{2,1,0:T(8,128)S(1)}) custom-call(s32[1,2]{1,0:T(1,128)S(1)} %get-tuple-element.19.offsets, f32[12,8,128]{2,1,0:T(8,128)S(1)} %get-tuple-element.18.coefs, s32[2,8]{1,0:T(2,128)S(1)} %copy-done.1, ...), custom_call_target="tpu_custom_call" | custom-call | tf_op jit(solution)/shard_map/diffuse_advect/pallas_call | solution.py:212
  49.9 1.6 %collective-permute-start.6 = (f32[16,32,128]{2,1,0:T(8,128)S(1)}, f32[16,32,128]{2,1,0:T(8,128)S(1)}, u32[]{:S(2)}, u32[]{:S(2)}) collective-permute-start(f32[16,32,128]{2,1,0:T(8,128)S(1)} %get-tuple-element.27), channel_id=1, source_target_pairs={{0,1},{2,3},{4,5},{6,7},{1,0},{3,2},{5,4},{7,6},{8,9},{10,11},{12,... | collective-permute-start | bytes 786440 | tf_op jit(solution)/shard_map/ppermute | solution.py:286
  51.5 1.0 %collective-permute-start.7 = (f32[16,32,128]{2,1,0:T(8,128)S(1)}, f32[16,32,128]{2,1,0:T(8,128)S(1)}, u32[]{:S(2)}, u32[]{:S(2)}) collective-permute-start(f32[16,32,128]{2,1,0:T(8,128)S(1)} %get-tuple-element.28), channel_id=1, source_target_pairs={{1,2},{3,4},{5,6},{7,0},{2,1},{4,3},{6,5},{0,7},{9,10},{11,12},{13... | collective-permute-start | bytes 786440 | tf_op jit(solution)/shard_map/ppermute | solution.py:287
  52.6 4.7 %collective-permute-start.5 = (f32[16,16,128]{2,1,0:T(8,128)S(1)}, f32[16,16,128]{2,1,0:T(8,128)S(1)}, u32[]{:S(2)}, u32[]{:S(2)}) collective-permute-start(f32[16,16,128]{2,1,0:T(8,128)S(1)} %get-tuple-element.26), channel_id=1, source_target_pairs={{16,32},{48,64},{80,96},{112,128},{144,160},{176,192},{208,224},{2... | collective-permute-start | bytes 393224 | tf_op jit(solution)/shard_map/ppermute | solution.py:289
  57.3 3.4 %collective-permute-done.5.h1 = f32[16,16,128]{2,1,0:T(8,128)S(1)} collective-permute-done((f32[16,16,128]{2,1,0:T(8,128)S(1)}, f32[16,16,128]{2,1,0:T(8,128)S(1)}, u32[]{:S(2)}, u32[]{:S(2)}) %collective-permute-start.5) | collective-permute-done | bytes 131104 | tf_op jit(solution)/shard_map/ppermute | solution.py:289
  60.6 0.9 %last_diffuse.1 = f32[16,128,128]{2,1,0:T(8,128)S(1)} custom-call(f32[12,8,128]{2,1,0:T(8,128)S(1)} %get-tuple-element.18.coefs, f32[16,128,128]{2,1,0:T(8,128)S(1)} %get-tuple-element.24.adv, f32[16,16,128]{2,1,0:T(8,128)S(1)} %collective-permute-done.4.h0, f32[16,16,128]{2,1,0:T(8,128)S(1)} %collective-permute-done.5.h1, ...), custom_call_target="tpu_custom_call" | custom-call | tf_op jit(solution)/shard_map/last_diffuse/pallas_call | solution.py:212
  61.6 30.5 %all_to_all.11.packed = f32[16,128,128]{2,1,0:T(8,128)S(1)} all-to-all(f32[16,128,128]{2,1,0:T(8,128)S(1)} %last_diffuse.1), channel_id=1, replica_groups=mesh['gx'=16,'gy'=16] {'gy'}, dimensions={0} | all-to-all | bytes 2097152 | tf_op jit(solution)/shard_map/all_to_all | solution.py:299
  92.0 1.0 %unpack.1 = f32[8,8,32,128]{3,2,1,0:T(8,128)} custom-call(f32[16,128,128]{2,1,0:T(8,128)S(1)} %all_to_all.11.packed), custom_call_target="tpu_custom_call" | custom-call | tf_op jit(solution)/shard_map/unpack/pallas_call | solution.py:212
  (10 shorter events, 0.0 us)
Async XLA Ops:
  0.0 1.2 %copy-start = (f32[8,8,32,128]{3,2,1,0:T(8,128)S(1)}, f32[8,8,32,128]{3,2,1,0:T(8,128)}, u32[]{:S(2)}) copy-start(f32[8,8,32,128]{3,2,1,0:T(8,128)} %state.1) | copy-start | bytes 3145732
  1.3 35.6 %copy-start.1 = (s32[2,8]{1,0:T(2,128)S(1)}, s32[2,8]{1,0:T(2,128)}, u32[]{:S(2)}) copy-start(s32[2,8]{1,0:T(2,128)} %shifts.3) | copy-start | bytes 196
  1.3 35.6 %copy-start.2 = (f32[2,8]{1,0:T(2,128)S(1)}, f32[2,8]{1,0:T(2,128)}, u32[]{:S(2)}) copy-start(f32[2,8]{1,0:T(2,128)} %fracs.3) | copy-start | bytes 196
  37.8 10.3 %collective-permute-start.2 = (f32[16,32,128]{2,1,0:T(8,128)S(1)}, f32[16,32,128]{2,1,0:T(8,128)S(1)}, u32[]{:S(2)}, u32[]{:S(2)}) collective-permute-start(f32[16,32,128]{2,1,0:T(8,128)S(1)} %get-tuple-element.22), channel_id=1, source_target_pairs={{0,1},{2,3},{4,5},{6,7},{1,0},{3,2},{5,4},{7,6},{8,9},{10,11},{12,... | collective-permute-start | bytes 786440 | tf_op jit(solution)/shard_map/ppermute | solution.py:286
  38.7 9.4 %collective-permute-start.3 = (f32[16,32,128]{2,1,0:T(8,128)S(1)}, f32[16,32,128]{2,1,0:T(8,128)S(1)}, u32[]{:S(2)}, u32[]{:S(2)}) collective-permute-start(f32[16,32,128]{2,1,0:T(8,128)S(1)} %get-tuple-element.23), channel_id=1, source_target_pairs={{1,2},{3,4},{5,6},{7,0},{2,1},{4,3},{6,5},{0,7},{9,10},{11,12},{13... | collective-permute-start | bytes 786440 | tf_op jit(solution)/shard_map/ppermute | solution.py:287
  40.0 6.0 %collective-permute-start = (f32[16,16,128]{2,1,0:T(8,128)S(1)}, f32[16,16,128]{2,1,0:T(8,128)S(1)}, u32[]{:S(2)}, u32[]{:S(2)}) collective-permute-start(f32[16,16,128]{2,1,0:T(8,128)S(1)} %get-tuple-element.20), channel_id=1, source_target_pairs={{0,16},{32,48},{64,80},{96,112},{128,144},{160,176},{192,208},{224... | collective-permute-start | bytes 393224 | tf_op jit(solution)/shard_map/ppermute | solution.py:288
  40.1 8.0 %collective-permute-start.1 = (f32[16,16,128]{2,1,0:T(8,128)S(1)}, f32[16,16,128]{2,1,0:T(8,128)S(1)}, u32[]{:S(2)}, u32[]{:S(2)}) collective-permute-start(f32[16,16,128]{2,1,0:T(8,128)S(1)} %get-tuple-element.21), channel_id=1, source_target_pairs={{16,32},{48,64},{80,96},{112,128},{144,160},{176,192},{208,224},{2... | collective-permute-start | bytes 393224 | tf_op jit(solution)/shard_map/ppermute | solution.py:289
  45.3 0.7 copy-start.3
  45.3 0.7 copy-start.4
  49.9 10.7 %collective-permute-start.6 = (f32[16,32,128]{2,1,0:T(8,128)S(1)}, f32[16,32,128]{2,1,0:T(8,128)S(1)}, u32[]{:S(2)}, u32[]{:S(2)}) collective-permute-start(f32[16,32,128]{2,1,0:T(8,128)S(1)} %get-tuple-element.27), channel_id=1, source_target_pairs={{0,1},{2,3},{4,5},{6,7},{1,0},{3,2},{5,4},{7,6},{8,9},{10,11},{12,... | collective-permute-start | bytes 786440 | tf_op jit(solution)/shard_map/ppermute | solution.py:286
  51.5 9.1 %collective-permute-start.7 = (f32[16,32,128]{2,1,0:T(8,128)S(1)}, f32[16,32,128]{2,1,0:T(8,128)S(1)}, u32[]{:S(2)}, u32[]{:S(2)}) collective-permute-start(f32[16,32,128]{2,1,0:T(8,128)S(1)} %get-tuple-element.28), channel_id=1, source_target_pairs={{1,2},{3,4},{5,6},{7,0},{2,1},{4,3},{6,5},{0,7},{9,10},{11,12},{13... | collective-permute-start | bytes 786440 | tf_op jit(solution)/shard_map/ppermute | solution.py:287
  52.6 4.7 %collective-permute-start.4 = (f32[16,16,128]{2,1,0:T(8,128)S(1)}, f32[16,16,128]{2,1,0:T(8,128)S(1)}, u32[]{:S(2)}, u32[]{:S(2)}) collective-permute-start(f32[16,16,128]{2,1,0:T(8,128)S(1)} %get-tuple-element.25), channel_id=1, source_target_pairs={{0,16},{32,48},{64,80},{96,112},{128,144},{160,176},{192,208},{224... | collective-permute-start | bytes 393224 | tf_op jit(solution)/shard_map/ppermute | solution.py:288
  52.6 8.0 %collective-permute-start.5 = (f32[16,16,128]{2,1,0:T(8,128)S(1)}, f32[16,16,128]{2,1,0:T(8,128)S(1)}, u32[]{:S(2)}, u32[]{:S(2)}) collective-permute-start(f32[16,16,128]{2,1,0:T(8,128)S(1)} %get-tuple-element.26), channel_id=1, source_target_pairs={{16,32},{48,64},{80,96},{112,128},{144,160},{176,192},{208,224},{2... | collective-permute-start | bytes 393224 | tf_op jit(solution)/shard_map/ppermute | solution.py:289

commit v4 on v3

--- a/solution.py
+++ b/solution.py
@@ -20,6 +20,8 @@
 HALVES = 2
 LEVEL_BLOCKS = 8
 VARS = HALVES * HALF_VARS
+RIM_COEFS = 4 + COLS
+COEFS = RIM_COEFS + 3 + COLS // 2
 
 F32 = jnp.float32
 VMEM = pl.BlockSpec(memory_space=pltpu.VMEM)
@@ -125,7 +127,8 @@
 
 
 def prepare(place, kappa, coefs):
-    radial, half = place[0], place[1]
+    radial, half, vertical = place[0], place[1], place[2]
+    var = row_index() & (HALF_VARS - 1)
     first_half = half == 0
     upper_rows = row_index() >= LEVELS
     for pair in range(2):
@@ -139,59 +142,90 @@
     total_x = float(place[3] * COLS)
     for col in range(COLS):
         position = ((radial * COLS + col).astype(F32) + 0.5) / total_x - 0.5
-        coefs[4 + col] = jnp.where(upper_rows, tidal_gain * position * coupled, 0.0)
-
-
-def diffuse(place, coefs, adv, col_near, col_far, level_near, level_far, out, under, over):
-    radial, vertical = place[0], place[2]
-    even = (radial & 1) == 0
-    level_even = (vertical & 1) == 0
+        tide = tidal_gain * position * coupled
+        coefs[4 + col] = jnp.where(upper_rows, tide, 0.0)
+        turned = jnp.where(var == 1, tide, jnp.where(var == 2, -spin_drag * coupled, 0.0))
+        if col % 2 == 0:
+            earlier = turned
+        else:
+            coefs[RIM_COEFS + 3 + col // 2] = jnp.where(upper_rows, turned, earlier)
+    rate = jnp.zeros((8, LANES), F32)
+    for index in range(HALF_VARS):
+        own = jnp.where(first_half, kappa[0, index], kappa[0, HALF_VARS + index])
+        rate = jnp.where(var == index, own, rate)
+    coefs[RIM_COEFS] = jnp.where(vertical > 0, rate, 0.0)
+    coefs[RIM_COEFS + 1] = jnp.where(vertical < LEVEL_BLOCKS - 1, rate, 0.0)
+    coefs[RIM_COEFS + 2] = jnp.where(var == 1, spin_gain * coupled, 0.0)
+
+
+def sourced(mixed, coefs, col):
+    gain = coefs[2]
+    drag = coefs[3]
+    swapped = [pltpu.roll(part, 4, 0) for part in mixed]
+    return mixed[0] + gain * swapped[1] + coefs[4 + col] * swapped[0], mixed[1] + drag * swapped[0]
+
+
+def interior(place, coefs, adv, out):
+    vertical = place[2]
     lanes = lane_index()
     level = row_index() & (LEVELS - 1)
     bottom = level == 0
     top = level == LEVELS - 1
+    keep_low = jnp.where(vertical > 0, 0.0, 1.0)
+    keep_high = jnp.where(vertical < LEVEL_BLOCKS - 1, 0.0, 1.0)
     rates = [coefs[0], coefs[1]]
-    gain = coefs[2]
-    drag = coefs[3]
-    tides = [coefs[4 + col] for col in range(COLS)]
-    has_below = vertical > 0
-    has_above = vertical < LEVEL_BLOCKS - 1
-    low_rim = pl.ds(0, RIM, stride=LEVELS)
-    high_rim = pl.ds(LEVELS - 1, RIM, stride=LEVELS)
-
     for block in range(BLOCKS):
         after = (block + 1) % BLOCKS
         before = (block - 1) % BLOCKS
-        below = jnp.where(level_even, level_far[block], level_near[block])
-        above = jnp.where(level_even, level_near[block], level_far[block])
-        under[block, low_rim, :] = jnp.where(has_below, below, adv[block, low_rim, :])
-        over[block, high_rim, :] = jnp.where(has_above, above, adv[block, high_rim, :])
         for col in range(COLS):
             mixed = []
             for pair in range(2):
                 base = col * COL_ROWS + pair * 8
                 rows = pl.ds(base, 8)
-                ghost = pl.ds(pair * 8, 8)
                 value = adv[block, rows, :]
-                if col > 0:
-                    inner = adv[block, pl.ds(base - COL_ROWS, 8), :]
-                else:
-                    inner = jnp.where(even, col_far[block, ghost, :], col_near[block, ghost, :])
-                if col < COLS - 1:
-                    outer = adv[block, pl.ds(base + COL_ROWS, 8), :]
-                else:
-                    outer = jnp.where(even, col_near[block, ghost, :], col_far[block, ghost, :])
+                beside = [
+                    adv[block, pl.ds(base + side * COL_ROWS, 8), :] for side in (-1, 1) if 0 <= col + side < COLS
+                ]
                 prior = pltpu.roll(jnp.where(lanes < LANES - 1, value, adv[before, rows, :]), 1, 1)
                 following = pltpu.roll(jnp.where(lanes >= 1, value, adv[after, rows, :]), LANES - 1, 1)
-                lower = jnp.where(bottom, under[block, rows, :], pltpu.roll(value, 1, 0))
-                upper = jnp.where(top, over[block, rows, :], pltpu.roll(value, 7, 0))
-                laplace = (inner + outer) + (prior + following) + (lower + upper) - 6.0 * value
+                lower = jnp.where(bottom, keep_low * value, pltpu.roll(value, 1, 0))
+                upper = jnp.where(top, keep_high * value, pltpu.roll(value, 7, 0))
+                laplace = sum(beside[1:], beside[0]) + (prior + following) + (lower + upper) - 6.0 * value
                 mixed.append(value + rates[pair] * laplace)
-            swapped = [pltpu.roll(part, 4, 0) for part in mixed]
-            first = mixed[0] + gain * swapped[1] + tides[col] * swapped[0]
-            second = mixed[1] + drag * swapped[0]
+            first, second = sourced(mixed, coefs, col)
             out[block, pl.ds(col * COL_ROWS, 8), :] = first
             out[block, pl.ds(col * COL_ROWS + 8, 8), :] = second
+
+
+def add_rims(place, coefs, inside, col_near, col_far, level_near, level_far, out):
+    even = (place[0] & 1) == 0
+    level_even = (place[2] & 1) == 0
+    rates = [coefs[0], coefs[1]]
+    onward = coefs[RIM_COEFS + 2]
+    for block in range(BLOCKS):
+        for col in range(COLS):
+            parts = [inside[block, pl.ds(col * COL_ROWS + pair * 8, 8), :] for pair in range(2)]
+            if col in (0, COLS - 1):
+                nears = [col_near[block, pl.ds(pair * 8, 8), :] for pair in range(2)]
+                fars = [col_far[block, pl.ds(pair * 8, 8), :] for pair in range(2)]
+                far_here = even if col == 0 else jnp.logical_not(even)
+                ghosts = [rates[pair] * jnp.where(far_here, fars[pair], nears[pair]) for pair in range(2)]
+                parts = [part + extra for part, extra in zip(parts, sourced(ghosts, coefs, col))]
+            for pair in range(2):
+                out[block, pl.ds(col * COL_ROWS + pair * 8, 8), :] = parts[pair]
+        for two in range(COLS // 2):
+            rows = pl.ds(two * 8, 8)
+            near = level_near[block, rows, :]
+            far = level_far[block, rows, :]
+            for edge, rim in ((0, jnp.where(level_even, far, near)), (1, jnp.where(level_even, near, far))):
+                rim = coefs[RIM_COEFS + edge] * rim
+                extra = (
+                    rim
+                    + onward * pltpu.roll(rim, 7, 0)
+                    + coefs[RIM_COEFS + 3 + two] * pltpu.roll(rim, 1, 0)
+                )
+                strided = pl.ds(two * 2 * COL_ROWS + edge * (LEVELS - 1), 8, stride=LEVELS)
+                out[block, strided, :] = out[block, strided, :] + extra
 
 
 def unpack(packed):
@@ -205,9 +239,6 @@
     shape(BLOCKS, RIM, LANES),
     shape(BLOCKS, RIM, LANES),
 )
-RIMS = [pltpu.VMEM((BLOCKS, ROWS, LANES), F32)] * 2
-
-
 def call(kernel, name, outs, *args, scratch=()):
     return pl.pallas_call(
         kernel,
@@ -231,40 +262,47 @@
     return call(kernel, "advect", ADVECTED, shifts, fracs, values)
 
 
-def constants(after, offsets, kappa):
-    def kernel(after, offsets, kappa, offsets_out, coefs):
+def first_interior(offsets, kappa, adv):
+    def kernel(offsets, kappa, adv, offsets_out, coefs, out):
+        place = where_am_i()
         offsets_out[...] = offsets[...]
-        prepare(where_am_i(), kappa[...], coefs)
-
-    return pl.pallas_call(
-        kernel,
-        out_shape=(jax.ShapeDtypeStruct(offsets.shape, offsets.dtype), shape(4 + COLS, 8, LANES)),
-        in_specs=[pl.BlockSpec(memory_space=pl.ANY), VMEM, VMEM],
-        out_specs=(VMEM, VMEM),
-        compiler_params=PARAMS,
-        name="constants",
-    )(after, offsets, kappa)
-
-
-def diffuse_advect(offsets, coefs, shifts, fracs, adv, halos):
-    def kernel(offsets, coefs, shifts, fracs, adv, h0, h1, h2, h3, o0, o1, o2, o3, o4, current, ghost, under, over):
+        prepare(place, kappa[...], coefs)
+        interior(place, coefs, adv, out)
+
+    outs = (
+        jax.ShapeDtypeStruct(offsets.shape, offsets.dtype),
+        shape(COEFS, 8, LANES),
+        shape(BLOCKS, ROWS, LANES),
+    )
+    return call(kernel, "interior", outs, offsets, kappa, adv)
+
+
+def rims_advect(offsets, coefs, shifts, fracs, inside, halos):
+    def kernel(offsets, coefs, shifts, fracs, inside, h0, h1, h2, h3, o0, o1, o2, o3, o4, current, ghost):
         place = where_am_i()
         offsets = offsets[...]
         far_ghost(place, offsets[0, 0], 1, h1, 0, ghost)
-        diffuse(place, coefs, adv, h0, ghost, h2, h3, current, under, over)
+        add_rims(place, coefs, inside, h0, ghost, h2, h3, current)
         advect(1, place, offsets[0, 1], shifts[...], fracs[...], current, o0, o1, o2, o3, o4)
 
-    scratch = [pltpu.VMEM((BLOCKS, ROWS, LANES), F32), pltpu.VMEM((BLOCKS, COL_ROWS, LANES), F32)] + RIMS
+    scratch = [pltpu.VMEM((BLOCKS, ROWS, LANES), F32), pltpu.VMEM((BLOCKS, COL_ROWS, LANES), F32)]
     return call(
-        kernel, "diffuse_advect", ADVECTED, offsets, coefs, shifts, fracs, adv, *halos, scratch=scratch
+        kernel, "rims_advect", ADVECTED, offsets, coefs, shifts, fracs, inside, *halos, scratch=scratch
     )
 
 
-def last_diffuse(coefs, adv, halos):
-    def kernel(coefs, adv, h0, h1, h2, h3, out, under, over):
-        diffuse(where_am_i(), coefs, adv, h0, h1, h2, h3, out, under, over)
-
-    return call(kernel, "last_diffuse", shape(BLOCKS, ROWS, LANES), coefs, adv, *halos, scratch=RIMS)
+def last_interior(coefs, adv):
+    def kernel(coefs, adv, out):
+        interior(where_am_i(), coefs, adv, out)
+
+    return call(kernel, "last_interior", shape(BLOCKS, ROWS, LANES), coefs, adv)
+
+
+def last_rims(coefs, inside, halos):
+    def kernel(coefs, inside, h0, h1, h2, h3, out):
+        add_rims(where_am_i(), coefs, inside, h0, h1, h2, h3, out)
+
+    return call(kernel, "last_rims", shape(BLOCKS, ROWS, LANES), coefs, inside, *halos)
 
 
 def swaps(count, first):
@@ -293,9 +331,12 @@
 def on_device(state, shifts, fracs, offsets, kappa):
     values = lax.all_to_all(pack(state), "gy", 0, 0, tiled=True)
     adv, *rims = first_advect(shifts, fracs, values)
-    offsets, coefs = constants(adv, offsets[None], kappa[None])
-    adv, *rims = diffuse_advect(offsets, coefs, shifts, fracs, adv, exchange(rims))
-    values = last_diffuse(coefs, adv, exchange(rims))
+    halos = exchange(rims)
+    offsets, coefs, inside = first_interior(offsets[None], kappa[None], adv)
+    adv, *rims = rims_advect(offsets, coefs, shifts, fracs, inside, halos)
+    halos = exchange(rims)
+    inside = last_interior(coefs, adv)
+    values = last_rims(coefs, inside, halos)
     return unpack(lax.all_to_all(values, "gy", 0, 0, tiled=True))
 
 

time: 94.9 us -> 93.4 us (0.984)
  waiting for transfers between devices: 5.37 us -> 3.89 us
    ppermute x2, waiting for transfers between devices: 5.35 us -> 3.88 us  [exchange(): col_far = lax.ppermute(col_far, 'gx', swaps(radial_size, 1))]
    pallas_call x5 -> x7, Pallas kernels: 4.76 us -> 4.86 us  [call(): pl.pallas_call(kernel, out_shape=outs, in_specs=[VMEM] * len(args), out_s...]
  transfers between devices with their start and end apart: 8 -> 8, of which waited for: 2 -> 2; matrix products, arithmetic and copies ran while one was open for 0% -> 0% of each run, Pallas kernels for 0% -> 2%
where the time goes in v4:
time: 93.4 us; the launch traced here: 91.6 us
  blocking collectives  66.1 us (71%)
  starting transfers between devices  14.8 us (16%)
  Pallas kernels  4.86 us (5%)
  waiting for transfers between devices  3.89 us (4%)
  local copies, waits for them, and re-layouts  1.91 us (2%)
    all_to_all x1, blocking collectives, on_device(): values = lax.all_to_all(pack(state), 'gy', 0, 0, tiled=True)  35.6 us
    all_to_all x1, blocking collectives, on_device(): return unpack(lax.all_to_all(values, 'gy', 0, 0, tiled=True))  30.5 us
    ppermute x2, starting transfers between devices, exchange(): col_far = lax.ppermute(col_far, 'gx', swaps(radial_size, 1))  9.86 us
    pallas_call x7, Pallas kernels, call(): pl.pallas_call(kernel, out_shape=outs, in_specs=[VMEM] * len(args), out_s...  4.86 us
    ppermute x2, waiting for transfers between devices, exchange(): col_far = lax.ppermute(col_far, 'gx', swaps(radial_size, 1))  3.88 us
    ppermute x2, starting transfers between devices, exchange(): level_near = lax.ppermute(level_near, 'gy', level_pairs[0])  2.52 us
    ppermute x2, starting transfers between devices, exchange(): level_far = lax.ppermute(level_far, 'gy', level_pairs[1])  2.41 us
    unnamed x10, local copies, waits for them, and re-layouts  1.91 us
  transfers between devices with their start and end apart: 8, of which 2 were waited for; matrix products, arithmetic and copies ran while one was open for 0% of the time, Pallas kernels for 2%

profile of v4, /device:TPU:32, one launch (start us, length us, event | category | flops | bytes accessed | tf_op | source)
XLA Modules:
  0.0 91.6 jit_solution(17092698537359197371)
XLA Ops:
  0.0 1.2 %copy-done = f32[8,8,32,128]{3,2,1,0:T(8,128)S(1)} copy-done((f32[8,8,32,128]{3,2,1,0:T(8,128)S(1)}, f32[8,8,32,128]{3,2,1,0:T(8,128)}, u32[]{:S(2)}) %copy-start) | copy-done | bytes 1048600
  1.2 0.1 pack.1
  1.3 0.0 copy-start.1
  1.3 0.0 copy-start.2
  1.3 35.6 %all_to_all.10.values = f32[16,128,128]{2,1,0:T(8,128)S(1)} all-to-all(f32[16,128,128]{2,1,0:T(8,128)S(1)} %pack.1), channel_id=1, replica_groups=mesh['gx'=16,'gy'=16] {'gy'}, dimensions={0} | all-to-all | bytes 2097152 | tf_op jit(solution)/shard_map/all_to_all | solution.py:332
  36.9 0.8 advect.1
  37.8 0.9 collective-permute-start.2
  38.7 1.4 %collective-permute-start.3 = (f32[16,32,128]{2,1,0:T(8,128)S(1)}, f32[16,32,128]{2,1,0:T(8,128)S(1)}, u32[]{:S(2)}, u32[]{:S(2)}) collective-permute-start(f32[16,32,128]{2,1,0:T(8,128)S(1)} %get-tuple-element.25), channel_id=1, source_target_pairs={{1,2},{3,4},{5,6},{7,0},{2,1},{4,3},{6,5},{0,7},{9,10},{11,12},{13... | collective-permute-start | bytes 786440 | tf_op jit(solution)/shard_map/ppermute | solution.py:325
  40.0 5.2 %collective-permute-start.1 = (f32[16,16,128]{2,1,0:T(8,128)S(1)}, f32[16,16,128]{2,1,0:T(8,128)S(1)}, u32[]{:S(2)}, u32[]{:S(2)}) collective-permute-start(f32[16,16,128]{2,1,0:T(8,128)S(1)} %get-tuple-element.23), channel_id=1, source_target_pairs={{16,32},{48,64},{80,96},{112,128},{144,160},{176,192},{208,224},{2... | collective-permute-start | bytes 393224 | tf_op jit(solution)/shard_map/ppermute | solution.py:327
  45.3 0.7 copy-done.3
  45.9 0.0 copy-done.4
  45.9 0.8 interior.1
  46.7 1.3 %collective-permute-done.1.h1 = f32[16,16,128]{2,1,0:T(8,128)S(1)} collective-permute-done((f32[16,16,128]{2,1,0:T(8,128)S(1)}, f32[16,16,128]{2,1,0:T(8,128)S(1)}, u32[]{:S(2)}, u32[]{:S(2)}) %collective-permute-start.1) | collective-permute-done | bytes 131104 | tf_op jit(solution)/shard_map/ppermute | solution.py:327
  48.1 0.0 collective-permute-done.2.h2
  48.1 1.1 %rims_advect.1 = (f32[16,128,128]{2,1,0:T(8,128)S(1)}, f32[16,16,128]{2,1,0:T(8,128)S(1)}, f32[16,16,128]{2,1,0:T(8,128)S(1)}, f32[16,32,128]{2,1,0:T(8,128)S(1)}, f32[16,32,128]{2,1,0:T(8,128)S(1)}) custom-call(s32[1,2]{1,0:T(1,128)S(1)} %get-tuple-element.20.offsets, f32[19,8,128]{2,1,0:T(8,128)S(1)} %get-tuple-element.19.coefs, s32[2,8]{1,0:T(2,128)S(1)} %copy-done.1, ...), custom_call_target="tpu_custom_call" | custom-call | tf_op jit(solution)/shard_map/rims_advect/pallas_call | solution.py:243
  49.1 1.6 %collective-permute-start.6 = (f32[16,32,128]{2,1,0:T(8,128)S(1)}, f32[16,32,128]{2,1,0:T(8,128)S(1)}, u32[]{:S(2)}, u32[]{:S(2)}) collective-permute-start(f32[16,32,128]{2,1,0:T(8,128)S(1)} %get-tuple-element.29), channel_id=1, source_target_pairs={{0,1},{2,3},{4,5},{6,7},{1,0},{3,2},{5,4},{7,6},{8,9},{10,11},{12,... | collective-permute-start | bytes 786440 | tf_op jit(solution)/shard_map/ppermute | solution.py:324
  50.7 1.0 %collective-permute-start.7 = (f32[16,32,128]{2,1,0:T(8,128)S(1)}, f32[16,32,128]{2,1,0:T(8,128)S(1)}, u32[]{:S(2)}, u32[]{:S(2)}) collective-permute-start(f32[16,32,128]{2,1,0:T(8,128)S(1)} %get-tuple-element.30), channel_id=1, source_target_pairs={{1,2},{3,4},{5,6},{7,0},{2,1},{4,3},{6,5},{0,7},{9,10},{11,12},{13... | collective-permute-start | bytes 786440 | tf_op jit(solution)/shard_map/ppermute | solution.py:325
  51.8 0.0 collective-permute-start.4
  51.8 4.6 %collective-permute-start.5 = (f32[16,16,128]{2,1,0:T(8,128)S(1)}, f32[16,16,128]{2,1,0:T(8,128)S(1)}, u32[]{:S(2)}, u32[]{:S(2)}) collective-permute-start(f32[16,16,128]{2,1,0:T(8,128)S(1)} %get-tuple-element.28), channel_id=1, source_target_pairs={{16,32},{48,64},{80,96},{112,128},{144,160},{176,192},{208,224},{2... | collective-permute-start | bytes 393224 | tf_op jit(solution)/shard_map/ppermute | solution.py:327
  56.4 0.8 last_interior.1.inside
  57.2 2.5 %collective-permute-done.5.h1 = f32[16,16,128]{2,1,0:T(8,128)S(1)} collective-permute-done((f32[16,16,128]{2,1,0:T(8,128)S(1)}, f32[16,16,128]{2,1,0:T(8,128)S(1)}, u32[]{:S(2)}, u32[]{:S(2)}) %collective-permute-start.5) | collective-permute-done | bytes 131104 | tf_op jit(solution)/shard_map/ppermute | solution.py:327
  59.8 0.3 last_rims.1
  60.1 30.5 %all_to_all.11.packed = f32[16,128,128]{2,1,0:T(8,128)S(1)} all-to-all(f32[16,128,128]{2,1,0:T(8,128)S(1)} %last_rims.1), channel_id=1, replica_groups=mesh['gx'=16,'gy'=16] {'gy'}, dimensions={0} | all-to-all | bytes 2097152 | tf_op jit(solution)/shard_map/all_to_all | solution.py:340
  90.5 1.0 %unpack.1 = f32[8,8,32,128]{3,2,1,0:T(8,128)} custom-call(f32[16,128,128]{2,1,0:T(8,128)S(1)} %all_to_all.11.packed), custom_call_target="tpu_custom_call" | custom-call | tf_op jit(solution)/shard_map/unpack/pallas_call | solution.py:243
  (11 shorter events, 0.0 us)
Async XLA Ops:
  0.0 1.2 %copy-start = (f32[8,8,32,128]{3,2,1,0:T(8,128)S(1)}, f32[8,8,32,128]{3,2,1,0:T(8,128)}, u32[]{:S(2)}) copy-start(f32[8,8,32,128]{3,2,1,0:T(8,128)} %state.1) | copy-start | bytes 3145732
  1.3 35.6 %copy-start.1 = (s32[2,8]{1,0:T(2,128)S(1)}, s32[2,8]{1,0:T(2,128)}, u32[]{:S(2)}) copy-start(s32[2,8]{1,0:T(2,128)} %shifts.3) | copy-start | bytes 196
  1.3 35.6 %copy-start.2 = (f32[2,8]{1,0:T(2,128)S(1)}, f32[2,8]{1,0:T(2,128)}, u32[]{:S(2)}) copy-start(f32[2,8]{1,0:T(2,128)} %fracs.3) | copy-start | bytes 196
  37.8 10.3 %collective-permute-start.2 = (f32[16,32,128]{2,1,0:T(8,128)S(1)}, f32[16,32,128]{2,1,0:T(8,128)S(1)}, u32[]{:S(2)}, u32[]{:S(2)}) collective-permute-start(f32[16,32,128]{2,1,0:T(8,128)S(1)} %get-tuple-element.24), channel_id=1, source_target_pairs={{0,1},{2,3},{4,5},{6,7},{1,0},{3,2},{5,4},{7,6},{8,9},{10,11},{12,... | collective-permute-start | bytes 786440 | tf_op jit(solution)/shard_map/ppermute | solution.py:324
  38.7 9.4 %collective-permute-start.3 = (f32[16,32,128]{2,1,0:T(8,128)S(1)}, f32[16,32,128]{2,1,0:T(8,128)S(1)}, u32[]{:S(2)}, u32[]{:S(2)}) collective-permute-start(f32[16,32,128]{2,1,0:T(8,128)S(1)} %get-tuple-element.25), channel_id=1, source_target_pairs={{1,2},{3,4},{5,6},{7,0},{2,1},{4,3},{6,5},{0,7},{9,10},{11,12},{13... | collective-permute-start | bytes 786440 | tf_op jit(solution)/shard_map/ppermute | solution.py:325
  40.0 6.7 %collective-permute-start = (f32[16,16,128]{2,1,0:T(8,128)S(1)}, f32[16,16,128]{2,1,0:T(8,128)S(1)}, u32[]{:S(2)}, u32[]{:S(2)}) collective-permute-start(f32[16,16,128]{2,1,0:T(8,128)S(1)} %get-tuple-element.22), channel_id=1, source_target_pairs={{0,16},{32,48},{64,80},{96,112},{128,144},{160,176},{192,208},{224... | collective-permute-start | bytes 393224 | tf_op jit(solution)/shard_map/ppermute | solution.py:326
  40.0 8.0 %collective-permute-start.1 = (f32[16,16,128]{2,1,0:T(8,128)S(1)}, f32[16,16,128]{2,1,0:T(8,128)S(1)}, u32[]{:S(2)}, u32[]{:S(2)}) collective-permute-start(f32[16,16,128]{2,1,0:T(8,128)S(1)} %get-tuple-element.23), channel_id=1, source_target_pairs={{16,32},{48,64},{80,96},{112,128},{144,160},{176,192},{208,224},{2... | collective-permute-start | bytes 393224 | tf_op jit(solution)/shard_map/ppermute | solution.py:327
  45.3 0.7 copy-start.3
  45.3 0.7 copy-start.4
  49.1 10.7 %collective-permute-start.6 = (f32[16,32,128]{2,1,0:T(8,128)S(1)}, f32[16,32,128]{2,1,0:T(8,128)S(1)}, u32[]{:S(2)}, u32[]{:S(2)}) collective-permute-start(f32[16,32,128]{2,1,0:T(8,128)S(1)} %get-tuple-element.29), channel_id=1, source_target_pairs={{0,1},{2,3},{4,5},{6,7},{1,0},{3,2},{5,4},{7,6},{8,9},{10,11},{12,... | collective-permute-start | bytes 786440 | tf_op jit(solution)/shard_map/ppermute | solution.py:324
  50.7 9.1 %collective-permute-start.7 = (f32[16,32,128]{2,1,0:T(8,128)S(1)}, f32[16,32,128]{2,1,0:T(8,128)S(1)}, u32[]{:S(2)}, u32[]{:S(2)}) collective-permute-start(f32[16,32,128]{2,1,0:T(8,128)S(1)} %get-tuple-element.30), channel_id=1, source_target_pairs={{1,2},{3,4},{5,6},{7,0},{2,1},{4,3},{6,5},{0,7},{9,10},{11,12},{13... | collective-permute-start | bytes 786440 | tf_op jit(solution)/shard_map/ppermute | solution.py:325
  51.8 5.5 %collective-permute-start.4 = (f32[16,16,128]{2,1,0:T(8,128)S(1)}, f32[16,16,128]{2,1,0:T(8,128)S(1)}, u32[]{:S(2)}, u32[]{:S(2)}) collective-permute-start(f32[16,16,128]{2,1,0:T(8,128)S(1)} %get-tuple-element.27), channel_id=1, source_target_pairs={{0,16},{32,48},{64,80},{96,112},{128,144},{160,176},{192,208},{224... | collective-permute-start | bytes 393224 | tf_op jit(solution)/shard_map/ppermute | solution.py:326
  51.8 8.0 %collective-permute-start.5 = (f32[16,16,128]{2,1,0:T(8,128)S(1)}, f32[16,16,128]{2,1,0:T(8,128)S(1)}, u32[]{:S(2)}, u32[]{:S(2)}) collective-permute-start(f32[16,16,128]{2,1,0:T(8,128)S(1)} %get-tuple-element.28), channel_id=1, source_target_pairs={{16,32},{48,64},{80,96},{112,128},{144,160},{176,192},{208,224},{2... | collective-permute-start | bytes 393224 | tf_op jit(solution)/shard_map/ppermute | solution.py:327

commit v5 on v3

v5 whole, which is shorter than its diff:
```python
import math
import jax
import jax.numpy as jnp
from jax import lax
from jax.experimental import pallas as pl
from jax.experimental.pallas import tpu as pltpu
from jax.sharding import PartitionSpec as P

spin_gain = 0.2
spin_drag = 0.05
tidal_gain = 0.3

LANES = 128
BLOCKS = 16
COLS = 8
HALF_VARS = 4
MODES = 4
COL_ROWS = HALF_VARS * MODES
ROWS = COLS * COL_ROWS
HALVES = 2
MODE_BLOCKS = 8
NZ = MODES * MODE_BLOCKS
VARS = HALVES * HALF_VARS
LAST = COLS - 1
EDGES = (0, LAST)
EDGE_ROWS = len(EDGES) * COL_ROWS
INNER_ROWS = ROWS - EDGE_ROWS
CENTERS = 4 + COLS
COEFS = CENTERS + 2

F32 = jnp.float32
VMEM = pl.BlockSpec(memory_space=pltpu.VMEM)
PARAMS = pltpu.CompilerParams(vmem_limit_bytes=28 * 1024 * 1024)


def shape(*dims):
    return jax.ShapeDtypeStruct(dims, F32)


def lane_index():
    return lax.broadcasted_iota(jnp.int32, (8, LANES), 1)


def row_index():
    return lax.broadcasted_iota(jnp.int32, (8, LANES), 0)


def rotated(block, earlier, amount, lanes):
    joined = jnp.where(lanes < LANES - amount, block, earlier)
    return pltpu.roll(joined, amount & (LANES - 1), 1)


def cosine(angle, mode):
    size = jnp.where(mode == 0, (1.0 / NZ) ** 0.5, (2.0 / NZ) ** 0.5)
    return size * jnp.cos((angle & (4 * NZ - 1)).astype(F32) * (math.pi / (2 * NZ)))


def to_modes(transposed):
    dims = (HALF_VARS * NZ, HALF_VARS * NZ)
    row = lax.broadcasted_iota(jnp.int32, dims, 1 if transposed else 0)
    column = lax.broadcasted_iota(jnp.int32, dims, 0 if transposed else 1)
    mode = (row // COL_ROWS) * MODES + row % MODES
    level = column % NZ
    same = (row // MODES) % HALF_VARS == column // NZ
    return jnp.where(same, cosine((2 * level + 1) * mode, mode), 0.0)


def exact_dot(left, right):
    return lax.dot(left, right, precision=lax.Precision.HIGHEST, preferred_element_type=F32)


def pack_kernel(state, out):
    basis = to_modes(False)
    for half in range(HALVES):
        for col in range(COLS):
            levels = jnp.concatenate([state[half * HALF_VARS + var, col] for var in range(HALF_VARS)], axis=0)
            modes = exact_dot(basis, levels)
            for block in range(MODE_BLOCKS):
                out[half * MODE_BLOCKS + block, col * COL_ROWS : (col + 1) * COL_ROWS, :] = modes[
                    block * COL_ROWS : (block + 1) * COL_ROWS
                ]


def unpack_kernel(back, packed, out):
    basis = back[...]
    for half in range(HALVES):
        for col in range(COLS):
            modes = jnp.concatenate(
                [
                    packed[half * MODE_BLOCKS + block, col * COL_ROWS : (col + 1) * COL_ROWS, :]
                    for block in range(MODE_BLOCKS)
                ],
                axis=0,
            )
            levels = exact_dot(basis, modes)
            for var in range(HALF_VARS):
                out[half * HALF_VARS + var, col] = levels[var * NZ : (var + 1) * NZ]


def mover(step, shifts, fracs):
    lanes = lane_index()
    turns = [shifts[step, col] for col in range(COLS)]
    far = [fracs[step, col] for col in range(COLS)]
    near = [1.0 - weight for weight in far]

    def move(values, block, start, col):
        source = (block - turns[col] // LANES) & (BLOCKS - 1)
        before = (source - 1) & (BLOCKS - 1)
        rest = turns[col] & (LANES - 1)
        rows = pl.ds(start, 8)
        here = values[source, rows, :]
        earlier = values[before, rows, :]
        nearer = rotated(here, earlier, rest, lanes)
        farther = rotated(here, earlier, rest + 1, lanes)
        return near[col] * nearer + far[col] * farther

    return move


def is_even(place):
    return (place[0] & 1) == 0


def far_ghost(place, offset, sign, source, start, target):
    radial, radial_size = place[0], place[3]
    lanes = lane_index()
    signed = jnp.where(radial == 0, sign, jnp.where(radial == radial_size - 1, -sign, 0))
    turn = (signed * offset) & (BLOCKS * LANES - 1)
    whole = turn // LANES
    rest = turn & (LANES - 1)
    for block in range(BLOCKS):
        here = (block - whole) & (BLOCKS - 1)
        before = (here - 1) & (BLOCKS - 1)
        for pair in range(2):
            rows = pl.ds(pl.multiple_of(start + pair * 8, 8), 8)
            target[block, pl.ds(pair * 8, 8), :] = rotated(source[here, rows, :], source[before, rows, :], rest, lanes)


def where_am_i():
    around = lax.axis_index("gy")
    return lax.axis_index("gx"), around // MODE_BLOCKS, around % MODE_BLOCKS, lax.axis_size("gx")


def prepare(place, kappa, coefs):
    radial, half, vertical = place[0], place[1], place[2]
    first_half = half == 0
    row = row_index()
    upper_rows = row >= MODES
    mode = vertical * MODES + (row & (MODES - 1))
    own = 2.0 * jnp.cos(mode.astype(F32) * (math.pi / NZ)) - 6.0
    for pair in range(2):
        lower, upper = [
            jnp.where(first_half, kappa[0, 2 * pair + var], kappa[0, HALF_VARS + 2 * pair + var]) for var in range(2)
        ]
        rate = jnp.where(upper_rows, upper, lower)
        coefs[pair] = rate
        coefs[CENTERS + pair] = 1.0 + rate * own
    coupled = jnp.where(first_half, 1.0, 0.0)
    coefs[2] = jnp.where(upper_rows, spin_gain * coupled, 0.0)
    coefs[3] = jnp.where(upper_rows, 0.0, -spin_drag * coupled)
    total_x = float(place[3] * COLS)
    for col in range(COLS):
        position = ((radial * COLS + col).astype(F32) + 0.5) / total_x - 0.5
        coefs[4 + col] = jnp.where(upper_rows, tidal_gain * position * coupled, 0.0)


def sourced(mixed, coefs, col):
    gain = coefs[2]
    drag = coefs[3]
    swapped = [pltpu.roll(part, 4, 0) for part in mixed]
    return mixed[0] + gain * swapped[1] + coefs[4 + col] * swapped[0], mixed[1] + drag * swapped[0]


def interior(coefs, adv, out):
    lanes = lane_index()
    for block in range(BLOCKS):
        after = (block + 1) % BLOCKS
        before = (block - 1) % BLOCKS
        for col in range(COLS):
            mixed = []
            for pair in range(2):
                base = col * COL_ROWS + pair * 8
                rows = pl.ds(base, 8)
                value = adv[block, rows, :]
                beside = [
                    adv[block, pl.ds(base + side * COL_ROWS, 8), :] for side in (-1, 1) if 0 <= col + side < COLS
                ]
                prior = pltpu.roll(jnp.where(lanes < LANES - 1, value, adv[before, rows, :]), 1, 1)
                following = pltpu.roll(jnp.where(lanes >= 1, value, adv[after, rows, :]), LANES - 1, 1)
                around = sum(beside[1:], beside[0]) + (prior + following)
                mixed.append(coefs[CENTERS + pair] * value + coefs[pair] * around)
            first, second = sourced(mixed, coefs, col)
            out[block, pl.ds(col * COL_ROWS, 8), :] = first
            out[block, pl.ds(col * COL_ROWS + 8, 8), :] = second


def with_ghosts(place, coefs, parts, near, far, block, col):
    even = is_even(place)
    far_here = even if col == 0 else jnp.logical_not(even)
    ghosts = [
        coefs[pair] * jnp.where(far_here, far[block, pl.ds(pair * 8, 8), :], near[block, pl.ds(pair * 8, 8), :])
        for pair in range(2)
    ]
    return [part + extra for part, extra in zip(parts, sourced(ghosts, coefs, col))]


def advect_edges_kernel(shifts, fracs, values, edges, near, far):
    even = is_even(where_am_i())
    move = mover(0, shifts[...], fracs[...])
    for block in range(BLOCKS):
        for pair in range(2):
            low, high = [move(values, block, col * COL_ROWS + pair * 8, col) for col in EDGES]
            rows = pl.ds(pair * 8, 8)
            edges[block, rows, :] = low
            edges[block, pl.ds(COL_ROWS + pair * 8, 8), :] = high
            near[block, rows, :] = jnp.where(even, high, low)
            far[block, rows, :] = jnp.where(even, low, high)


def inner_kernel(offsets, kappa, shifts, fracs, values, edges, offsets_out, coefs, back, inner, partial, adv, current):
    offsets_out[...] = offsets[...]
    back[...] = to_modes(True)
    prepare(where_am_i(), kappa[...], coefs)
    shifts = shifts[...]
    fracs = fracs[...]
    move = mover(0, shifts, fracs)
    for block in range(BLOCKS):
        adv[block, pl.ds(0, COL_ROWS), :] = edges[block, pl.ds(0, COL_ROWS), :]
        adv[block, pl.ds(LAST * COL_ROWS, COL_ROWS), :] = edges[block, pl.ds(COL_ROWS, COL_ROWS), :]
        for col in range(1, LAST):
            for pair in range(2):
                start = col * COL_ROWS + pair * 8
                adv[block, pl.ds(start, 8), :] = move(values, block, start, col)
    interior(coefs, adv, current)
    move = mover(1, shifts, fracs)
    for block in range(BLOCKS):
        partial[block, pl.ds(0, COL_ROWS), :] = current[block, pl.ds(0, COL_ROWS), :]
        partial[block, pl.ds(COL_ROWS, COL_ROWS), :] = current[block, pl.ds(LAST * COL_ROWS, COL_ROWS), :]
        for col in range(1, LAST):
            for pair in range(2):
                start = col * COL_ROWS + pair * 8
                inner[block, pl.ds(start - COL_ROWS, 8), :] = move(current, block, start, col)


def edges_kernel(offsets, coefs, shifts, fracs, partial, col_near, col_far, edges, near, far, ghost, whole):
    place = where_am_i()
    even = is_even(place)
    offsets = offsets[...]
    far_ghost(place, offsets[0, 0], 1, col_far, 0, ghost)
    for block in range(BLOCKS):
        for side, col in enumerate(EDGES):
            rows = [pl.ds(side * COL_ROWS + pair * 8, 8) for pair in range(2)]
            parts = [partial[block, row, :] for row in rows]
            for row, part in zip(rows, with_ghosts(place, coefs, parts, col_near, ghost, block, col)):
                whole[block, row, :] = part
    move = mover(1, shifts[...], fracs[...])
    for block in range(BLOCKS):
        for pair in range(2):
            low, high = [move(whole, block, side * COL_ROWS + pair * 8, col) for side, col in enumerate(EDGES)]
            edges[block, pl.ds(pair * 8, 8), :] = low
            edges[block, pl.ds(COL_ROWS + pair * 8, 8), :] = high
            near[block, pl.ds(pair * 8, 8), :] = jnp.where(even, high, low)
    far_ghost(place, offsets[0, 1], -1, edges, jnp.where(even, 0, COL_ROWS), far)


def last_interior_kernel(coefs, inner, edges, out, adv):
    for block in range(BLOCKS):
        adv[block, pl.ds(0, COL_ROWS), :] = edges[block, pl.ds(0, COL_ROWS), :]
        adv[block, pl.ds(LAST * COL_ROWS, COL_ROWS), :] = edges[block, pl.ds(COL_ROWS, COL_ROWS), :]
        adv[block, pl.ds(COL_ROWS, INNER_ROWS), :] = inner[block]
    interior(coefs, adv, out)


def last_edges_kernel(coefs, inside, col_near, col_far, out):
    place = where_am_i()
    for block in range(BLOCKS):
        out[block, pl.ds(COL_ROWS, INNER_ROWS), :] = inside[block, pl.ds(COL_ROWS, INNER_ROWS), :]
        for col in EDGES:
            rows = [pl.ds(col * COL_ROWS + pair * 8, 8) for pair in range(2)]
            parts = [inside[block, row, :] for row in rows]
            for row, part in zip(rows, with_ghosts(place, coefs, parts, col_near, col_far, block, col)):
                out[block, row, :] = part


def call(kernel, name, outs, *args, scratch=()):
    return pl.pallas_call(
        kernel,
        out_shape=outs,
        in_specs=[VMEM] * len(args),
        out_specs=jax.tree.map(lambda _: VMEM, outs),
        scratch_shapes=scratch,
        compiler_params=PARAMS,
        name=name,
    )(*args)


def swaps(count, first):
    pairs = [(i % count, (i + 1) % count) for i in range(first, count, 2)]
    return pairs + [(target, source) for source, target in pairs]


def exchange(near, far):
    radial_size = lax.axis_size("gx")
    return lax.ppermute(near, "gx", swaps(radial_size, 0)), lax.ppermute(far, "gx", swaps(radial_size, 1))


def across(values):
    return lax.all_to_all(values, "gy", 0, 0, tiled=True)


def on_device(state, shifts, fracs, offsets, kappa):
    whole = shape(BLOCKS, ROWS, LANES)
    column = shape(BLOCKS, COL_ROWS, LANES)
    edge = shape(BLOCKS, EDGE_ROWS, LANES)
    offsets = offsets[None]
    kappa = kappa[None]
    values = across(call(pack_kernel, "pack", whole, state))
    edges, near, far = call(advect_edges_kernel, "advect_edges", (edge, column, column), shifts, fracs, values)
    halos = exchange(near, far)
    offsets, coefs, back, inner, partial = call(
        inner_kernel,
        "inner",
        (
            jax.ShapeDtypeStruct(offsets.shape, offsets.dtype),
            shape(COEFS, 8, LANES),
            shape(HALF_VARS * NZ, HALF_VARS * NZ),
            shape(BLOCKS, INNER_ROWS, LANES),
            edge,
        ),
        offsets,
        kappa,
        shifts,
        fracs,
        values,
        edges,
        scratch=[pltpu.VMEM((BLOCKS, ROWS, LANES), F32)] * 2,
    )
    edges, near, far = call(
        edges_kernel,
        "edges",
        (edge, column, column),
        offsets,
        coefs,
        shifts,
        fracs,
        partial,
        *halos,
        scratch=[pltpu.VMEM((BLOCKS, COL_ROWS, LANES), F32), pltpu.VMEM((BLOCKS, EDGE_ROWS, LANES), F32)],
    )
    halos = exchange(near, far)
    inside = call(
        last_interior_kernel,
        "last_interior",
        whole,
        coefs,
        inner,
        edges,
        scratch=[pltpu.VMEM((BLOCKS, ROWS, LANES), F32)],
    )
    values = across(call(last_edges_kernel, "last_edges", whole, coefs, inside, *halos))
    return call(unpack_kernel, "unpack", shape(VARS, COLS, NZ, LANES), back, values)


def solution(mesh):
    placed = (P(None, "gx", None, "gy"), P(None, "gx"), P(None, "gx"), P(), P())
    return jax.shard_map(
        on_device, mesh=mesh, in_specs=placed, out_specs=P(None, "gx", None, "gy"), check_vma=False
    )
```

time: 94.9 us -> 88.7 us (0.935)
  starting transfers between devices: 14.8 us -> 10.6 us
  waiting for transfers between devices: 5.37 us -> 2.28 us
  Pallas kernels: 4.87 us -> 6.94 us
    ppermute x8 -> x4, starting transfers between devices: 14.8 us -> 10.6 us  [the longest x2 10.4 us: exchange(): lax.ppermute(far, 'gx', swaps(radial_size, 1))]
    ppermute x8 -> x4, waiting for transfers between devices: 5.37 us -> 2.28 us  [the longest x2 2.27 us: exchange(): lax.ppermute(far, 'gx', swaps(radial_size, 1))]
    pallas_call x5 -> x7, Pallas kernels: 4.76 us -> 6.94 us  [call(): pl.pallas_call(kernel, out_shape=outs, in_specs=[VMEM] * len(args), out_s...]
  transfers between devices with their start and end apart: 8 -> 4, of which waited for: 2 -> 1; matrix products, arithmetic and copies ran while one was open for 0% -> 0% of each run, Pallas kernels for 0% -> 3%
where the time goes in v5:
time: 88.7 us; the launch traced here: 87.3 us
  blocking collectives  65.5 us (74%)
  starting transfers between devices  10.6 us (12%)
  Pallas kernels  6.94 us (8%)
  waiting for transfers between devices  2.28 us (3%)
  local copies, waits for them, and re-layouts  1.91 us (2%)
    all_to_all x2, blocking collectives, across(): return lax.all_to_all(values, 'gy', 0, 0, tiled=True)  65.5 us
    ppermute x2, starting transfers between devices, exchange(): lax.ppermute(far, 'gx', swaps(radial_size, 1))  10.4 us
    pallas_call x7, Pallas kernels, call(): pl.pallas_call(kernel, out_shape=outs, in_specs=[VMEM] * len(args), out_s...  6.94 us
    ppermute x2, waiting for transfers between devices, exchange(): lax.ppermute(far, 'gx', swaps(radial_size, 1))  2.27 us
    unnamed x10, local copies, waits for them, and re-layouts  1.91 us
  transfers between devices with their start and end apart: 4, of which 1 were waited for; matrix products, arithmetic and copies ran while one was open for 0% of the time, Pallas kernels for 3%

profile of v5, /device:TPU:32, one launch (start us, length us, event | category | flops | bytes accessed | tf_op | source)
XLA Modules:
  0.0 87.3 jit_solution(1528781610918542433)
XLA Ops:
  0.0 1.2 %copy-done = f32[8,8,32,128]{3,2,1,0:T(8,128)S(1)} copy-done((f32[8,8,32,128]{3,2,1,0:T(8,128)S(1)}, f32[8,8,32,128]{3,2,1,0:T(8,128)}, u32[]{:S(2)}) %copy-start) | copy-done | bytes 1048600
  1.2 1.3 %pack.1 = f32[16,128,128]{2,1,0:T(8,128)S(1)} custom-call(f32[8,8,32,128]{3,2,1,0:T(8,128)S(1)} %copy-done), custom_call_target="tpu_custom_call" | custom-call | tf_op jit(solution)/shard_map/pack/pallas_call | solution.py:286
  2.5 0.0 copy-start.1
  2.5 0.0 copy-start.2
  2.5 35.6 %all_to_all.10.values = f32[16,128,128]{2,1,0:T(8,128)S(1)} all-to-all(f32[16,128,128]{2,1,0:T(8,128)S(1)} %pack.1), channel_id=1, replica_groups=mesh['gx'=16,'gy'=16] {'gy'}, dimensions={0} | all-to-all | bytes 2097152 | tf_op jit(solution)/shard_map/all_to_all | solution.py:308
  38.1 0.0 copy-done.1
  38.1 0.0 copy-done.2
  38.1 0.3 advect_edges.1
  38.4 0.1 collective-permute-start
  38.5 5.2 %collective-permute-start.1 = (f32[16,16,128]{2,1,0:T(8,128)S(1)}, f32[16,16,128]{2,1,0:T(8,128)S(1)}, u32[]{:S(2)}, u32[]{:S(2)}) collective-permute-start(f32[16,16,128]{2,1,0:T(8,128)S(1)} %get-tuple-element.23), channel_id=1, source_target_pairs={{16,32},{48,64},{80,96},{112,128},{144,160},{176,192},{208,224},{2... | collective-permute-start | bytes 393224 | tf_op jit(solution)/shard_map/ppermute | solution.py:304
  43.7 0.7 copy-done.3
  44.4 0.0 copy-done.4
  44.4 2.2 %inner.1 = (s32[1,2]{1,0:T(1,128)S(1)}, f32[14,8,128]{2,1,0:T(8,128)S(1)}, f32[128,128]{1,0:T(8,128)S(1)}, f32[16,96,128]{2,1,0:T(8,128)S(1)}, f32[16,32,128]{2,1,0:T(8,128)S(1)}) custom-call(s32[1,2]{1,0:T(1,128)S(1)} %bitcast.2, f32[1,8]{1,0:T(1,128)S(1)} %bitcast.3, s32[2,8]{1,0:T(2,128)S(1)} %copy-done.1, f32[2,8]{1,0:T(2,128)S(1)} %copy-done.2, ...), custom_call_target="tpu_custom_call" | custom-call | tf_op jit(solution)/shard_map/inner/pallas_call | solution.py:286
  46.6 0.0 collective-permute-done.col_near
  46.6 0.0 collective-permute-done.1.col_far
  46.6 0.5 edges.1
  47.1 0.1 collective-permute-start.2
  47.2 5.2 %collective-permute-start.3 = (f32[16,16,128]{2,1,0:T(8,128)S(1)}, f32[16,16,128]{2,1,0:T(8,128)S(1)}, u32[]{:S(2)}, u32[]{:S(2)}) collective-permute-start(f32[16,16,128]{2,1,0:T(8,128)S(1)} %get-tuple-element.26), channel_id=1, source_target_pairs={{16,32},{48,64},{80,96},{112,128},{144,160},{176,192},{208,224},{2... | collective-permute-start | bytes 393224 | tf_op jit(solution)/shard_map/ppermute | solution.py:304
  52.4 0.6 last_interior.1.inside
  53.0 0.0 collective-permute-done.2.col_near
  53.1 2.3 %collective-permute-done.3.col_far = f32[16,16,128]{2,1,0:T(8,128)S(1)} collective-permute-done((f32[16,16,128]{2,1,0:T(8,128)S(1)}, f32[16,16,128]{2,1,0:T(8,128)S(1)}, u32[]{:S(2)}, u32[]{:S(2)}) %collective-permute-start.3) | collective-permute-done | bytes 131104 | tf_op jit(solution)/shard_map/ppermute | solution.py:304
  55.3 0.1 last_edges.1
  55.4 29.9 %all_to_all.11.packed = f32[16,128,128]{2,1,0:T(8,128)S(1)} all-to-all(f32[16,128,128]{2,1,0:T(8,128)S(1)} %last_edges.1), channel_id=1, replica_groups=mesh['gx'=16,'gy'=16] {'gy'}, dimensions={0} | all-to-all | bytes 2097152 | tf_op jit(solution)/shard_map/all_to_all | solution.py:308
  85.3 2.0 %unpack.1 = f32[8,8,32,128]{3,2,1,0:T(8,128)} custom-call(f32[128,128]{1,0:T(8,128)S(1)} %get-tuple-element.17.back, f32[16,128,128]{2,1,0:T(8,128)S(1)} %all_to_all.11.packed), custom_call_target="tpu_custom_call" | custom-call | tf_op jit(solution)/shard_map/unpack/pallas_call | solution.py:286
  (3 shorter events, 0.0 us)
Async XLA Ops:
  0.0 1.2 %copy-start = (f32[8,8,32,128]{3,2,1,0:T(8,128)S(1)}, f32[8,8,32,128]{3,2,1,0:T(8,128)}, u32[]{:S(2)}) copy-start(f32[8,8,32,128]{3,2,1,0:T(8,128)} %state.1) | copy-start | bytes 3145732
  2.5 35.6 %copy-start.1 = (s32[2,8]{1,0:T(2,128)S(1)}, s32[2,8]{1,0:T(2,128)}, u32[]{:S(2)}) copy-start(s32[2,8]{1,0:T(2,128)} %shifts.5) | copy-start | bytes 196
  2.5 35.6 %copy-start.2 = (f32[2,8]{1,0:T(2,128)S(1)}, f32[2,8]{1,0:T(2,128)}, u32[]{:S(2)}) copy-start(f32[2,8]{1,0:T(2,128)} %fracs.5) | copy-start | bytes 196
  38.4 8.2 %collective-permute-start = (f32[16,16,128]{2,1,0:T(8,128)S(1)}, f32[16,16,128]{2,1,0:T(8,128)S(1)}, u32[]{:S(2)}, u32[]{:S(2)}) collective-permute-start(f32[16,16,128]{2,1,0:T(8,128)S(1)} %get-tuple-element.22), channel_id=1, source_target_pairs={{0,16},{32,48},{64,80},{96,112},{128,144},{160,176},{192,208},{224... | collective-permute-start | bytes 393224 | tf_op jit(solution)/shard_map/ppermute | solution.py:304
  38.5 8.1 %collective-permute-start.1 = (f32[16,16,128]{2,1,0:T(8,128)S(1)}, f32[16,16,128]{2,1,0:T(8,128)S(1)}, u32[]{:S(2)}, u32[]{:S(2)}) collective-permute-start(f32[16,16,128]{2,1,0:T(8,128)S(1)} %get-tuple-element.23), channel_id=1, source_target_pairs={{16,32},{48,64},{80,96},{112,128},{144,160},{176,192},{208,224},{2... | collective-permute-start | bytes 393224 | tf_op jit(solution)/shard_map/ppermute | solution.py:304
  43.7 0.7 copy-start.3
  43.7 0.7 copy-start.4
  47.1 5.9 %collective-permute-start.2 = (f32[16,16,128]{2,1,0:T(8,128)S(1)}, f32[16,16,128]{2,1,0:T(8,128)S(1)}, u32[]{:S(2)}, u32[]{:S(2)}) collective-permute-start(f32[16,16,128]{2,1,0:T(8,128)S(1)} %get-tuple-element.25), channel_id=1, source_target_pairs={{0,16},{32,48},{64,80},{96,112},{128,144},{160,176},{192,208},{224... | collective-permute-start | bytes 393224 | tf_op jit(solution)/shard_map/ppermute | solution.py:304
  47.2 8.1 %collective-permute-start.3 = (f32[16,16,128]{2,1,0:T(8,128)S(1)}, f32[16,16,128]{2,1,0:T(8,128)S(1)}, u32[]{:S(2)}, u32[]{:S(2)}) collective-permute-start(f32[16,16,128]{2,1,0:T(8,128)S(1)} %get-tuple-element.26), channel_id=1, source_target_pairs={{16,32},{48,64},{80,96},{112,128},{144,160},{176,192},{208,224},{2... | collective-permute-start | bytes 393224 | tf_op jit(solution)/shard_map/ppermute | solution.py:304

commit v6 on v5

v6 whole, which is shorter than its diff:
```python
import math
import jax
import jax.numpy as jnp
from jax import lax
from jax.experimental import pallas as pl
from jax.experimental.pallas import tpu as pltpu
from jax.sharding import PartitionSpec as P

spin_gain = 0.2
spin_drag = 0.05
tidal_gain = 0.3

LANES = 128
BLOCKS = 16
COLS = 8
HALF_VARS = 4
MODES = 4
COL_ROWS = HALF_VARS * MODES
ROWS = COLS * COL_ROWS
HALVES = 2
MODE_BLOCKS = 8
NZ = MODES * MODE_BLOCKS
VARS = HALVES * HALF_VARS
LAST = COLS - 1
SIDE_ROWS = 2 * COL_ROWS
CENTERS = 4 + COLS
GHOST_TIDES = CENTERS + 2
COEFS = GHOST_TIDES + 2

F32 = jnp.float32
VMEM = pl.BlockSpec(memory_space=pltpu.VMEM)
PARAMS = pltpu.CompilerParams(vmem_limit_bytes=28 * 1024 * 1024)


def shape(*dims):
    return jax.ShapeDtypeStruct(dims, F32)


def lane_index():
    return lax.broadcasted_iota(jnp.int32, (8, LANES), 1)


def row_index():
    return lax.broadcasted_iota(jnp.int32, (8, LANES), 0)


def rotated(block, earlier, amount, lanes):
    joined = jnp.where(lanes < LANES - amount, block, earlier)
    return pltpu.roll(joined, amount & (LANES - 1), 1)


def cosine(angle, mode):
    size = jnp.where(mode == 0, (1.0 / NZ) ** 0.5, (2.0 / NZ) ** 0.5)
    return size * jnp.cos((angle & (4 * NZ - 1)).astype(F32) * (math.pi / (2 * NZ)))


def to_modes(transposed):
    dims = (HALF_VARS * NZ, HALF_VARS * NZ)
    row = lax.broadcasted_iota(jnp.int32, dims, 1 if transposed else 0)
    column = lax.broadcasted_iota(jnp.int32, dims, 0 if transposed else 1)
    mode = (row // COL_ROWS) * MODES + row % MODES
    level = column % NZ
    same = (row // MODES) % HALF_VARS == column // NZ
    return jnp.where(same, cosine((2 * level + 1) * mode, mode), 0.0)


def exact_dot(left, right):
    return lax.dot(left, right, precision=lax.Precision.HIGHEST, preferred_element_type=F32)


def pack_kernel(state, out):
    basis = to_modes(False)
    for half in range(HALVES):
        for col in range(COLS):
            levels = jnp.concatenate([state[half * HALF_VARS + var, col] for var in range(HALF_VARS)], axis=0)
            modes = exact_dot(basis, levels)
            for block in range(MODE_BLOCKS):
                out[half * MODE_BLOCKS + block, col * COL_ROWS : (col + 1) * COL_ROWS, :] = modes[
                    block * COL_ROWS : (block + 1) * COL_ROWS
                ]


def unpack_kernel(back, packed, out):
    basis = back[...]
    for half in range(HALVES):
        for col in range(COLS):
            modes = jnp.concatenate(
                [
                    packed[half * MODE_BLOCKS + block, col * COL_ROWS : (col + 1) * COL_ROWS, :]
                    for block in range(MODE_BLOCKS)
                ],
                axis=0,
            )
            levels = exact_dot(basis, modes)
            for var in range(HALF_VARS):
                out[half * HALF_VARS + var, col] = levels[var * NZ : (var + 1) * NZ]


def move(values, block, rows, turn, weight):
    source = (block - turn // LANES) & (BLOCKS - 1)
    before = (source - 1) & (BLOCKS - 1)
    rest = turn & (LANES - 1)
    lanes = lane_index()
    here = values[source, rows, :]
    earlier = values[before, rows, :]
    nearer = rotated(here, earlier, rest, lanes)
    farther = rotated(here, earlier, rest + 1, lanes)
    return (1.0 - weight) * nearer + weight * farther


def is_even(place):
    return (place[0] & 1) == 0


def turned(values, block, rows, turn):
    here = (block - turn // LANES) & (BLOCKS - 1)
    before = (here - 1) & (BLOCKS - 1)
    return rotated(values[here, rows, :], values[before, rows, :], turn & (LANES - 1), lane_index())


def where_am_i():
    around = lax.axis_index("gy")
    return lax.axis_index("gx"), around // MODE_BLOCKS, around % MODE_BLOCKS, lax.axis_size("gx")


def prepare(place, kappa, coefs):
    radial, half, vertical = place[0], place[1], place[2]
    first_half = half == 0
    row = row_index()
    upper_rows = row >= MODES
    mode = vertical * MODES + (row & (MODES - 1))
    own = 2.0 * jnp.cos(mode.astype(F32) * (math.pi / NZ)) - 6.0
    for pair in range(2):
        lower, upper = [
            jnp.where(first_half, kappa[0, 2 * pair + var], kappa[0, HALF_VARS + 2 * pair + var]) for var in range(2)
        ]
        rate = jnp.where(upper_rows, upper, lower)
        coefs[pair] = rate
        coefs[CENTERS + pair] = 1.0 + rate * own
    coupled = jnp.where(first_half, 1.0, 0.0)
    coefs[2] = jnp.where(upper_rows, spin_gain * coupled, 0.0)
    coefs[3] = jnp.where(upper_rows, 0.0, -spin_drag * coupled)
    total = place[3] * COLS
    columns = [(4 + col, radial * COLS + col) for col in range(COLS)]
    columns.append((GHOST_TIDES, jnp.where(radial == 0, total - 1, radial * COLS - 1)))
    columns.append((GHOST_TIDES + 1, jnp.where(radial == place[3] - 1, 0, radial * COLS + COLS)))
    for slot, column in columns:
        position = (column.astype(F32) + 0.5) / float(total) - 0.5
        coefs[slot] = jnp.where(upper_rows, tidal_gain * position * coupled, 0.0)


def sourced(mixed, coefs, tide):
    swapped = [pltpu.roll(part, 4, 0) for part in mixed]
    return mixed[0] + coefs[2] * swapped[1] + tide * swapped[0], mixed[1] + coefs[3] * swapped[0]


def around(values, block, rows):
    lanes = lane_index()
    value = values[block, rows, :]
    after = values[(block + 1) % BLOCKS, rows, :]
    before = values[(block - 1) % BLOCKS, rows, :]
    prior = pltpu.roll(jnp.where(lanes < LANES - 1, value, before), 1, 1)
    following = pltpu.roll(jnp.where(lanes >= 1, value, after), LANES - 1, 1)
    return prior + following


def tiles(start):
    return [pl.ds(start + pair * 8, 8) for pair in range(2)]


def interior(coefs, adv, block, col, low, high):
    mixed = []
    for pair, rows in enumerate(tiles(col * COL_ROWS)):
        beside = [
            adv[block, pl.ds((col + side) * COL_ROWS + pair * 8, 8), :]
            for side in (-1, 1)
            if low <= col + side <= high
        ]
        total = sum(beside[1:], beside[0]) + around(adv, block, rows)
        mixed.append(coefs[CENTERS + pair] * adv[block, rows, :] + coefs[pair] * total)
    return sourced(mixed, coefs, coefs[4 + col])


def advect_edges_kernel(shifts, fracs, values, edges, near, far):
    even = is_even(where_am_i())
    shifts = shifts[...]
    fracs = fracs[...]
    for block in range(BLOCKS):
        for depth in range(2):
            low_col, high_col = depth, LAST - depth
            for pair in range(2):
                low, high = [
                    move(values, block, pl.ds(col * COL_ROWS + pair * 8, 8), shifts[0, col], fracs[0, col])
                    for col in (low_col, high_col)
                ]
                start = depth * SIDE_ROWS + pair * 8
                edges[block, pl.ds(start, 8), :] = low
                edges[block, pl.ds(start + COL_ROWS, 8), :] = high
                rows = pl.ds(depth * COL_ROWS + pair * 8, 8)
                near[block, rows, :] = jnp.where(even, high, low)
                far[block, rows, :] = jnp.where(even, low, high)
    lanes = lane_index()
    low, high = [
        jnp.where(lanes == 0, shifts[1, col].astype(F32), jnp.where(lanes == 1, fracs[1, col], 0.0))
        for col in (0, LAST)
    ]
    for target, side in ((near, jnp.where(even, high, low)), (far, jnp.where(even, low, high))):
        target[BLOCKS] = jnp.zeros((SIDE_ROWS, LANES), F32)
        target[BLOCKS, pl.ds(0, 8), :] = side


def inner_kernel(offsets, kappa, shifts, fracs, values, edges, offsets_out, coefs, back, partial, beyond, unfinished,
                 middle, adv, current):
    offsets_out[...] = offsets[...]
    back[...] = to_modes(True)
    prepare(where_am_i(), kappa[...], coefs)
    shifts = shifts[...]
    fracs = fracs[...]
    for block in range(BLOCKS):
        for slot, col in enumerate((0, LAST, 1, LAST - 1)):
            adv[block, pl.ds(col * COL_ROWS, COL_ROWS), :] = edges[block, pl.ds(slot * COL_ROWS, COL_ROWS), :]
        for col in range(2, LAST - 1):
            for rows in tiles(col * COL_ROWS):
                adv[block, rows, :] = move(values, block, rows, shifts[0, col], fracs[0, col])
    for block in range(BLOCKS):
        for col in range(COLS):
            for rows, result in zip(tiles(col * COL_ROWS), interior(coefs, adv, block, col, 0, LAST)):
                current[block, rows, :] = result
        partial[block, pl.ds(0, COL_ROWS), :] = current[block, pl.ds(0, COL_ROWS), :]
        partial[block, pl.ds(COL_ROWS, COL_ROWS), :] = current[block, pl.ds(LAST * COL_ROWS, COL_ROWS), :]
    for block in range(BLOCKS):
        for col in range(1, LAST):
            for rows in tiles(col * COL_ROWS):
                adv[block, rows, :] = move(current, block, rows, shifts[1, col], fracs[1, col])
    for block in range(BLOCKS):
        for slot, col in enumerate((1, LAST - 1)):
            beyond[block, pl.ds(slot * COL_ROWS, COL_ROWS), :] = adv[block, pl.ds(col * COL_ROWS, COL_ROWS), :]
        for col in range(1, LAST):
            for pair, result in enumerate(interior(coefs, adv, block, col, 1, LAST - 1)):
                if col == 1:
                    unfinished[block, pl.ds(pair * 8, 8), :] = result
                elif col == LAST - 1:
                    unfinished[block, pl.ds(COL_ROWS + pair * 8, 8), :] = result
                else:
                    middle[block, pl.ds((col - 2) * COL_ROWS + pair * 8, 8), :] = result


def outer_kernel(offsets, coefs, shifts, fracs, edges, partial, beyond, unfinished, middle, near, far, out,
                 own, ghost, own_moved, ghost_moved):
    place = where_am_i()
    even = is_even(place)
    radial, radial_size = place[0], place[3]
    shifts = shifts[...]
    fracs = fracs[...]
    offsets = offsets[...]
    signed = jnp.where(radial == 0, 1, jnp.where(radial == radial_size - 1, -1, 0))
    total_y = BLOCKS * LANES

    def side_tiles(side, base=0):
        return [pl.ds(pl.multiple_of(base + side * COL_ROWS + pair * 8, 8), 8) for pair in range(2)]

    for index, (message, side) in enumerate(((near, jnp.where(even, 1, 0)), (far, jnp.where(even, 0, 1)))):
        crosses = index == 1
        slots = tiles(index * COL_ROWS)
        own_tide = coefs[4 + LAST * side]
        ghost_tide = coefs[GHOST_TIDES + side]
        next_tide = coefs[5 + (LAST - 2) * side]
        mine = side_tiles(side)
        scalars = message[BLOCKS, pl.ds(0, 8), :]
        ghost_turn = scalars.astype(jnp.int32)[0, 0]
        ghost_weight = scalars[0, 1]
        own_turn = jnp.where(side == 0, shifts[1, 0], shifts[1, LAST])
        own_weight = jnp.where(side == 0, fracs[1, 0], fracs[1, LAST])

        first_turn = (signed * offsets[0, 0]) & (total_y - 1)
        back_turn = (-signed * offsets[0, 0]) & (total_y - 1)
        for block in range(BLOCKS):
            arrived = []
            mixed = []
            for pair, rows in enumerate(tiles(0)):
                value = message[block, rows, :]
                if crosses:
                    incoming = turned(message, block, rows, first_turn)
                    outgoing = turned(edges, block, mine[pair], back_turn)
                else:
                    incoming = value
                    outgoing = edges[block, mine[pair], :]
                arrived.append(coefs[pair] * incoming)
                other = message[block, tiles(COL_ROWS)[pair], :]
                total = (other + outgoing) + around(message, block, rows)
                mixed.append(coefs[CENTERS + pair] * value + coefs[pair] * total)
            for pair, extra in enumerate(sourced(arrived, coefs, own_tide)):
                own[block, slots[pair], :] = partial[block, mine[pair], :] + extra
            for pair, result in enumerate(sourced(mixed, coefs, ghost_tide)):
                ghost[block, slots[pair], :] = result
        for block in range(BLOCKS):
            for rows in slots:
                own_moved[block, rows, :] = move(own, block, rows, own_turn, own_weight)
                ghost_moved[block, rows, :] = move(ghost, block, rows, ghost_turn, ghost_weight)
        last_turn = (signed * offsets[0, 1]) & (total_y - 1)
        own_out = [
            pl.ds(pl.multiple_of(LAST * COL_ROWS * side + pair * 8, 8), 8) for pair in range(2)
        ]
        next_out = [
            pl.ds(pl.multiple_of(COL_ROWS + (LAST - 2) * COL_ROWS * side + pair * 8, 8), 8) for pair in range(2)
        ]
        for block in range(BLOCKS):
            mixed = []
            arrived = []
            for pair, rows in enumerate(slots):
                value = own_moved[block, rows, :]
                if crosses:
                    incoming = turned(ghost_moved, block, rows, last_turn)
                else:
                    incoming = ghost_moved[block, rows, :]
                total = (incoming + beyond[block, mine[pair], :]) + around(own_moved, block, rows)
                mixed.append(coefs[CENTERS + pair] * value + coefs[pair] * total)
                arrived.append(coefs[pair] * value)
            for pair, result in enumerate(sourced(mixed, coefs, own_tide)):
                out[block, own_out[pair], :] = result
            for pair, extra in enumerate(sourced(arrived, coefs, next_tide)):
                out[block, next_out[pair], :] = unfinished[block, mine[pair], :] + extra
    for block in range(BLOCKS):
        out[block, pl.ds(SIDE_ROWS, 4 * COL_ROWS), :] = middle[block]


def call(kernel, name, outs, *args, scratch=()):
    return pl.pallas_call(
        kernel,
        out_shape=outs,
        in_specs=[VMEM] * len(args),
        out_specs=jax.tree.map(lambda _: VMEM, outs),
        scratch_shapes=scratch,
        compiler_params=PARAMS,
        name=name,
    )(*args)


def swaps(count, first):
    pairs = [(i % count, (i + 1) % count) for i in range(first, count, 2)]
    return pairs + [(target, source) for source, target in pairs]


def exchange(near, far):
    radial_size = lax.axis_size("gx")
    return lax.ppermute(near, "gx", swaps(radial_size, 0)), lax.ppermute(far, "gx", swaps(radial_size, 1))


def across(values):
    return lax.all_to_all(values, "gy", 0, 0, tiled=True)


def on_device(state, shifts, fracs, offsets, kappa):
    whole = shape(BLOCKS, ROWS, LANES)
    side = shape(BLOCKS, SIDE_ROWS, LANES)
    message = shape(BLOCKS + 1, SIDE_ROWS, LANES)
    offsets = offsets[None]
    kappa = kappa[None]
    values = across(call(pack_kernel, "pack", whole, state))
    edges, near, far = call(
        advect_edges_kernel,
        "advect_edges",
        (shape(BLOCKS, 2 * SIDE_ROWS, LANES), message, message),
        shifts,
        fracs,
        values,
    )
    halos = exchange(near, far)
    offsets, coefs, back, partial, beyond, unfinished, middle = call(
        inner_kernel,
        "inner",
        (
            jax.ShapeDtypeStruct(offsets.shape, offsets.dtype),
            shape(COEFS, 8, LANES),
            shape(HALF_VARS * NZ, HALF_VARS * NZ),
            side,
            side,
            side,
            shape(BLOCKS, 4 * COL_ROWS, LANES),
        ),
        offsets,
        kappa,
        shifts,
        fracs,
        values,
        edges,
        scratch=[pltpu.VMEM((BLOCKS, ROWS, LANES), F32)] * 2,
    )
    values = call(
        outer_kernel,
        "outer",
        whole,
        offsets,
        coefs,
        shifts,
        fracs,
        edges,
        partial,
        beyond,
        unfinished,
        middle,
        *halos,
        scratch=[pltpu.VMEM((BLOCKS, SIDE_ROWS, LANES), F32)] * 4,
    )
    return call(unpack_kernel, "unpack", shape(VARS, COLS, NZ, LANES), back, across(values))


def solution(mesh):
    placed = (P(None, "gx", None, "gy"), P(None, "gx"), P(None, "gx"), P(), P())
    return jax.shard_map(
        on_device, mesh=mesh, in_specs=placed, out_specs=P(None, "gx", None, "gy"), check_vma=False
    )
```

time: 88.7 us -> 86 us (0.970)
  starting transfers between devices: 10.6 us -> 5.29 us
  blocking collectives: 65.5 us -> 68.6 us
  waiting for transfers between devices: 2.28 us -> 1.09 us
    ppermute x2 -> x1, starting transfers between devices: 10.4 us -> 5.2 us  [exchange(): lax.ppermute(far, 'gx', swaps(radial_size, 1))]
    all_to_all x2, blocking collectives: 65.5 us -> 68.6 us  [across(): return lax.all_to_all(values, 'gy', 0, 0, tiled=True)]
    ppermute x2 -> x1, waiting for transfers between devices: 2.27 us -> 1.09 us  [exchange(): lax.ppermute(far, 'gx', swaps(radial_size, 1))]
    pallas_call x7 -> x5, Pallas kernels: 6.94 us -> 7.71 us  [call(): pl.pallas_call(kernel, out_shape=outs, in_specs=[VMEM] * len(args), out_s...]
  transfers between devices with their start and end apart: 4 -> 2, of which waited for: 1 -> 1; matrix products, arithmetic and copies ran while one was open for 0% -> 0% of each run, Pallas kernels for 3% -> 3%
where the time goes in v6:
time: 86 us; the launch traced here: 84.7 us
  blocking collectives  68.6 us (80%)
  Pallas kernels  7.71 us (9%)
  starting transfers between devices  5.29 us (6%)
  local copies, waits for them, and re-layouts  1.91 us (2%)
  waiting for transfers between devices  1.09 us (1%)
    all_to_all x2, blocking collectives, across(): return lax.all_to_all(values, 'gy', 0, 0, tiled=True)  68.6 us
    pallas_call x5, Pallas kernels, call(): pl.pallas_call(kernel, out_shape=outs, in_specs=[VMEM] * len(args), out_s...  7.71 us
    ppermute x1, starting transfers between devices, exchange(): lax.ppermute(far, 'gx', swaps(radial_size, 1))  5.2 us
    unnamed x10, local copies, waits for them, and re-layouts  1.91 us
  transfers between devices with their start and end apart: 2, of which 1 were waited for; matrix products, arithmetic and copies ran while one was open for 0% of the time, Pallas kernels for 3%

profile of v6, /device:TPU:32, one launch (start us, length us, event | category | flops | bytes accessed | tf_op | source)
XLA Modules:
  0.0 84.7 jit_solution(4811518517833583011)
XLA Ops:
  0.0 0.0 copy-start
  0.0 1.2 %copy-done = f32[8,8,32,128]{3,2,1,0:T(8,128)S(1)} copy-done((f32[8,8,32,128]{3,2,1,0:T(8,128)S(1)}, f32[8,8,32,128]{3,2,1,0:T(8,128)}, u32[]{:S(2)}) %copy-start) | copy-done | bytes 1048600
  1.2 1.3 %pack.1 = f32[16,128,128]{2,1,0:T(8,128)S(1)} custom-call(f32[8,8,32,128]{3,2,1,0:T(8,128)S(1)} %copy-done), custom_call_target="tpu_custom_call" | custom-call | tf_op jit(solution)/shard_map/pack/pallas_call | solution.py:328
  2.5 0.0 copy-start.1
  2.5 0.0 copy-start.2
  2.5 35.6 %all_to_all.10.values = f32[16,128,128]{2,1,0:T(8,128)S(1)} all-to-all(f32[16,128,128]{2,1,0:T(8,128)S(1)} %pack.1), channel_id=1, replica_groups=mesh['gx'=16,'gy'=16] {'gy'}, dimensions={0} | all-to-all | bytes 2097152 | tf_op jit(solution)/shard_map/all_to_all | solution.py:350
  38.1 0.0 copy-done.1
  38.1 0.0 copy-done.2
  38.1 0.4 advect_edges.1
  38.6 0.1 collective-permute-start
  38.7 5.2 %collective-permute-start.1 = (f32[17,32,128]{2,1,0:T(8,128)S(1)}, f32[17,32,128]{2,1,0:T(8,128)S(1)}, u32[]{:S(2)}, u32[]{:S(2)}) collective-permute-start(f32[17,32,128]{2,1,0:T(8,128)S(1)} %get-tuple-element.24), channel_id=1, source_target_pairs={{16,32},{48,64},{80,96},{112,128},{144,160},{176,192},{208,224},{2... | collective-permute-start | bytes 835592 | tf_op jit(solution)/shard_map/ppermute | solution.py:346
  43.9 0.0 copy-start.3
  43.9 0.0 copy-start.4
  43.9 0.7 copy-done.3
  44.6 0.0 copy-done.4
  44.6 2.8 %inner.1 = (s32[1,2]{1,0:T(1,128)S(1)}, f32[16,8,128]{2,1,0:T(8,128)S(1)}, f32[128,128]{1,0:T(8,128)S(1)}, f32[16,32,128]{2,1,0:T(8,128)S(1)}, f32[16,32,128]{2,...) custom-call(s32[1,2]{1,0:T(1,128)S(1)} %bitcast.2, f32[1,8]{1,0:T(1,128)S(1)} %bitcast.3, ...), custom_call_target="tpu_custom_call" | custom-call | tf_op jit(solution)/shard_map/inner/pallas_call | solution.py:328
  47.4 0.0 collective-permute-done.near
  47.4 1.1 %collective-permute-done.1.far = f32[17,32,128]{2,1,0:T(8,128)S(1)} collective-permute-done((f32[17,32,128]{2,1,0:T(8,128)S(1)}, f32[17,32,128]{2,1,0:T(8,128)S(1)}, u32[]{:S(2)}, u32[]{:S(2)}) %collective-permute-start.1) | collective-permute-done | bytes 278560 | tf_op jit(solution)/shard_map/ppermute | solution.py:346
  48.5 1.2 %outer.1 = f32[16,128,128]{2,1,0:T(8,128)S(1)} custom-call(s32[1,2]{1,0:T(1,128)S(1)} %get-tuple-element.17.offsets, f32[16,8,128]{2,1,0:T(8,128)S(1)} %get-tuple-element.18.coefs, s32[2,8]{1,0:T(2,128)S(1)} %copy-done.1, f32[2,8]{1,0:T(2,128)S(1)} %copy-done.2, f32[16,64,128]{2,1,0:T(8,128)S(1)} %get-tuple-element.15.edges, ...), custom_call_target="tpu_custom_call" | custom-call | tf_op jit(solution)/shard_map/outer/pallas_call | solution.py:328
  49.7 33.0 %all_to_all.11.packed = f32[16,128,128]{2,1,0:T(8,128)S(1)} all-to-all(f32[16,128,128]{2,1,0:T(8,128)S(1)} %outer.1), channel_id=1, replica_groups=mesh['gx'=16,'gy'=16] {'gy'}, dimensions={0} | all-to-all | bytes 2097152 | tf_op jit(solution)/shard_map/all_to_all | solution.py:350
  82.7 2.0 %unpack.1 = f32[8,8,32,128]{3,2,1,0:T(8,128)} custom-call(f32[128,128]{1,0:T(8,128)S(1)} %get-tuple-element.16.back, f32[16,128,128]{2,1,0:T(8,128)S(1)} %all_to_all.11.packed), custom_call_target="tpu_custom_call" | custom-call | tf_op jit(solution)/shard_map/unpack/pallas_call | solution.py:328
Async XLA Ops:
  0.0 1.2 %copy-start = (f32[8,8,32,128]{3,2,1,0:T(8,128)S(1)}, f32[8,8,32,128]{3,2,1,0:T(8,128)}, u32[]{:S(2)}) copy-start(f32[8,8,32,128]{3,2,1,0:T(8,128)} %state.1) | copy-start | bytes 3145732
  2.5 35.6 %copy-start.1 = (s32[2,8]{1,0:T(2,128)S(1)}, s32[2,8]{1,0:T(2,128)}, u32[]{:S(2)}) copy-start(s32[2,8]{1,0:T(2,128)} %shifts.5) | copy-start | bytes 196
  2.5 35.6 %copy-start.2 = (f32[2,8]{1,0:T(2,128)S(1)}, f32[2,8]{1,0:T(2,128)}, u32[]{:S(2)}) copy-start(f32[2,8]{1,0:T(2,128)} %fracs.5) | copy-start | bytes 196
  38.6 8.8 %collective-permute-start = (f32[17,32,128]{2,1,0:T(8,128)S(1)}, f32[17,32,128]{2,1,0:T(8,128)S(1)}, u32[]{:S(2)}, u32[]{:S(2)}) collective-permute-start(f32[17,32,128]{2,1,0:T(8,128)S(1)} %get-tuple-element.23), channel_id=1, source_target_pairs={{0,16},{32,48},{64,80},{96,112},{128,144},{160,176},{192,208},{224... | collective-permute-start | bytes 835592 | tf_op jit(solution)/shard_map/ppermute | solution.py:346
  38.7 9.8 %collective-permute-start.1 = (f32[17,32,128]{2,1,0:T(8,128)S(1)}, f32[17,32,128]{2,1,0:T(8,128)S(1)}, u32[]{:S(2)}, u32[]{:S(2)}) collective-permute-start(f32[17,32,128]{2,1,0:T(8,128)S(1)} %get-tuple-element.24), channel_id=1, source_target_pairs={{16,32},{48,64},{80,96},{112,128},{144,160},{176,192},{208,224},{2... | collective-permute-start | bytes 835592 | tf_op jit(solution)/shard_map/ppermute | solution.py:346
  43.9 0.7 copy-start.3
  43.9 0.7 copy-start.4

commit v7 on v6

--- a/solution.py
+++ b/solution.py
@@ -181,44 +181,53 @@
     return sourced(mixed, coefs, coefs[4 + col])
 
 
-def advect_edges_kernel(shifts, fracs, values, edges, near, far):
-    even = is_even(where_am_i())
-    shifts = shifts[...]
-    fracs = fracs[...]
-    for block in range(BLOCKS):
-        for depth in range(2):
-            low_col, high_col = depth, LAST - depth
+def side_of(place, crosses):
+    even = is_even(place)
+    return jnp.where(even, 0, 1) if crosses else jnp.where(even, 1, 0)
+
+
+def edge_column(side, depth):
+    return jnp.where(side == 0, depth, LAST - depth)
+
+
+def advect_side(crosses, shifts, fracs, values, message):
+    side = side_of(where_am_i(), crosses)
+
+    def pick(table, step, depth):
+        return jnp.where(side == 0, table[step, depth], table[step, LAST - depth])
+
+    for depth in range(2):
+        turn, weight = pick(shifts, 0, depth), pick(fracs, 0, depth)
+        start = edge_column(side, depth) * COL_ROWS
+        for block in range(BLOCKS):
             for pair in range(2):
-                low, high = [
-                    move(values, block, pl.ds(col * COL_ROWS + pair * 8, 8), shifts[0, col], fracs[0, col])
-                    for col in (low_col, high_col)
-                ]
-                start = depth * SIDE_ROWS + pair * 8
-                edges[block, pl.ds(start, 8), :] = low
-                edges[block, pl.ds(start + COL_ROWS, 8), :] = high
-                rows = pl.ds(depth * COL_ROWS + pair * 8, 8)
-                near[block, rows, :] = jnp.where(even, high, low)
-                far[block, rows, :] = jnp.where(even, low, high)
+                rows = pl.ds(pl.multiple_of(start + pair * 8, 8), 8)
+                message[block, pl.ds(depth * COL_ROWS + pair * 8, 8), :] = move(values, block, rows, turn, weight)
     lanes = lane_index()
-    low, high = [
-        jnp.where(lanes == 0, shifts[1, col].astype(F32), jnp.where(lanes == 1, fracs[1, col], 0.0))
-        for col in (0, LAST)
-    ]
-    for target, side in ((near, jnp.where(even, high, low)), (far, jnp.where(even, low, high))):
-        target[BLOCKS] = jnp.zeros((SIDE_ROWS, LANES), F32)
-        target[BLOCKS, pl.ds(0, 8), :] = side
-
-
-def inner_kernel(offsets, kappa, shifts, fracs, values, edges, offsets_out, coefs, back, partial, beyond, unfinished,
+    turn, weight = pick(shifts, 1, 0).astype(F32), pick(fracs, 1, 0)
+    message[BLOCKS] = jnp.zeros((SIDE_ROWS, LANES), F32)
+    message[BLOCKS, pl.ds(0, 8), :] = jnp.where(lanes == 0, turn, jnp.where(lanes == 1, weight, 0.0))
+
+
+def advect_far_kernel(shifts, fracs, values, message):
+    advect_side(True, shifts[...], fracs[...], values, message)
+
+
+def inner_kernel(offsets, kappa, shifts, fracs, values, far, near, offsets_out, coefs, back, partial, beyond, unfinished,
                  middle, adv, current):
     offsets_out[...] = offsets[...]
     back[...] = to_modes(True)
-    prepare(where_am_i(), kappa[...], coefs)
+    place = where_am_i()
+    prepare(place, kappa[...], coefs)
     shifts = shifts[...]
     fracs = fracs[...]
+    advect_side(False, shifts, fracs, values, near)
     for block in range(BLOCKS):
-        for slot, col in enumerate((0, LAST, 1, LAST - 1)):
-            adv[block, pl.ds(col * COL_ROWS, COL_ROWS), :] = edges[block, pl.ds(slot * COL_ROWS, COL_ROWS), :]
+        for message, crosses in ((near, False), (far, True)):
+            side = side_of(place, crosses)
+            for depth in range(2):
+                start = pl.multiple_of(edge_column(side, depth) * COL_ROWS, COL_ROWS)
+                adv[block, pl.ds(start, COL_ROWS), :] = message[block, pl.ds(depth * COL_ROWS, COL_ROWS), :]
         for col in range(2, LAST - 1):
             for rows in tiles(col * COL_ROWS):
                 adv[block, rows, :] = move(values, block, rows, shifts[0, col], fracs[0, col])
@@ -245,10 +254,9 @@
                     middle[block, pl.ds((col - 2) * COL_ROWS + pair * 8, 8), :] = result
 
 
-def outer_kernel(offsets, coefs, shifts, fracs, edges, partial, beyond, unfinished, middle, near, far, out,
+def outer_kernel(offsets, coefs, shifts, fracs, near_sent, far_sent, partial, beyond, unfinished, middle, near, far, out,
                  own, ghost, own_moved, ghost_moved):
     place = where_am_i()
-    even = is_even(place)
     radial, radial_size = place[0], place[3]
     shifts = shifts[...]
     fracs = fracs[...]
@@ -259,8 +267,9 @@
     def side_tiles(side, base=0):
         return [pl.ds(pl.multiple_of(base + side * COL_ROWS + pair * 8, 8), 8) for pair in range(2)]
 
-    for index, (message, side) in enumerate(((near, jnp.where(even, 1, 0)), (far, jnp.where(even, 0, 1)))):
+    for index, (message, sent) in enumerate(((near, near_sent), (far, far_sent))):
         crosses = index == 1
+        side = side_of(place, crosses)
         slots = tiles(index * COL_ROWS)
         own_tide = coefs[4 + LAST * side]
         ghost_tide = coefs[GHOST_TIDES + side]
@@ -281,10 +290,10 @@
                 value = message[block, rows, :]
                 if crosses:
                     incoming = turned(message, block, rows, first_turn)
-                    outgoing = turned(edges, block, mine[pair], back_turn)
+                    outgoing = turned(sent, block, rows, back_turn)
                 else:
                     incoming = value
-                    outgoing = edges[block, mine[pair], :]
+                    outgoing = sent[block, rows, :]
                 arrived.append(coefs[pair] * incoming)
                 other = message[block, tiles(COL_ROWS)[pair], :]
                 total = (other + outgoing) + around(message, block, rows)
@@ -341,11 +350,6 @@
     return pairs + [(target, source) for source, target in pairs]
 
 
-def exchange(near, far):
-    radial_size = lax.axis_size("gx")
-    return lax.ppermute(near, "gx", swaps(radial_size, 0)), lax.ppermute(far, "gx", swaps(radial_size, 1))
-
-
 def across(values):
     return lax.all_to_all(values, "gy", 0, 0, tiled=True)
 
@@ -353,23 +357,18 @@
 def on_device(state, shifts, fracs, offsets, kappa):
     whole = shape(BLOCKS, ROWS, LANES)
     side = shape(BLOCKS, SIDE_ROWS, LANES)
-    message = shape(BLOCKS + 1, SIDE_ROWS, LANES)
     offsets = offsets[None]
     kappa = kappa[None]
     values = across(call(pack_kernel, "pack", whole, state))
-    edges, near, far = call(
-        advect_edges_kernel,
-        "advect_edges",
-        (shape(BLOCKS, 2 * SIDE_ROWS, LANES), message, message),
-        shifts,
-        fracs,
-        values,
-    )
-    halos = exchange(near, far)
-    offsets, coefs, back, partial, beyond, unfinished, middle = call(
+    message = shape(BLOCKS + 1, SIDE_ROWS, LANES)
+    radial_size = lax.axis_size("gx")
+    far_sent = call(advect_far_kernel, "advect_far", message, shifts, fracs, values)
+    far = lax.ppermute(far_sent, "gx", swaps(radial_size, 1))
+    near_sent, offsets, coefs, back, partial, beyond, unfinished, middle = call(
         inner_kernel,
         "inner",
         (
+            message,
             jax.ShapeDtypeStruct(offsets.shape, offsets.dtype),
             shape(COEFS, 8, LANES),
             shape(HALF_VARS * NZ, HALF_VARS * NZ),
@@ -383,9 +382,10 @@
         shifts,
         fracs,
         values,
-        edges,
+        far_sent,
         scratch=[pltpu.VMEM((BLOCKS, ROWS, LANES), F32)] * 2,
     )
+    near = lax.ppermute(near_sent, "gx", swaps(radial_size, 0))
     values = call(
         outer_kernel,
         "outer",
@@ -394,12 +394,14 @@
         coefs,
         shifts,
         fracs,
-        edges,
+        near_sent,
+        far_sent,
         partial,
         beyond,
         unfinished,
         middle,
-        *halos,
+        near,
+        far,
         scratch=[pltpu.VMEM((BLOCKS, SIDE_ROWS, LANES), F32)] * 4,
     )
     return call(unpack_kernel, "unpack", shape(VARS, COLS, NZ, LANES), back, across(values))

time: 86 us -> 83.7 us (0.973); the launches traced: 84.7 us -> 83.4 us
  starting transfers between devices: 5.29 us -> 3.74 us
  blocking collectives: 68.6 us -> 67.6 us
    ppermute x2, starting transfers between devices: 5.29 us -> 3.74 us  [the longest x1 3.65 us: on_device(): far = lax.ppermute(far_sent, 'gx', swaps(radial_size, 1))]
    all_to_all x2, blocking collectives: 68.6 us -> 67.6 us  [across(): return lax.all_to_all(values, 'gy', 0, 0, tiled=True)]
  transfers between devices with their start and end apart: 2 -> 2, of which waited for: 1 -> 1; matrix products, arithmetic and copies ran while one was open for 0% -> 0% of each run, Pallas kernels for 3% -> 4%
where the time goes in v7:
time: 83.7 us; the launch traced here: 83.4 us
  blocking collectives  67.6 us (81%)
  Pallas kernels  8.21 us (10%)
  starting transfers between devices  3.74 us (4%)
  waiting for transfers between devices  1.92 us (2%)
  local copies, waits for them, and re-layouts  1.91 us (2%)
    all_to_all x2, blocking collectives, across(): return lax.all_to_all(values, 'gy', 0, 0, tiled=True)  67.6 us
    pallas_call x5, Pallas kernels, call(): pl.pallas_call(kernel, out_shape=outs, in_specs=[VMEM] * len(args), out_s...  8.21 us
    ppermute x1, starting transfers between devices, on_device(): far = lax.ppermute(far_sent, 'gx', swaps(radial_size, 1))  3.65 us
    ppermute x1, waiting for transfers between devices, on_device(): far = lax.ppermute(far_sent, 'gx', swaps(radial_size, 1))  1.92 us
    unnamed x10, local copies, waits for them, and re-layouts  1.91 us
  transfers between devices with their start and end apart: 2, of which 1 were waited for; matrix products, arithmetic and copies ran while one was open for 0% of the time, Pallas kernels for 4%

profile of v7, /device:TPU:32, one launch (start us, length us, event | category | flops | bytes accessed | tf_op | source)
XLA Modules:
  0.0 83.4 jit_solution(6052530801454017356)
XLA Ops:
  0.0 0.0 copy-start
  0.0 1.2 %copy-done = f32[8,8,32,128]{3,2,1,0:T(8,128)S(1)} copy-done((f32[8,8,32,128]{3,2,1,0:T(8,128)S(1)}, f32[8,8,32,128]{3,2,1,0:T(8,128)}, u32[]{:S(2)}) %copy-start) | copy-done | bytes 1048600
  1.2 1.3 %pack.1 = f32[16,128,128]{2,1,0:T(8,128)S(1)} custom-call(f32[8,8,32,128]{3,2,1,0:T(8,128)S(1)} %copy-done), custom_call_target="tpu_custom_call" | custom-call | tf_op jit(solution)/shard_map/pack/pallas_call | solution.py:337
  2.5 0.0 copy-start.1
  2.5 0.0 copy-start.2
  2.5 35.6 %all_to_all.10.values = f32[16,128,128]{2,1,0:T(8,128)S(1)} all-to-all(f32[16,128,128]{2,1,0:T(8,128)S(1)} %pack.1), channel_id=1, replica_groups=mesh['gx'=16,'gy'=16] {'gy'}, dimensions={0} | all-to-all | bytes 2097152 | tf_op jit(solution)/shard_map/all_to_all | solution.py:354
  38.1 0.0 copy-done.1
  38.1 0.0 copy-done.2
  38.1 0.3 advect_far.1.far.far_sent
  38.5 3.7 %collective-permute-start.1 = (f32[17,32,128]{2,1,0:T(8,128)S(1)}, f32[17,32,128]{2,1,0:T(8,128)S(1)}, u32[]{:S(2)}, u32[]{:S(2)}) collective-permute-start(f32[17,32,128]{2,1,0:T(8,128)S(1)} %advect_far.1.far.far_sent), channel_id=1, source_target_pairs={{16,32},{48,64},{80,96},{112,128},{144,160},{176,192},{208,224},{2... | collective-permute-start | bytes 835592 | tf_op jit(solution)/shard_map/ppermute | solution.py:366
  42.1 0.0 copy-start.3
  42.1 0.0 copy-start.4
  42.1 0.7 copy-done.3
  42.8 0.0 copy-done.4
  42.8 3.4 %inner.1 = (f32[17,32,128]{2,1,0:T(8,128)S(1)}, s32[1,2]{1,0:T(1,128)S(1)}, f32[16,8,128]{2,1,0:T(8,128)S(1)}, f32[128,128]{1,0:T(8,128)S(1)}, f32[16,32,128]{2,...) custom-call(s32[1,2]{1,0:T(1,128)S(1)} %bitcast.2, ...), custom_call_target="tpu_custom_call" | custom-call | tf_op jit(solution)/shard_map/inner/pallas_call | solution.py:337
  46.2 0.1 collective-permute-start
  46.3 1.9 %collective-permute-done.1.far = f32[17,32,128]{2,1,0:T(8,128)S(1)} collective-permute-done((f32[17,32,128]{2,1,0:T(8,128)S(1)}, f32[17,32,128]{2,1,0:T(8,128)S(1)}, u32[]{:S(2)}, u32[]{:S(2)}) %collective-permute-start.1) | collective-permute-done | bytes 278560 | tf_op jit(solution)/shard_map/ppermute | solution.py:366
  48.2 0.0 collective-permute-done.near
  48.2 1.2 %outer.1 = f32[16,128,128]{2,1,0:T(8,128)S(1)} custom-call(s32[1,2]{1,0:T(1,128)S(1)} %get-tuple-element.14.offsets, f32[16,8,128]{2,1,0:T(8,128)S(1)} %get-tuple-element.15.coefs, s32[2,8]{1,0:T(2,128)S(1)} %copy-done.1, f32[2,8]{1,0:T(2,128)S(1)} %copy-done.2, f32[17,32,128]{2,1,0:T(8,128)S(1)} %get-tuple-element.16.near_sent, ...), custom_call_target="tpu_custom_call" | custom-call | tf_op jit(solution)/shard_map/outer/pallas_call | solution.py:337
  49.5 32.0 %all_to_all.11.packed = f32[16,128,128]{2,1,0:T(8,128)S(1)} all-to-all(f32[16,128,128]{2,1,0:T(8,128)S(1)} %outer.1), channel_id=1, replica_groups=mesh['gx'=16,'gy'=16] {'gy'}, dimensions={0} | all-to-all | bytes 2097152 | tf_op jit(solution)/shard_map/all_to_all | solution.py:354
  81.5 2.0 %unpack.1 = f32[8,8,32,128]{3,2,1,0:T(8,128)} custom-call(f32[128,128]{1,0:T(8,128)S(1)} %get-tuple-element.13.back, f32[16,128,128]{2,1,0:T(8,128)S(1)} %all_to_all.11.packed), custom_call_target="tpu_custom_call" | custom-call | tf_op jit(solution)/shard_map/unpack/pallas_call | solution.py:337
Async XLA Ops:
  0.0 1.2 %copy-start = (f32[8,8,32,128]{3,2,1,0:T(8,128)S(1)}, f32[8,8,32,128]{3,2,1,0:T(8,128)}, u32[]{:S(2)}) copy-start(f32[8,8,32,128]{3,2,1,0:T(8,128)} %state.1) | copy-start | bytes 3145732
  2.5 35.6 %copy-start.1 = (s32[2,8]{1,0:T(2,128)S(1)}, s32[2,8]{1,0:T(2,128)}, u32[]{:S(2)}) copy-start(s32[2,8]{1,0:T(2,128)} %shifts.5) | copy-start | bytes 196
  2.5 35.6 %copy-start.2 = (f32[2,8]{1,0:T(2,128)S(1)}, f32[2,8]{1,0:T(2,128)}, u32[]{:S(2)}) copy-start(f32[2,8]{1,0:T(2,128)} %fracs.5) | copy-start | bytes 196
  38.5 9.8 %collective-permute-start.1 = (f32[17,32,128]{2,1,0:T(8,128)S(1)}, f32[17,32,128]{2,1,0:T(8,128)S(1)}, u32[]{:S(2)}, u32[]{:S(2)}) collective-permute-start(f32[17,32,128]{2,1,0:T(8,128)S(1)} %advect_far.1.far.far_sent), channel_id=1, source_target_pairs={{16,32},{48,64},{80,96},{112,128},{144,160},{176,192},{208,224},{2... | collective-permute-start | bytes 835592 | tf_op jit(solution)/shard_map/ppermute | solution.py:366
  42.1 0.7 copy-start.3
  42.1 0.7 copy-start.4
  46.2 2.0 %collective-permute-start = (f32[17,32,128]{2,1,0:T(8,128)S(1)}, f32[17,32,128]{2,1,0:T(8,128)S(1)}, u32[]{:S(2)}, u32[]{:S(2)}) collective-permute-start(f32[17,32,128]{2,1,0:T(8,128)S(1)} %get-tuple-element.16.near_sent), channel_id=1, source_target_pairs={{0,16},{32,48},{64,80},{96,112},{128,144},{160,176},{192,208},{224... | collective-permute-start | bytes 835592 | tf_op jit(solution)/shard_map/ppermute | solution.py:388

commit v8 on v7

--- a/solution.py
+++ b/solution.py
@@ -80,8 +80,9 @@
                 ]
 
 
-def unpack_kernel(back, packed, out):
+def unpack_kernel(back, packed, out, held, left):
     basis = back[...]
+    copies = []
     for half in range(HALVES):
         for col in range(COLS):
             modes = jnp.concatenate(
@@ -93,7 +94,13 @@
             )
             levels = exact_dot(basis, modes)
             for var in range(HALF_VARS):
-                out[half * HALF_VARS + var, col] = levels[var * NZ : (var + 1) * NZ]
+                held[half * HALF_VARS + var, col] = levels[var * NZ : (var + 1) * NZ]
+            part = pl.ds(half * HALF_VARS, HALF_VARS)
+            copy = pltpu.make_async_copy(held.at[part, col], out.at[part, col], left.at[half * COLS + col])
+            copy.start()
+            copies.append(copy)
+    for copy in copies:
+        copy.wait()
 
 
 def move(values, block, rows, turn, weight):
@@ -345,6 +352,19 @@
     )(*args)
 
 
+def unpack(back, values):
+    dims = (VARS, COLS, NZ, LANES)
+    return pl.pallas_call(
+        unpack_kernel,
+        out_shape=shape(*dims),
+        in_specs=[VMEM, VMEM],
+        out_specs=pl.BlockSpec(memory_space=pl.ANY),
+        scratch_shapes=[pltpu.VMEM(dims, F32), pltpu.SemaphoreType.DMA((HALVES * COLS,))],
+        compiler_params=PARAMS,
+        name="unpack",
+    )(back, values)
+
+
 def swaps(count, first):
     pairs = [(i % count, (i + 1) % count) for i in range(first, count, 2)]
     return pairs + [(target, source) for source, target in pairs]
@@ -404,7 +424,7 @@
         far,
         scratch=[pltpu.VMEM((BLOCKS, SIDE_ROWS, LANES), F32)] * 4,
     )
-    return call(unpack_kernel, "unpack", shape(VARS, COLS, NZ, LANES), back, across(values))
+    return unpack(back, across(values))
 
 
 def solution(mesh):

time: 83.7 us -> 83.5 us (level)
    pallas_call x5 -> x4, Pallas kernels: 8.21 us -> 6.24 us  [call(): pl.pallas_call(kernel, out_shape=outs, in_specs=[VMEM] * len(args), out_s...]
    pallas_call x0 -> x1, Pallas kernels: none -> 1.78 us  [unpack(): pl.pallas_call(unpack_kernel, out_shape=shape(*dims), in_specs=[VMEM, VME...]
where the time goes in v8:
time: 83.5 us; the launch traced here: 83.3 us
  blocking collectives  67.6 us (81%)
  Pallas kernels  8.02 us (10%)
  starting transfers between devices  3.74 us (4%)
  waiting for transfers between devices  1.92 us (2%)
  local copies, waits for them, and re-layouts  1.91 us (2%)
    all_to_all x2, blocking collectives, across(): return lax.all_to_all(values, 'gy', 0, 0, tiled=True)  67.6 us
    pallas_call x4, Pallas kernels, call(): pl.pallas_call(kernel, out_shape=outs, in_specs=[VMEM] * len(args), out_s...  6.24 us
    ppermute x1, starting transfers between devices, on_device(): far = lax.ppermute(far_sent, 'gx', swaps(radial_size, 1))  3.65 us
    ppermute x1, waiting for transfers between devices, on_device(): far = lax.ppermute(far_sent, 'gx', swaps(radial_size, 1))  1.92 us
    unnamed x10, local copies, waits for them, and re-layouts  1.91 us
    pallas_call x1, Pallas kernels, unpack(): pl.pallas_call(unpack_kernel, out_shape=shape(*dims), in_specs=[VMEM, VME...  1.78 us
  transfers between devices with their start and end apart: 2, of which 1 were waited for; matrix products, arithmetic and copies ran while one was open for 0% of the time, Pallas kernels for 4%

profile of v8, /device:TPU:32, one launch (start us, length us, event | category | flops | bytes accessed | tf_op | source)
XLA Modules:
  0.0 83.3 jit_solution(10962785637125310841)
XLA Ops:
  0.0 0.0 copy-start
  0.0 1.2 %copy-done = f32[8,8,32,128]{3,2,1,0:T(8,128)S(1)} copy-done((f32[8,8,32,128]{3,2,1,0:T(8,128)S(1)}, f32[8,8,32,128]{3,2,1,0:T(8,128)}, u32[]{:S(2)}) %copy-start) | copy-done | bytes 1048600
  1.2 1.3 %pack.1 = f32[16,128,128]{2,1,0:T(8,128)S(1)} custom-call(f32[8,8,32,128]{3,2,1,0:T(8,128)S(1)} %copy-done), custom_call_target="tpu_custom_call" | custom-call | tf_op jit(solution)/shard_map/pack/pallas_call | solution.py:344
  2.5 0.0 copy-start.1
  2.5 0.0 copy-start.2
  2.5 35.6 %all_to_all.10.values = f32[16,128,128]{2,1,0:T(8,128)S(1)} all-to-all(f32[16,128,128]{2,1,0:T(8,128)S(1)} %pack.1), channel_id=1, replica_groups=mesh['gx'=16,'gy'=16] {'gy'}, dimensions={0} | all-to-all | bytes 2097152 | tf_op jit(solution)/shard_map/all_to_all | solution.py:374
  38.1 0.0 copy-done.1
  38.1 0.0 copy-done.2
  38.1 0.3 advect_far.1.far.far_sent
  38.5 3.7 %collective-permute-start.1 = (f32[17,32,128]{2,1,0:T(8,128)S(1)}, f32[17,32,128]{2,1,0:T(8,128)S(1)}, u32[]{:S(2)}, u32[]{:S(2)}) collective-permute-start(f32[17,32,128]{2,1,0:T(8,128)S(1)} %advect_far.1.far.far_sent), channel_id=1, source_target_pairs={{16,32},{48,64},{80,96},{112,128},{144,160},{176,192},{208,224},{2... | collective-permute-start | bytes 835592 | tf_op jit(solution)/shard_map/ppermute | solution.py:386
  42.1 0.0 copy-start.3
  42.1 0.0 copy-start.4
  42.1 0.7 copy-done.3
  42.8 0.0 copy-done.4
  42.8 3.4 %inner.1 = (f32[17,32,128]{2,1,0:T(8,128)S(1)}, s32[1,2]{1,0:T(1,128)S(1)}, f32[16,8,128]{2,1,0:T(8,128)S(1)}, f32[128,128]{1,0:T(8,128)S(1)}, f32[16,32,128]{2,...) custom-call(s32[1,2]{1,0:T(1,128)S(1)} %bitcast.2, ...), custom_call_target="tpu_custom_call" | custom-call | tf_op jit(solution)/shard_map/inner/pallas_call | solution.py:344
  46.2 0.1 collective-permute-start
  46.3 1.9 %collective-permute-done.1.far = f32[17,32,128]{2,1,0:T(8,128)S(1)} collective-permute-done((f32[17,32,128]{2,1,0:T(8,128)S(1)}, f32[17,32,128]{2,1,0:T(8,128)S(1)}, u32[]{:S(2)}, u32[]{:S(2)}) %collective-permute-start.1) | collective-permute-done | bytes 278560 | tf_op jit(solution)/shard_map/ppermute | solution.py:386
  48.2 0.0 collective-permute-done.near
  48.2 1.2 %outer.1 = f32[16,128,128]{2,1,0:T(8,128)S(1)} custom-call(s32[1,2]{1,0:T(1,128)S(1)} %get-tuple-element.14.offsets, f32[16,8,128]{2,1,0:T(8,128)S(1)} %get-tuple-element.15.coefs, s32[2,8]{1,0:T(2,128)S(1)} %copy-done.1, f32[2,8]{1,0:T(2,128)S(1)} %copy-done.2, f32[17,32,128]{2,1,0:T(8,128)S(1)} %get-tuple-element.16.near_sent, ...), custom_call_target="tpu_custom_call" | custom-call | tf_op jit(solution)/shard_map/outer/pallas_call | solution.py:344
  49.5 32.0 %all_to_all.11.packed = f32[16,128,128]{2,1,0:T(8,128)S(1)} all-to-all(f32[16,128,128]{2,1,0:T(8,128)S(1)} %outer.1), channel_id=1, replica_groups=mesh['gx'=16,'gy'=16] {'gy'}, dimensions={0} | all-to-all | bytes 2097152 | tf_op jit(solution)/shard_map/all_to_all | solution.py:374
  81.5 1.8 %unpack.1 = f32[8,8,32,128]{3,2,1,0:T(8,128)} custom-call(f32[128,128]{1,0:T(8,128)S(1)} %get-tuple-element.13.back, f32[16,128,128]{2,1,0:T(8,128)S(1)} %all_to_all.11.packed), custom_call_target="tpu_custom_call" | custom-call | tf_op jit(solution)/shard_map/unpack/pallas_call | solution.py:357
Async XLA Ops:
  0.0 1.2 %copy-start = (f32[8,8,32,128]{3,2,1,0:T(8,128)S(1)}, f32[8,8,32,128]{3,2,1,0:T(8,128)}, u32[]{:S(2)}) copy-start(f32[8,8,32,128]{3,2,1,0:T(8,128)} %state.1) | copy-start | bytes 3145732
  2.5 35.6 %copy-start.1 = (s32[2,8]{1,0:T(2,128)S(1)}, s32[2,8]{1,0:T(2,128)}, u32[]{:S(2)}) copy-start(s32[2,8]{1,0:T(2,128)} %shifts.5) | copy-start | bytes 196
  2.5 35.6 %copy-start.2 = (f32[2,8]{1,0:T(2,128)S(1)}, f32[2,8]{1,0:T(2,128)}, u32[]{:S(2)}) copy-start(f32[2,8]{1,0:T(2,128)} %fracs.5) | copy-start | bytes 196
  38.5 9.8 %collective-permute-start.1 = (f32[17,32,128]{2,1,0:T(8,128)S(1)}, f32[17,32,128]{2,1,0:T(8,128)S(1)}, u32[]{:S(2)}, u32[]{:S(2)}) collective-permute-start(f32[17,32,128]{2,1,0:T(8,128)S(1)} %advect_far.1.far.far_sent), channel_id=1, source_target_pairs={{16,32},{48,64},{80,96},{112,128},{144,160},{176,192},{208,224},{2... | collective-permute-start | bytes 835592 | tf_op jit(solution)/shard_map/ppermute | solution.py:386
  42.1 0.7 copy-start.3
  42.1 0.7 copy-start.4
  46.2 2.0 %collective-permute-start = (f32[17,32,128]{2,1,0:T(8,128)S(1)}, f32[17,32,128]{2,1,0:T(8,128)S(1)}, u32[]{:S(2)}, u32[]{:S(2)}) collective-permute-start(f32[17,32,128]{2,1,0:T(8,128)S(1)} %get-tuple-element.16.near_sent), channel_id=1, source_target_pairs={{0,16},{32,48},{64,80},{96,112},{128,144},{160,176},{192,208},{224... | collective-permute-start | bytes 835592 | tf_op jit(solution)/shard_map/ppermute | solution.py:408

commit v9 on v8

--- a/solution.py
+++ b/solution.py
@@ -68,8 +68,12 @@
     return lax.dot(left, right, precision=lax.Precision.HIGHEST, preferred_element_type=F32)
 
 
-def pack_kernel(state, out):
-    basis = to_modes(False)
+def basis_kernel(out):
+    out[...] = to_modes(False)
+
+
+def pack_kernel(forth, state, out):
+    basis = forth[...]
     for half in range(HALVES):
         for col in range(COLS):
             levels = jnp.concatenate([state[half * HALF_VARS + var, col] for var in range(HALF_VARS)], axis=0)
@@ -379,7 +383,8 @@
     side = shape(BLOCKS, SIDE_ROWS, LANES)
     offsets = offsets[None]
     kappa = kappa[None]
-    values = across(call(pack_kernel, "pack", whole, state))
+    forth = call(basis_kernel, "basis", shape(HALF_VARS * NZ, HALF_VARS * NZ))
+    values = across(call(pack_kernel, "pack", whole, forth, state))
     message = shape(BLOCKS + 1, SIDE_ROWS, LANES)
     radial_size = lax.axis_size("gx")
     far_sent = call(advect_far_kernel, "advect_far", message, shifts, fracs, values)

time: 83.5 us -> 83.5 us (level)
    pallas_call x4 -> x5, Pallas kernels: 6.24 us -> 6.22 us  [call(): pl.pallas_call(kernel, out_shape=outs, in_specs=[VMEM] * len(args), out_s...]
where the time goes in v9:
time: 83.5 us; the launch traced here: 83.2 us
  blocking collectives  67.6 us (81%)
  Pallas kernels  8 us (10%)
  starting transfers between devices  3.74 us (4%)
  waiting for transfers between devices  1.93 us (2%)
  local copies, waits for them, and re-layouts  1.9 us (2%)
    all_to_all x2, blocking collectives, across(): return lax.all_to_all(values, 'gy', 0, 0, tiled=True)  67.6 us
    pallas_call x5, Pallas kernels, call(): pl.pallas_call(kernel, out_shape=outs, in_specs=[VMEM] * len(args), out_s...  6.22 us
    ppermute x1, starting transfers between devices, on_device(): far = lax.ppermute(far_sent, 'gx', swaps(radial_size, 1))  3.65 us
    ppermute x1, waiting for transfers between devices, on_device(): far = lax.ppermute(far_sent, 'gx', swaps(radial_size, 1))  1.93 us
    unnamed x10, local copies, waits for them, and re-layouts  1.9 us
    pallas_call x1, Pallas kernels, unpack(): pl.pallas_call(unpack_kernel, out_shape=shape(*dims), in_specs=[VMEM, VME...  1.78 us
  transfers between devices with their start and end apart: 2, of which 1 were waited for; matrix products, arithmetic and copies ran while one was open for 0% of the time, Pallas kernels for 4%

profile of v9, /device:TPU:32, one launch (start us, length us, event | category | flops | bytes accessed | tf_op | source)
XLA Modules:
  0.0 83.2 jit_solution(15446096831986170067)
XLA Ops:
  0.0 0.3 basis.1.forth
  0.3 0.0 copy-start
  0.3 1.2 %copy-done = f32[8,8,32,128]{3,2,1,0:T(8,128)S(1)} copy-done((f32[8,8,32,128]{3,2,1,0:T(8,128)S(1)}, f32[8,8,32,128]{3,2,1,0:T(8,128)}, u32[]{:S(2)}) %copy-start) | copy-done | bytes 1048600
  1.5 1.0 %pack.1 = f32[16,128,128]{2,1,0:T(8,128)S(1)} custom-call(f32[128,128]{1,0:T(8,128)S(1)} %basis.1.forth, f32[8,8,32,128]{3,2,1,0:T(8,128)S(1)} %copy-done), custom_call_target="tpu_custom_call" | custom-call | tf_op jit(solution)/shard_map/pack/pallas_call | solution.py:348
  2.5 0.0 copy-start.1
  2.5 0.0 copy-start.2
  2.5 35.6 %all_to_all.10.values = f32[16,128,128]{2,1,0:T(8,128)S(1)} all-to-all(f32[16,128,128]{2,1,0:T(8,128)S(1)} %pack.1), channel_id=1, replica_groups=mesh['gx'=16,'gy'=16] {'gy'}, dimensions={0} | all-to-all | bytes 2097152 | tf_op jit(solution)/shard_map/all_to_all | solution.py:378
  38.1 0.0 copy-done.1
  38.1 0.0 copy-done.2
  38.1 0.3 advect_far.1.far.far_sent
  38.5 3.6 %collective-permute-start.1 = (f32[17,32,128]{2,1,0:T(8,128)S(1)}, f32[17,32,128]{2,1,0:T(8,128)S(1)}, u32[]{:S(2)}, u32[]{:S(2)}) collective-permute-start(f32[17,32,128]{2,1,0:T(8,128)S(1)} %advect_far.1.far.far_sent), channel_id=1, source_target_pairs={{16,32},{48,64},{80,96},{112,128},{144,160},{176,192},{208,224},{2... | collective-permute-start | bytes 835592 | tf_op jit(solution)/shard_map/ppermute | solution.py:391
  42.1 0.0 copy-start.3
  42.1 0.0 copy-start.4
  42.1 0.7 copy-done.3
  42.8 0.0 copy-done.4
  42.8 3.4 %inner.1 = (f32[17,32,128]{2,1,0:T(8,128)S(1)}, s32[1,2]{1,0:T(1,128)S(1)}, f32[16,8,128]{2,1,0:T(8,128)S(1)}, f32[128,128]{1,0:T(8,128)S(1)}, f32[16,32,128]{2,...) custom-call(s32[1,2]{1,0:T(1,128)S(1)} %bitcast.2, ...), custom_call_target="tpu_custom_call" | custom-call | tf_op jit(solution)/shard_map/inner/pallas_call | solution.py:348
  46.2 0.1 collective-permute-start
  46.3 1.9 %collective-permute-done.1.far = f32[17,32,128]{2,1,0:T(8,128)S(1)} collective-permute-done((f32[17,32,128]{2,1,0:T(8,128)S(1)}, f32[17,32,128]{2,1,0:T(8,128)S(1)}, u32[]{:S(2)}, u32[]{:S(2)}) %collective-permute-start.1) | collective-permute-done | bytes 278560 | tf_op jit(solution)/shard_map/ppermute | solution.py:391
  48.2 0.0 collective-permute-done.near
  48.2 1.2 %outer.1 = f32[16,128,128]{2,1,0:T(8,128)S(1)} custom-call(s32[1,2]{1,0:T(1,128)S(1)} %get-tuple-element.14.offsets, f32[16,8,128]{2,1,0:T(8,128)S(1)} %get-tuple-element.15.coefs, s32[2,8]{1,0:T(2,128)S(1)} %copy-done.1, f32[2,8]{1,0:T(2,128)S(1)} %copy-done.2, f32[17,32,128]{2,1,0:T(8,128)S(1)} %get-tuple-element.16.near_sent, ...), custom_call_target="tpu_custom_call" | custom-call | tf_op jit(solution)/shard_map/outer/pallas_call | solution.py:348
  49.5 32.0 %all_to_all.11.packed = f32[16,128,128]{2,1,0:T(8,128)S(1)} all-to-all(f32[16,128,128]{2,1,0:T(8,128)S(1)} %outer.1), channel_id=1, replica_groups=mesh['gx'=16,'gy'=16] {'gy'}, dimensions={0} | all-to-all | bytes 2097152 | tf_op jit(solution)/shard_map/all_to_all | solution.py:378
  81.5 1.8 %unpack.1 = f32[8,8,32,128]{3,2,1,0:T(8,128)} custom-call(f32[128,128]{1,0:T(8,128)S(1)} %get-tuple-element.13.back, f32[16,128,128]{2,1,0:T(8,128)S(1)} %all_to_all.11.packed), custom_call_target="tpu_custom_call" | custom-call | tf_op jit(solution)/shard_map/unpack/pallas_call | solution.py:361
Async XLA Ops:
  0.3 1.2 %copy-start = (f32[8,8,32,128]{3,2,1,0:T(8,128)S(1)}, f32[8,8,32,128]{3,2,1,0:T(8,128)}, u32[]{:S(2)}) copy-start(f32[8,8,32,128]{3,2,1,0:T(8,128)} %state.1) | copy-start | bytes 3145732
  2.5 35.6 %copy-start.1 = (s32[2,8]{1,0:T(2,128)S(1)}, s32[2,8]{1,0:T(2,128)}, u32[]{:S(2)}) copy-start(s32[2,8]{1,0:T(2,128)} %shifts.5) | copy-start | bytes 196
  2.5 35.6 %copy-start.2 = (f32[2,8]{1,0:T(2,128)S(1)}, f32[2,8]{1,0:T(2,128)}, u32[]{:S(2)}) copy-start(f32[2,8]{1,0:T(2,128)} %fracs.5) | copy-start | bytes 196
  38.5 9.8 %collective-permute-start.1 = (f32[17,32,128]{2,1,0:T(8,128)S(1)}, f32[17,32,128]{2,1,0:T(8,128)S(1)}, u32[]{:S(2)}, u32[]{:S(2)}) collective-permute-start(f32[17,32,128]{2,1,0:T(8,128)S(1)} %advect_far.1.far.far_sent), channel_id=1, source_target_pairs={{16,32},{48,64},{80,96},{112,128},{144,160},{176,192},{208,224},{2... | collective-permute-start | bytes 835592 | tf_op jit(solution)/shard_map/ppermute | solution.py:391
  42.1 0.7 copy-start.3
  42.1 0.7 copy-start.4
  46.2 2.0 %collective-permute-start = (f32[17,32,128]{2,1,0:T(8,128)S(1)}, f32[17,32,128]{2,1,0:T(8,128)S(1)}, u32[]{:S(2)}, u32[]{:S(2)}) collective-permute-start(f32[17,32,128]{2,1,0:T(8,128)S(1)} %get-tuple-element.16.near_sent), channel_id=1, source_target_pairs={{0,16},{32,48},{64,80},{96,112},{128,144},{160,176},{192,208},{224... | collective-permute-start | bytes 835592 | tf_op jit(solution)/shard_map/ppermute | solution.py:413
